TPU v7x, 32 devices: a whole 2x2x4 slice. The times are simulated.
32 devices in a mesh: shard: 4 (over x, core), ctx: 4 (over z), tp: 2 (over y).
Axes of the slice: x: 2, y: 2, z: 4, core: 2. Of those that a mesh axis runs over, the one named last changes fastest.
Arguments:
- tokens: bfloat16 [8, 1024, 2048], P('shard', 'ctx'), may hold values from -6 to 6
- cotangent: bfloat16 [8, 1024, 2048], P('shard', 'ctx'), may hold values from -6 to 6
- buckets: int32 [1024, 1024], P('ctx'), may hold values from 0 to 31, as said below
- query_weight: bfloat16 [2048, 2048], P('shard', 'tp'), may hold values from -0.03125 to 0.03125
- key_weight: bfloat16 [2048, 2048], P('shard', 'tp'), may hold values from -0.125 to 0.125
- value_weight: bfloat16 [2048, 2048], P('shard', 'tp'), may hold values from -0.125 to 0.125
- output_weight: bfloat16 [2048, 2048], P('shard', 'tp'), may hold values from -0.375 to 0.375
- gate_weight: bfloat16 [2048, 5120], P('shard', 'tp'), may hold values from -0.125 to 0.125
- up_weight: bfloat16 [2048, 5120], P('shard', 'tp'), may hold values from -0.125 to 0.125
- down_weight: bfloat16 [2048, 5120], P('shard', 'tp'), may hold values from -0.078125 to 0.078125
- norm_gain: bfloat16 [2048], replicated, may hold values from 0.25 to 1.75
- ffn_gain: bfloat16 [2048], replicated, may hold values from 0.25 to 1.75
- bucket_bias_table: bfloat16 [32, 32], P(None, 'tp'), may hold values from -4 to 4
Outputs:
- layer_output: bfloat16 [8, 1024, 2048], P('shard', 'ctx')
- input_grad: float32 [8, 1024, 2048], P('shard', 'ctx')
- query_grad: float32 [2048, 2048], P('shard', 'tp')
- key_grad: float32 [2048, 2048], P('shard', 'tp')
- value_grad: float32 [2048, 2048], P('shard', 'tp')
- output_grad: float32 [2048, 2048], P('shard', 'tp')
- gate_grad: float32 [2048, 5120], P('shard', 'tp')
- up_grad: float32 [2048, 5120], P('shard', 'tp')
- down_grad: float32 [2048, 5120], P('shard', 'tp')
- norm_gain_grad: float32 [2048], replicated
- ffn_gain_grad: float32 [2048], replicated
- table_grad: float32 [32, 32], P(None, 'tp')
Inputs may be any that keep to these rules, and one draw needn't show every extreme that they name: buckets[i, j] is T5's bidirectional relative position bucket of the offset j - i (32 buckets, maximum distance 128), its bucket number relabelled by one permutation of the 32 buckets; it depends only on j - i, and one table serves every sequence.
All inputs are finite; a program needn't handle non-finite values.
Results may differ from a plain program's by a relative error of at most 0.023.
Values may be sent and summed in bfloat16 or wider, within the bound.
A program may use at most 256 MiB of HBM per device.

v0:
```python
import jax
import jax.numpy as jnp
from jax import lax
from jax.sharding import PartitionSpec as P


def contract_rows(left, right):
    return lax.dot_general(
        left, right, (((0,), (0,)), ((), ())), preferred_element_type=jnp.float32
    )


def contract_cols(left, right):
    return lax.dot_general(
        left, right, (((1,), (1,)), ((), ())), preferred_element_type=jnp.float32
    )


def rms_scale(values):
    return lax.rsqrt(jnp.mean(values * values, axis=-1, keepdims=True) + 1e-06)


def rms_back(values, scale, gain, upstream):
    weighted = upstream * gain
    inner_average = jnp.mean(values * weighted, axis=-1, keepdims=True)
    return scale * weighted - values * scale * scale * scale * inner_average


def geglu(gate, up):
    return jax.nn.gelu(gate, approximate=True) * up


def per_device(
    tokens,
    cotangent,
    buckets,
    query_weight,
    key_weight,
    value_weight,
    output_weight,
    gate_weight,
    up_weight,
    down_weight,
    norm_gain,
    ffn_gain,
    bucket_bias_table,
):
    seqs, local_len, width = tokens.shape
    rows = seqs * local_len
    slots, heads = bucket_bias_table.shape
    inner_width = query_weight.shape[1]
    head_dim = inner_width // heads
    gain_one = norm_gain.astype(jnp.float32)
    gain_two = ffn_gain.astype(jnp.float32)
    wq, wk, wv, wo = (
        lax.all_gather(query_weight, "shard", axis=0, tiled=True),
        lax.all_gather(key_weight, "shard", axis=0, tiled=True),
        lax.all_gather(value_weight, "shard", axis=0, tiled=True),
        lax.all_gather(output_weight, "shard", axis=0, tiled=True),
    )
    inputs = tokens.reshape(rows, width).astype(jnp.float32)
    scale_one = rms_scale(inputs)
    normed = (inputs * scale_one * gain_one).astype(jnp.bfloat16)
    query = jnp.dot(normed, wq, preferred_element_type=jnp.float32).astype(jnp.bfloat16)
    key = jnp.dot(normed, wk, preferred_element_type=jnp.float32).astype(jnp.bfloat16)
    value = jnp.dot(normed, wv, preferred_element_type=jnp.float32).astype(jnp.bfloat16)
    query_seq = query.reshape(seqs, local_len, inner_width)
    key_all, value_all = (
        lax.all_gather(key.reshape(seqs, local_len, inner_width), "ctx", axis=1, tiled=True),
        lax.all_gather(value.reshape(seqs, local_len, inner_width), "ctx", axis=1, tiled=True),
    )
    full_len = key_all.shape[1]
    bucket_indicator = (
        buckets[None, :, :] == jnp.arange(slots, dtype=jnp.int32)[:, None, None]
    ).astype(jnp.bfloat16)
    position_bias = jnp.einsum(
        "lev,lr->rev", bucket_indicator, bucket_bias_table, preferred_element_type=jnp.float32
    )

    def score_block(q_blk, k_blk):
        q_heads = q_blk.reshape(local_len, heads, head_dim)
        k_heads = k_blk.reshape(full_len, heads, head_dim)
        return (
            jnp.einsum("qhd,khd->hqk", q_heads, k_heads, preferred_element_type=jnp.float32)
            + position_bias
        )

    def attend(block):
        q_blk, k_blk, v_blk = block
        scores = score_block(q_blk, k_blk)
        peak = jnp.max(scores, axis=-1, keepdims=True)
        expo = jnp.exp(scores - peak)
        total = jnp.sum(expo, axis=-1, keepdims=True)
        probs = (expo / total).astype(jnp.bfloat16)
        mixed = jnp.einsum(
            "hqk,khd->qhd",
            probs,
            v_blk.reshape(full_len, heads, head_dim),
            preferred_element_type=jnp.float32,
        )
        return (
            mixed.reshape(local_len, inner_width).astype(jnp.bfloat16),
            peak[..., 0] + jnp.log(total[..., 0]),
        )

    attended, log_totals = lax.map(attend, (query_seq, key_all, value_all))
    attended = attended.reshape(rows, inner_width)
    branch = lax.psum(contract_cols(attended, wo).astype(jnp.bfloat16), "tp").astype(jnp.float32)
    hidden = inputs + branch
    wi0, wi1, wff = (
        lax.all_gather(gate_weight, "shard", axis=0, tiled=True),
        lax.all_gather(up_weight, "shard", axis=0, tiled=True),
        lax.all_gather(down_weight, "shard", axis=0, tiled=True),
    )
    scale_two = rms_scale(hidden)
    normed_two = (hidden * scale_two * gain_two).astype(jnp.bfloat16)
    gate = jnp.dot(normed_two, wi0, preferred_element_type=jnp.float32)
    up = jnp.dot(normed_two, wi1, preferred_element_type=jnp.float32)
    inner = geglu(gate, up).astype(jnp.bfloat16)
    ffn_out = lax.psum(contract_cols(inner, wff).astype(jnp.bfloat16), "tp").astype(jnp.float32)
    result = (hidden + ffn_out).astype(jnp.bfloat16).reshape(seqs, local_len, width)
    upstream = cotangent.reshape(rows, width).astype(jnp.float32)
    upstream_low = cotangent.reshape(rows, width)
    grad_down_w = contract_rows(upstream_low, inner)
    grad_inner = jnp.dot(upstream_low, wff, preferred_element_type=jnp.float32)
    unused, geglu_backward_pull = jax.vjp(geglu, gate, up)
    grad_gate, grad_up = geglu_backward_pull(grad_inner)
    grad_gate = grad_gate.astype(jnp.bfloat16)
    grad_up = grad_up.astype(jnp.bfloat16)
    grad_gate_w = contract_rows(normed_two, grad_gate)
    grad_up_w = contract_rows(normed_two, grad_up)
    grad_normed_two = lax.psum(
        (contract_cols(grad_gate, wi0) + contract_cols(grad_up, wi1)).astype(jnp.bfloat16), "tp"
    ).astype(jnp.float32)
    grad_ffn_gain = jnp.sum(grad_normed_two * hidden * scale_two, axis=0)
    grad_hidden = upstream + rms_back(hidden, scale_two, gain_two, grad_normed_two)
    branch_low = grad_hidden.astype(jnp.bfloat16)
    grad_output_w = contract_rows(branch_low, attended)
    grad_attended = jnp.dot(branch_low, wo, preferred_element_type=jnp.float32).astype(jnp.bfloat16)

    def attend_back(block):
        q_blk, k_blk, v_blk, g_blk, lse_blk = block
        scores = score_block(q_blk, k_blk)
        probs = jnp.exp(scores - lse_blk[..., None])
        g_heads = g_blk.reshape(local_len, heads, head_dim)
        grad_probs = jnp.einsum(
            "qhd,khd->hqk",
            g_heads,
            v_blk.reshape(full_len, heads, head_dim),
            preferred_element_type=jnp.float32,
        )
        delta = jnp.sum(grad_probs * probs, axis=-1, keepdims=True)
        score_gradient = (probs * (grad_probs - delta)).astype(jnp.bfloat16)
        grad_q = jnp.einsum(
            "hqk,khd->qhd",
            score_gradient,
            k_blk.reshape(full_len, heads, head_dim),
            preferred_element_type=jnp.float32,
        )
        grad_k = jnp.einsum(
            "hqk,qhd->khd",
            score_gradient,
            q_blk.reshape(local_len, heads, head_dim),
            preferred_element_type=jnp.float32,
        )
        grad_v = jnp.einsum(
            "hqk,qhd->khd", probs.astype(jnp.bfloat16), g_heads, preferred_element_type=jnp.float32
        )
        grad_tab = jnp.einsum(
            "gij,sij->gs", bucket_indicator, score_gradient, preferred_element_type=jnp.float32
        )
        return (
            grad_q.reshape(local_len, inner_width).astype(jnp.bfloat16),
            grad_k.reshape(full_len, inner_width),
            grad_v.reshape(full_len, inner_width),
            grad_tab,
        )

    grad_query, key_terms, value_terms, table_terms = lax.map(
        attend_back,
        (
            query_seq,
            key_all,
            value_all,
            grad_attended.reshape(seqs, local_len, inner_width),
            log_totals,
        ),
    )
    key_sums, value_sums = (
        lax.psum_scatter(
            key_terms.astype(jnp.bfloat16), "ctx", scatter_dimension=1, tiled=True
        ).astype(jnp.float32),
        lax.psum_scatter(
            value_terms.astype(jnp.bfloat16), "ctx", scatter_dimension=1, tiled=True
        ).astype(jnp.float32),
    )
    grad_query = grad_query.reshape(rows, inner_width)
    grad_key = key_sums.astype(jnp.bfloat16).reshape(rows, inner_width)
    grad_value = value_sums.astype(jnp.bfloat16).reshape(rows, inner_width)
    grad_table = jnp.sum(table_terms, axis=0)
    grad_normed = lax.psum(
        (
            contract_cols(grad_query, wq)
            + contract_cols(grad_key, wk)
            + contract_cols(grad_value, wv)
        ).astype(jnp.bfloat16),
        "tp",
    ).astype(jnp.float32)
    grad_norm_gain = jnp.sum(grad_normed * inputs * scale_one, axis=0)
    grad_inputs = grad_hidden + rms_back(inputs, scale_one, gain_one, grad_normed)
    grad_query_w = contract_rows(normed, grad_query)
    grad_key_w = contract_rows(normed, grad_key)
    grad_value_w = contract_rows(normed, grad_value)
    small = lax.psum((grad_norm_gain, grad_ffn_gain, grad_table), ("shard", "ctx"))
    pieces = (
        lax.psum_scatter(
            grad_query_w.astype(jnp.bfloat16), "shard", scatter_dimension=0, tiled=True
        ).astype(jnp.float32),
        lax.psum_scatter(
            grad_key_w.astype(jnp.bfloat16), "shard", scatter_dimension=0, tiled=True
        ).astype(jnp.float32),
        lax.psum_scatter(
            grad_value_w.astype(jnp.bfloat16), "shard", scatter_dimension=0, tiled=True
        ).astype(jnp.float32),
        lax.psum_scatter(
            grad_output_w.astype(jnp.bfloat16), "shard", scatter_dimension=0, tiled=True
        ).astype(jnp.float32),
        lax.psum_scatter(
            grad_gate_w.astype(jnp.bfloat16), "shard", scatter_dimension=0, tiled=True
        ).astype(jnp.float32),
        lax.psum_scatter(
            grad_up_w.astype(jnp.bfloat16), "shard", scatter_dimension=0, tiled=True
        ).astype(jnp.float32),
        lax.psum_scatter(
            grad_down_w.astype(jnp.bfloat16), "shard", scatter_dimension=0, tiled=True
        ).astype(jnp.float32),
    )
    summed = (
        lax.psum(pieces[0].astype(jnp.bfloat16), "ctx").astype(jnp.float32),
        lax.psum(pieces[1].astype(jnp.bfloat16), "ctx").astype(jnp.float32),
        lax.psum(pieces[2].astype(jnp.bfloat16), "ctx").astype(jnp.float32),
        lax.psum(pieces[3].astype(jnp.bfloat16), "ctx").astype(jnp.float32),
        lax.psum(pieces[4].astype(jnp.bfloat16), "ctx").astype(jnp.float32),
        lax.psum(pieces[5].astype(jnp.bfloat16), "ctx").astype(jnp.float32),
        lax.psum(pieces[6].astype(jnp.bfloat16), "ctx").astype(jnp.float32),
    )
    return (
        result,
        grad_inputs.reshape(seqs, local_len, width),
        summed[0],
        summed[1],
        summed[2],
        summed[3],
        summed[4],
        summed[5],
        summed[6],
        small[0],
        small[1],
        small[2],
    )


def solution(mesh):
    return jax.shard_map(
        per_device,
        mesh=mesh,
        in_specs=(
            P("shard", "ctx", None),
            P("shard", "ctx", None),
            P("ctx", None),
            P("shard", "tp"),
            P("shard", "tp"),
            P("shard", "tp"),
            P("shard", "tp"),
            P("shard", "tp"),
            P("shard", "tp"),
            P("shard", "tp"),
            P(),
            P(),
            P(None, "tp"),
        ),
        out_specs=(
            P("shard", "ctx", None),
            P("shard", "ctx", None),
            P("shard", "tp"),
            P("shard", "tp"),
            P("shard", "tp"),
            P("shard", "tp"),
            P("shard", "tp"),
            P("shard", "tp"),
            P("shard", "tp"),
            P(),
            P(),
            P(None, "tp"),
        ),
        check_vma=False,
    )
```

profile of v0, /device:TPU:0, one launch (start us, length us, event | category | flops | bytes accessed | tf_op | source)
XLA Modules:
  0.0 2081.5 jit_solution(17504024944867056232)
XLA Ops:
  13.7 33.1 %all-gather.10.cloned.1.call-done = bf16[2048,1024]{1,0:T(8,128)(2,1)} async-done(((bf16[512,1024]{1,0:T(8,128)(2,1)}), bf16[2048,1024]{1,0:T(8,128)(2,1)}) %all-gather.10.cloned.1.call-update) | async-done | bytes 4194320 | tf_op jit(solution)/shard_map/all_gather | solution.py:58
  53.4 29.5 %all-gather.16.cloned.1.call-done = bf16[2048,1024]{1,0:T(8,128)(2,1)} async-done(((bf16[512,1024]{1,0:T(8,128)(2,1)}), bf16[2048,1024]{1,0:T(8,128)(2,1)}) %all-gather.16.cloned.1.call-update) | async-done | bytes 4194320 | tf_op jit(solution)/shard_map/all_gather | solution.py:57
  96.8 18.9 copy.44
  124.7 76.9 %all-gather.12.cloned.1.call-done = bf16[2,1024,1024]{1,2,0:T(8,128)(2,1)} async-done(((bf16[2,256,1024]{1,2,0:T(8,128)(2,1)}), bf16[2,1024,1024]{1,2,0:T(8,128)(2,1)}) %all-gather.12.cloned.1.call-update) | async-done | bytes 4194320 | tf_op jit(solution)/shard_map/all_gather | solution.py:70
  201.6 80.8 %all-gather.18.cloned.1.call-done = bf16[2,1024,1024]{1,2,0:T(8,128)(2,1)} async-done(((bf16[2,256,1024]{1,2,0:T(8,128)(2,1)}), bf16[2,1024,1024]{1,2,0:T(8,128)(2,1)}) %all-gather.18.cloned.1.call-update) | async-done | bytes 4194320 | tf_op jit(solution)/shard_map/all_gather | solution.py:69
  282.3 66.5 %while.29 = (s32[]{:T(128)}, bf16[2,256,1024]{2,1,0:T(8,128)(2,1)}, f32[2,16,256]{2,1,0:T(8,128)S(1)}, bf16[2,1024,1024]{1,2,0:T(8,128)(2,1)}, bf16[2,256,1024]{...) while((s32[]{:T(128)}, bf16[2,256,1024]{2,1,0:T(8,128)(2,1)}, ...), condition=%wide.region_4.5_spmd, body=%wide.region_1.4_spmd.sunk | while | flops 1103360000 | bytes 151126160 | solution.py:106
  357.7 58.8 %all-reduce.8.cloned.1.call-done = bf16[512,2048]{1,0:T(8,128)(2,1)} async-done(((bf16[512,2048]{1,0:T(8,128)(2,1)}), bf16[512,2048]{1,0:T(8,128)(2,1)}) %all-reduce.8.cloned.1.call-update) | async-done | bytes 2097168 | tf_op jit(solution)/shard_map/psum | solution.py:108
  421.5 66.9 %all-gather.22.cloned.1.call-done = bf16[2048,2560]{1,0:T(8,128)(2,1)} async-done(((bf16[512,2560]{1,0:T(8,128)(2,1)}), bf16[2048,2560]{1,0:T(8,128)(2,1)}) %all-gather.22.cloned.1.call-update) | async-done | bytes 10485776 | tf_op jit(solution)/shard_map/all_gather | solution.py:111
  488.4 23.2 %fusion.64 = f32[512,2560]{1,0:T(8,128)} fusion(bf16[512,2048]{1,0:T(8,128)(2,1)} %multiply_convert_fusion.3, bf16[2048,2560]{1,0:T(8,128)(2,1)} %all-gather.22.cloned.1.call-done), kind=kOutput, calls=%fused_computation.108 | convolution fusion | flops 5368709120 | bytes 17825792 | tf_op jit(solution)/shard_map/dot_general | solution.py:117
  511.6 48.7 %all-gather.24.cloned.1.call-done = bf16[2048,2560]{1,0:T(8,128)(2,1)} async-done(((bf16[512,2560]{1,0:T(8,128)(2,1)}), bf16[2048,2560]{1,0:T(8,128)(2,1)}) %all-gather.24.cloned.1.call-update) | async-done | bytes 10485776 | tf_op jit(solution)/shard_map/all_gather | solution.py:112
  570.6 61.3 %all-gather.26.cloned.1.call-done = bf16[2048,2560]{1,0:T(8,128)(2,1)} async-done(((bf16[512,2560]{1,0:T(8,128)(2,1)}), bf16[2048,2560]{1,0:T(8,128)(2,1)}) %all-gather.26.cloned.1.call-update) | async-done | bytes 10485776 | tf_op jit(solution)/shard_map/all_gather | solution.py:113
  664.8 63.0 %all-reduce.10.cloned.1.call-done = bf16[512,2048]{1,0:T(8,128)(2,1)} async-done(((bf16[512,2048]{1,0:T(8,128)(2,1)}), bf16[512,2048]{1,0:T(8,128)(2,1)}) %all-reduce.10.cloned.1.call-update) | async-done | bytes 2097168 | tf_op jit(solution)/shard_map/psum | solution.py:132
  738.4 175.4 %while.30 = (s32[]{:T(128)}, bf16[2,256,1024]{1,2,0:T(8,128)(2,1)}, bf16[2,1024,1024]{2,1,0:T(8,128)(2,1)}, bf16[2,1024,1024]{2,1,0:T(8,128)(2,1)}, f32[2,32,16]...) while((s32[]{:T(128)}, bf16[2,256,1024]{1,2,0:T(8,128)(2,1)}, ...), condition=%wide.region_12.13_spmd.clone, body=%wide.region_10.12_spmd.clone.sunk | while | flops 3003379712 | bytes 265904560 | solution.py:179
  927.4 63.3 %reduce-scatter.10.cloned.1.call-done = bf16[2,256,1024]{2,1,0:T(8,128)(2,1)} async-done(((bf16[2,1024,1024]{2,1,0:T(8,128)(2,1)}), bf16[2,256,1024]{2,1,0:T(8,128)(2,1)}) %reduce-scatter.10.cloned.1.call-update) | async-done | bytes 1048592 | tf_op jit(solution)/shard_map/reduce_scatter | solution.py:190
  996.6 74.4 %reduce-scatter.12.cloned.1.call-done = bf16[2,256,1024]{2,1,0:T(8,128)(2,1)} async-done(((bf16[2,1024,1024]{2,1,0:T(8,128)(2,1)}), bf16[2,256,1024]{2,1,0:T(8,128)(2,1)}) %reduce-scatter.12.cloned.1.call-update) | async-done | bytes 1048592 | tf_op jit(solution)/shard_map/reduce_scatter | solution.py:193
  1131.6 34.5 %reduce-scatter.20.cloned.1.call-done = bf16[512,1024]{1,0:T(8,128)(2,1)} async-done(((bf16[2048,1024]{1,0:T(8,128)(2,1)}), bf16[512,1024]{1,0:T(8,128)(2,1)}) %reduce-scatter.20.cloned.1.call-update) | async-done | bytes 1048592 | tf_op jit(solution)/shard_map/reduce_scatter | solution.py:225
  1166.1 47.5 %reduce-scatter.16.cloned.1.call-done = bf16[512,1024]{1,0:T(8,128)(2,1)} async-done(((bf16[2048,1024]{1,0:T(8,128)(2,1)}), bf16[512,1024]{1,0:T(8,128)(2,1)}) %reduce-scatter.16.cloned.1.call-update) | async-done | bytes 1048592 | tf_op jit(solution)/shard_map/reduce_scatter | solution.py:219
  1213.6 47.7 %reduce-scatter.18.cloned.1.call-done = bf16[512,1024]{1,0:T(8,128)(2,1)} async-done(((bf16[2048,1024]{1,0:T(8,128)(2,1)}), bf16[512,1024]{1,0:T(8,128)(2,1)}) %reduce-scatter.18.cloned.1.call-update) | async-done | bytes 1048592 | tf_op jit(solution)/shard_map/reduce_scatter | solution.py:222
  1261.3 87.8 %reduce-scatter.26.cloned.1.call-done = bf16[512,2560]{0,1:T(8,128)(2,1)} async-done(((bf16[2048,2560]{0,1:T(8,128)(2,1)}), bf16[512,2560]{0,1:T(8,128)(2,1)}) %reduce-scatter.26.cloned.1.call-update) | async-done | bytes 2621456 | tf_op jit(solution)/shard_map/reduce_scatter | solution.py:234
  1349.1 87.9 %reduce-scatter.22.cloned.1.call-done = bf16[512,2560]{1,0:T(8,128)(2,1)} async-done(((bf16[2048,2560]{1,0:T(8,128)(2,1)}), bf16[512,2560]{1,0:T(8,128)(2,1)}) %reduce-scatter.22.cloned.1.call-update) | async-done | bytes 2621456 | tf_op jit(solution)/shard_map/reduce_scatter | solution.py:228
  1437.0 87.8 %reduce-scatter.24.cloned.1.call-done = bf16[512,2560]{1,0:T(8,128)(2,1)} async-done(((bf16[2048,2560]{1,0:T(8,128)(2,1)}), bf16[512,2560]{1,0:T(8,128)(2,1)}) %reduce-scatter.24.cloned.1.call-update) | async-done | bytes 2621456 | tf_op jit(solution)/shard_map/reduce_scatter | solution.py:231
  1524.8 111.3 %all-reduce.14.cloned.1.call-done = (bf16[512,2048]{1,0:T(8,128)(2,1)}, bf16[512,2048]{1,0:T(8,128)(2,1)}) async-done(((bf16[512,2048]{1,0:T(8,128)(2,1)}, bf16[512,2048]{1,0:T(8,128)(2,1)}), (bf16[512,2048]{1,0:T(8,128)(2,1)}, bf16[512,2048]{1,0:T(8,128)(2,1)})) %all-reduce.14.cloned.1.call-update) | async-done | bytes 4194320 | tf_op jit(solution)/shard_map/psum | solution.py:120
  1639.3 77.8 %all-reduce = (f32[2048]{0:T(1024)}, f32[2048]{0:T(1024)}, f32[32,16]{0,1:T(8,128)}) all-reduce(f32[2048]{0:T(1024)S(1)} %get-tuple-element.212, f32[2048]{0:T(1024)S(1)} %copy-done.30, f32[32,16]{0,1:T(8,128)S(1)} %reduce_sum.87), channel_id=1, replica_groups=mesh['shard'=4,'ctx'=4,'tp'=2] {'shard','ctx'}, use_global_device_ids=true, to_apply=%region_32.33 | all-reduce | flops 4608 | bytes 36864 | tf_op jit(solution)/shard_map/psum | solution.py:214
  1724.2 331.5 %all-reduce.12.cloned.1.call-done = (bf16[512,2560]{0,1:T(8,128)(2,1)}, bf16[512,1024]{1,0:T(8,128)(2,1)}, bf16[512,1024]{1,0:T(8,128)(2,1)}, bf16[512,1024]{1,0...) async-done(((bf16[512,2560]{0,1:T(8,128)(2,1)}, bf16[512,1024]{1,0:T(8,128)(2,1)}, bf16[512,1024]{1,0:T(8,128)(2,1)}, ...) | async-done | bytes 12058640 | tf_op jit(solution)/shard_map/psum | solution.py:245
  (268 shorter events, 452.5 us)
Async XLA Ops:
  7.2 39.6 %all-gather.10.cloned.1.call-start = ((), (), s32[]{:S(2)}) async-start(), calls=%async_computation.9 | async-start | bytes 5242880 | tf_op jit(solution)/shard_map/all_gather | solution.py:58
  7.9 74.9 %all-gather.16.cloned.1.call-start = ((), (), s32[]{:S(2)}) async-start(), calls=%async_computation.12 | async-start | bytes 5242880 | tf_op jit(solution)/shard_map/all_gather | solution.py:57
  8.7 110.3 %all-gather.14.cloned.1.call-start = ((), (), s32[]{:S(2)}) async-start(), calls=%async_computation.11 | async-start | bytes 5242880 | tf_op jit(solution)/shard_map/all_gather | solution.py:56
  9.4 192.1 %all-gather.12.cloned.1.call-start = ((), (), s32[]{:S(2)}) async-start(), calls=%async_computation.10 | async-start | bytes 5242880 | tf_op jit(solution)/shard_map/all_gather | solution.py:70
  53.3 229.0 %all-gather.18.cloned.1.call-start = ((), (), s32[]{:S(2)}) async-start(), calls=%async_computation.13 | async-start | bytes 5242880 | tf_op jit(solution)/shard_map/all_gather | solution.py:69
  90.8 258.1 %all-gather.20.cloned.1.call-start = ((), (), s32[]{:S(2)}) async-start(), calls=%async_computation.14 | async-start | bytes 5242880 | tf_op jit(solution)/shard_map/all_gather | solution.py:59
  91.4 325.1 %all-reduce.8.cloned.1.call-start = ((), (), s32[]{:S(2)}) async-start(), calls=%async_computation.15 | async-start | bytes 4194304 | tf_op jit(solution)/shard_map/psum | solution.py:108
  115.7 166.6 %copy-start.25 = (f32[2,16,256]{2,1,0:T(8,128)S(1)}, f32[2,16,256]{2,1,0:T(8,128)}, u32[]{:S(2)}) copy-start(f32[2,16,256]{2,1,0:T(8,128)} %custom-call.1) | copy-start | bytes 98308
  355.5 132.8 %all-gather.22.cloned.1.call-start = ((), (), s32[]{:S(2)}) async-start(), calls=%async_computation.16 | async-start | bytes 13107200 | tf_op jit(solution)/shard_map/all_gather | solution.py:111
  356.3 204.0 %all-gather.24.cloned.1.call-start = ((), (), s32[]{:S(2)}) async-start(), calls=%async_computation.17 | async-start | bytes 13107200 | tf_op jit(solution)/shard_map/all_gather | solution.py:112
  357.0 274.9 %all-gather.26.cloned.1.call-start = ((), (), s32[]{:S(2)}) async-start(), calls=%async_computation.18 | async-start | bytes 13107200 | tf_op jit(solution)/shard_map/all_gather | solution.py:113
  357.6 370.2 %all-reduce.10.cloned.1.call-start = ((), (), s32[]{:S(2)}) async-start(), calls=%async_computation.19 | async-start | bytes 4194304 | tf_op jit(solution)/shard_map/psum | solution.py:132
  664.7 326.1 %reduce-scatter.10.cloned.1.call-start = ((), (), s32[]{:S(2)}) async-start(), calls=%async_computation.20 | async-start | bytes 5242880 | tf_op jit(solution)/shard_map/reduce_scatter | solution.py:190
  913.9 157.2 %reduce-scatter.12.cloned.1.call-start = ((), (), s32[]{:S(2)}) async-start(), calls=%async_computation.21 | async-start | bytes 5242880 | tf_op jit(solution)/shard_map/reduce_scatter | solution.py:193
  914.6 217.0 %reduce-scatter.14.cloned.1.call-start = ((), (), s32[]{:S(2)}) async-start(), calls=%async_computation.22 | async-start | bytes 5242880 | tf_op jit(solution)/shard_map/reduce_scatter | solution.py:216
  920.4 245.8 %reduce-scatter.20.cloned.1.call-start = ((), (), s32[]{:S(2)}) async-start(), calls=%async_computation.25 | async-start | bytes 5242880 | tf_op jit(solution)/shard_map/reduce_scatter | solution.py:225
  927.4 286.2 %reduce-scatter.16.cloned.1.call-start = ((), (), s32[]{:S(2)}) async-start(), calls=%async_computation.23 | async-start | bytes 5242880 | tf_op jit(solution)/shard_map/reduce_scatter | solution.py:219
  996.6 264.7 %reduce-scatter.18.cloned.1.call-start = ((), (), s32[]{:S(2)}) async-start(), calls=%async_computation.24 | async-start | bytes 5242880 | tf_op jit(solution)/shard_map/reduce_scatter | solution.py:222
  1076.8 272.3 %reduce-scatter.26.cloned.1.call-start = ((), (), s32[]{:S(2)}) async-start(), calls=%async_computation.28 | async-start | bytes 13107200 | tf_op jit(solution)/shard_map/reduce_scatter | solution.py:234
  1087.4 349.6 %reduce-scatter.22.cloned.1.call-start = ((), (), s32[]{:S(2)}) async-start(), calls=%async_computation.26 | async-start | bytes 13107200 | tf_op jit(solution)/shard_map/reduce_scatter | solution.py:228
  1097.7 427.1 %reduce-scatter.24.cloned.1.call-start = ((), (), s32[]{:S(2)}) async-start(), calls=%async_computation.27 | async-start | bytes 13107200 | tf_op jit(solution)/shard_map/reduce_scatter | solution.py:231
  1108.1 528.0 %all-reduce.14.cloned.1.call-start = ((), (), s32[]{:S(2)}) async-start(), calls=%async_computation.30 | async-start | bytes 8388608 | tf_op jit(solution)/shard_map/psum | solution.py:120
  1131.5 924.1 %all-reduce.12.cloned.1.call-start = ((), (), s32[]{:S(2)}) async-start(), calls=%async_computation.29 | async-start | bytes 24117248 | tf_op jit(solution)/shard_map/psum | solution.py:245
  1524.8 114.5 %copy-start.30 = (f32[2048]{0:T(1024)S(1)}, f32[2048]{0:T(1024)}, u32[]{:S(2)}) copy-start(f32[2048]{0:T(1024)} %get-tuple-element.210) | copy-start | bytes 24580
  (55 other events, 760.1 us)
Sparse Core Ops, SparseCore 0:
  9.6 37.1 all-gather.9
  48.4 34.4 all-gather.15
  84.5 34.4 all-gather.13
  121.0 80.5 all-gather.11
  203.5 78.7 all-gather.17
  283.7 32.6 all-gather.19
  355.6 60.8 all-reduce.7
  418.1 70.1 all-gather.21
  490.0 70.1 all-gather.23
  561.7 70.1 all-gather.25
  664.8 62.9 all-reduce.9
  914.0 76.7 reduce-scatter.9
  993.7 77.2 reduce-scatter.11
  1074.0 44.9 reduce-scatter.13
  1121.6 44.5 reduce-scatter.19
  1169.1 44.4 reduce-scatter.15
  1216.7 44.5 reduce-scatter.17
  1263.7 85.2 reduce-scatter.25
  1351.7 85.2 reduce-scatter.21
  1439.4 85.2 reduce-scatter.23
  1527.9 108.2 all-reduce.13
  1640.0 415.6 all-reduce.11
where the time goes:
time: 2090 us; the launch traced here: 2080 us
  waiting for transfers between devices  1500 us (72%)
  matrix products  321 us (15%)
  other arithmetic  87.2 us (4%)
  blocking collectives  77.8 us (4%)
  local copies, waits for them, and re-layouts  76.4 us (4%)
    psum x1, waiting for transfers between devices, per_device(): lax.psum(pieces[6].astype(jnp.bfloat16), 'ctx').astype(jnp.float32)  331 us
    psum x1, waiting for transfers between devices, per_device(): lax.psum(contract_cols(inner, wff).astype(jnp.bfloat16), 'tp')  111 us
    reduce_scatter x1, waiting for transfers between devices, per_device(): lax.psum_scatter(grad_gate_w.astype(jnp.bfloat16), 'shard', scatter_dimen...  87.9 us
    reduce_scatter x1, waiting for transfers between devices, per_device(): lax.psum_scatter(grad_down_w.astype(jnp.bfloat16), 'shard', scatter_dimen...  87.8 us
    reduce_scatter x1, waiting for transfers between devices, per_device(): lax.psum_scatter(grad_up_w.astype(jnp.bfloat16), 'shard', scatter_dimensi...  87.8 us
    all_gather x1, waiting for transfers between devices, per_device(): lax.all_gather(key.reshape(seqs, local_len, inner_width), 'ctx', axis=1,...  80.8 us
    psum x1, blocking collectives, per_device(): lax.psum((grad_norm_gain, grad_ffn_gain, grad_table), ('shard', 'ctx'))  77.8 us
    all_gather x1, waiting for transfers between devices, per_device(): lax.all_gather(value.reshape(seqs, local_len, inner_width), 'ctx', axis=1...  76.9 us
  transfers between devices with their start and end apart: 22, of which 20 were waited for; matrix products, arithmetic and copies ran while one was open for 11% of the time, Pallas kernels for 0%

commit v1 on v0

v1 whole, which is shorter than its diff:
```python
import functools

import jax
import jax.numpy as jnp
from jax import lax
from jax.experimental import pallas as pl
from jax.experimental.pallas import tpu as pltpu
from jax.sharding import PartitionSpec as P

F32 = jnp.float32
BF16 = jnp.bfloat16
VMEM_LIMIT = 48 * 2**20


def contract_rows(left, right):
    return lax.dot_general(left, right, (((0,), (0,)), ((), ())), preferred_element_type=F32)


def contract_cols(left, right):
    return lax.dot_general(left, right, (((1,), (1,)), ((), ())), preferred_element_type=F32)


def dot(left, right):
    return jnp.dot(left, right, preferred_element_type=F32)


def rms_scale(values):
    return lax.rsqrt(jnp.mean(values * values, axis=-1, keepdims=True) + 1e-06)


def rms_back(values, scale, gain, upstream):
    weighted = upstream * gain
    inner_average = jnp.mean(values * weighted, axis=-1, keepdims=True)
    return scale * weighted - values * scale * scale * scale * inner_average


def geglu(gate, up):
    return jax.nn.gelu(gate, approximate=True) * up


def bias_rows(table_row, out):
    span = out.shape[1]
    out[0:1, :] = table_row
    done = 1
    while done < out.shape[0]:
        out[done : 2 * done, :] = pltpu.roll(out[0:done, :], done, 1)
        done *= 2
    del span


def diagonal_sums(acc):
    rows, span = acc.shape
    total = acc[...]
    while rows > 1:
        rows //= 2
        total = total[:rows] + pltpu.roll(total[rows:], span - rows, 1)
    return total


def head_mask(shape, head, head_dim):
    lane = lax.broadcasted_iota(jnp.int32, shape, 1)
    return (lane >= head * head_dim) & (lane < (head + 1) * head_dim)


def window(me, n, part, query, key):
    q_at = lax.rem(me - query + n, n)
    k_at = lax.rem(me - key + n, n)
    return pl.multiple_of((n + k_at - q_at) * part, part)


def attend_kernel(n, head_dim, me_ref, table_ref, *refs):
    pieces, outs, lse_ref, bias, keys, values = (
        refs[:n], refs[n : 2 * n], refs[2 * n], refs[2 * n + 1], refs[2 * n + 2], refs[2 * n + 3],
    )
    part, lanes = pieces[0].shape[2:]
    per = lanes // head_dim
    me = me_ref[0]

    @pl.when(pl.program_id(1) == 0)
    def _():
        for head in range(per):
            bias_rows(table_ref[0, head : head + 1, :], bias.at[head])

    for b in range(n):
        keys[b * part : (b + 1) * part, :] = pieces[b][1, 0]
        values[b * part : (b + 1) * part, :] = pieces[b][2, 0]
    for a in range(n):
        lse = jnp.zeros((part, lanes), F32)
        mixed = jnp.zeros((part, lanes), F32)
        lane = lax.broadcasted_iota(jnp.int32, (part, lanes), 1)
        for head in range(per):
            mask = head_mask((part, lanes), head, head_dim)
            query = jnp.where(mask, pieces[a][0, 0], 0)
            scores = contract_cols(query, keys[...])
            scores = scores + jnp.concatenate(
                [bias[head, :, pl.ds(window(me, n, part, a, b), part)] for b in range(n)], axis=1
            )
            peak = jnp.max(scores, axis=1, keepdims=True)
            expo = jnp.exp(scores - peak)
            total = jnp.sum(expo, axis=1, keepdims=True)
            probs = (expo * (1.0 / total)).astype(BF16)
            mixed = jnp.where(mask, dot(probs, values[...]), mixed)
            lse = jnp.where(lane == head, peak + jnp.log(total), lse)
        outs[a][0] = mixed.astype(BF16)
        lse_ref[0, 0, a] = lse


def attend_back_kernel(n, head_dim, me_ref, table_ref, *refs):
    pieces, grads, lse_ref = refs[:n], refs[n : 2 * n], refs[2 * n]
    outs, table_out = refs[2 * n + 1 : 3 * n + 1], refs[3 * n + 1]
    bias, sums, keys, values, grad_k, grad_v = refs[3 * n + 2 :]
    part, lanes = pieces[0].shape[2:]
    per = lanes // head_dim
    me = me_ref[0]

    @pl.when(pl.program_id(1) == 0)
    def _():
        for head in range(per):
            bias_rows(table_ref[0, head : head + 1, :], bias.at[head])
        sums[...] = jnp.zeros_like(sums)

    for b in range(n):
        keys[b * part : (b + 1) * part, :] = pieces[b][1, 0]
        values[b * part : (b + 1) * part, :] = pieces[b][2, 0]
    grad_k[...] = jnp.zeros_like(grad_k)
    grad_v[...] = jnp.zeros_like(grad_v)
    for a in range(n):
        grad_q = jnp.zeros((part, lanes), F32)
        for head in range(per):
            mask = head_mask((part, lanes), head, head_dim)
            query = jnp.where(mask, pieces[a][0, 0], 0)
            upstream = jnp.where(mask, grads[a][0], 0)
            starts = [window(me, n, part, a, b) for b in range(n)]
            scores = contract_cols(query, keys[...])
            scores = scores + jnp.concatenate(
                [bias[head, :, pl.ds(start, part)] for start in starts], axis=1
            )
            probs = jnp.exp(scores - lse_ref[0, 0, a][:, head : head + 1])
            grad_probs = contract_cols(upstream, values[...])
            delta = jnp.sum(grad_probs * probs, axis=1, keepdims=True)
            grad_scores = (probs * (grad_probs - delta)).astype(BF16)
            for b, start in enumerate(starts):
                sums[head, :, pl.ds(start, part)] += grad_scores[:, b * part : (b + 1) * part].astype(F32)
            grad_q = jnp.where(mask, dot(grad_scores, keys[...]), grad_q)
            grad_k[...] += contract_rows(grad_scores, query)
            grad_v[...] += contract_rows(probs.astype(BF16), upstream)
        outs[a][0, 0] = grad_q.astype(BF16)
    for b in range(n):
        outs[b][1, 0] = grad_k[b * part : (b + 1) * part, :].astype(BF16)
        outs[b][2, 0] = grad_v[b * part : (b + 1) * part, :].astype(BF16)

    @pl.when(pl.program_id(1) == pl.num_programs(1) - 1)
    def _():
        for head in range(per):
            table_out[0, head : head + 1, :] = diagonal_sums(sums.at[head])


def attention_calls(n, seqs, part, cols, head_dim):
    lanes = 2 * head_dim
    groups, per, span = cols // lanes, lanes // head_dim, 2 * n * part
    smem = pl.BlockSpec(memory_space=pltpu.SMEM)
    table_spec = pl.BlockSpec((1, per, span), lambda g, s: (g, 0, 0))
    three = pl.BlockSpec((3, 1, part, lanes), lambda g, s: (0, s, 0, g))
    one = pl.BlockSpec((1, part, lanes), lambda g, s: (s, 0, g))
    lse_spec = pl.BlockSpec((1, 1, n, part, lanes), lambda g, s: (g, s, 0, 0, 0))
    piece = jax.ShapeDtypeStruct((3, seqs, part, cols), BF16)
    single = jax.ShapeDtypeStruct((seqs, part, cols), BF16)
    lse = jax.ShapeDtypeStruct((groups, seqs, n, part, lanes), F32)
    table = jax.ShapeDtypeStruct((groups, per, span), F32)
    length = n * part
    pairs = seqs * (cols // head_dim) * length * length
    forward = pl.pallas_call(
        functools.partial(attend_kernel, n, head_dim),
        grid=(groups, seqs),
        in_specs=[smem, table_spec] + [three] * n,
        out_specs=[one] * n + [lse_spec],
        out_shape=[single] * n + [lse],
        scratch_shapes=[
            pltpu.VMEM((per, part, span), F32),
            pltpu.VMEM((length, lanes), BF16),
            pltpu.VMEM((length, lanes), BF16),
        ],
        compiler_params=pltpu.CompilerParams(vmem_limit_bytes=VMEM_LIMIT),
        cost_estimate=pl.CostEstimate(
            flops=4 * pairs * 256, bytes_accessed=2**23, transcendentals=pairs
        ),
        name="attend",
    )
    backward = pl.pallas_call(
        functools.partial(attend_back_kernel, n, head_dim),
        grid=(groups, seqs),
        in_specs=[smem, table_spec] + [three] * n + [one] * n + [lse_spec],
        out_specs=[three] * n + [table_spec],
        out_shape=[piece] * n + [table],
        scratch_shapes=[
            pltpu.VMEM((per, part, span), F32),
            pltpu.VMEM((per, part, span), F32),
            pltpu.VMEM((length, lanes), BF16),
            pltpu.VMEM((length, lanes), BF16),
            pltpu.VMEM((length, lanes), F32),
            pltpu.VMEM((length, lanes), F32),
        ],
        compiler_params=pltpu.CompilerParams(vmem_limit_bytes=VMEM_LIMIT),
        cost_estimate=pl.CostEstimate(
            flops=10 * pairs * 256, bytes_accessed=2**24, transcendentals=pairs
        ),
        name="attend_back",
    )
    return forward, backward


def ring(n, d):
    return [(i, (i + d) % n) for i in range(n)]


class Links:
    def __init__(self, mesh):
        self.shard, self.ctx, self.tp = mesh.shape["shard"], mesh.shape["ctx"], mesh.shape["tp"]
        self.chips = self.shard // 2

    def to_core(self, value):
        return lax.ppermute(value, "shard", [(i, i ^ 1) for i in range(self.shard)])

    def to_chip(self, value, d):
        n = self.shard
        return lax.ppermute(value, "shard", [(i, (i + 2 * d) % n) for i in range(n)])

    def tp_sum(self, value):
        if self.tp != 2:
            return lax.psum(value, "tp").astype(F32)
        other = lax.ppermute(value, "tp", ring(2, 1))
        return value.astype(F32) + other.astype(F32)

    def ctx_sum(self, value):
        low = value.astype(BF16)
        if self.ctx != 4:
            return lax.psum(low, "ctx").astype(F32)
        inward = lax.ppermute(low, "ctx", [(0, 1), (3, 2)])
        half = (low.astype(F32) + inward.astype(F32)).astype(BF16)
        across = lax.ppermute(half, "ctx", [(1, 2), (2, 1)])
        whole = (half.astype(F32) + across.astype(F32)).astype(BF16)
        outward = lax.ppermute(whole, "ctx", [(1, 0), (2, 3)])
        me = lax.axis_index("ctx")
        middle = (me == 1) | (me == 2)
        return jnp.where(middle, whole, outward).astype(F32)

    def shard_sums(self, left, right):
        n, chips = self.shard, self.chips
        rows = left.shape[1] // n
        me = lax.axis_index("shard")
        chip, core = me // 2, me % 2

        def term(chip_at, core_at):
            at = (2 * chip_at + core_at) * rows
            return contract_rows(lax.dynamic_slice_in_dim(left, at, rows, 1), right)

        def chip_of(d):
            return lax.rem(chip + d, chips)

        order = list(range(1, chips)) + [0]
        got = {d: self.to_core(term(chip_of(d), 1 - core).astype(BF16)) for d in order}
        total = None
        arrived = []
        for d in order:
            pair = term(chip_of(d), core) + got[d].astype(F32)
            if d:
                arrived.append(self.to_chip(pair.astype(BF16), d))
            else:
                total = pair
        for value in arrived:
            total = total + value.astype(F32)
        return total

    def small_sum(self, value):
        for axis, n in (("shard", self.shard), ("ctx", self.ctx)):
            step = 1
            while step < n:
                value = value + lax.ppermute(value, axis, [(i, i ^ step) for i in range(n)])
                step *= 2
        return value


def per_device(
    links,
    tokens,
    cotangent,
    buckets,
    query_weight,
    key_weight,
    value_weight,
    output_weight,
    gate_weight,
    up_weight,
    down_weight,
    norm_gain,
    ffn_gain,
    bucket_bias_table,
):
    seqs, part, width = tokens.shape
    rows = seqs * part
    slots, heads = bucket_bias_table.shape
    inner_width = query_weight.shape[1]
    head_dim = inner_width // heads
    n = links.ctx
    cols = inner_width // n
    own_heads = heads // n
    me = lax.axis_index("ctx")
    gain_one = norm_gain.astype(F32)
    gain_two = ffn_gain.astype(F32)

    def gathered(weight):
        return lax.all_gather(weight, "shard", axis=0, tiled=True)

    def at_ctx(d):
        return lax.rem(me + d + n, n)

    corner = lax.dynamic_slice(buckets, (0, me * part), (part, part))
    later, earlier = corner[0, :], corner[:, 0]
    reach = n * part
    by_offset = jnp.concatenate(
        [
            jnp.broadcast_to(earlier[part - 1 :], (reach - part + 1,)),
            earlier[:0:-1],
            later,
            jnp.broadcast_to(later[part - 1 :], (reach - part,)),
        ]
    )
    indicator = by_offset[None, :] == jnp.arange(slots, dtype=jnp.int32)[:, None]
    own_table = lax.dynamic_slice(bucket_bias_table, (0, me * own_heads), (slots, own_heads))
    offset_bias = lax.dot_general(
        own_table, indicator.astype(BF16), (((0,), (0,)), ((), ())), preferred_element_type=F32
    )
    groups = cols // (2 * head_dim)
    offset_bias = offset_bias.reshape(groups, 2, 2 * reach)
    where_am_i = me.astype(jnp.int32).reshape(1)
    attend, attend_back = attention_calls(n, seqs, part, cols, head_dim)

    wq, wk, wv = gathered(query_weight), gathered(key_weight), gathered(value_weight)
    inputs = tokens.reshape(rows, width).astype(F32)
    scale_one = rms_scale(inputs)
    normed = (inputs * scale_one * gain_one).astype(BF16)
    projected = [dot(normed, w).astype(BF16) for w in (wq, wk, wv)]

    def heads_of(values, d):
        start = at_ctx(d) * cols
        return [lax.dynamic_slice_in_dim(v, start, cols, 1).reshape(seqs, part, cols) for v in values]

    pieces = [jnp.stack(heads_of(projected, d)) for d in range(n)]
    pieces = [pieces[0]] + [lax.ppermute(pieces[d], "ctx", ring(n, d)) for d in range(1, n)]
    *mixed, lse = attend(where_am_i, offset_bias, *pieces)

    def heads_back(blocks):
        blocks = [blocks[0]] + [lax.ppermute(blocks[d], "ctx", ring(n, n - d)) for d in range(1, n)]
        around = jnp.concatenate(blocks, axis=-1)
        twice = jnp.concatenate([around, around], axis=-1)
        return lax.dynamic_slice_in_dim(twice, (n - me) * cols, n * cols, around.ndim - 1)

    attended = heads_back(mixed).reshape(rows, inner_width)
    wo = gathered(output_weight)
    branch = links.tp_sum(contract_cols(attended, wo).astype(BF16))
    hidden = inputs + branch
    wi0, wi1, wff = gathered(gate_weight), gathered(up_weight), gathered(down_weight)
    scale_two = rms_scale(hidden)
    normed_two = (hidden * scale_two * gain_two).astype(BF16)
    gate = dot(normed_two, wi0)
    up = dot(normed_two, wi1)
    inner = geglu(gate, up).astype(BF16)
    ffn_out = links.tp_sum(contract_cols(inner, wff).astype(BF16))
    result = (hidden + ffn_out).astype(BF16).reshape(seqs, part, width)

    upstream = cotangent.reshape(rows, width).astype(F32)
    upstream_low = cotangent.reshape(rows, width)
    grad_down_w = links.ctx_sum(links.shard_sums(upstream_low, inner))
    grad_inner = dot(upstream_low, wff)
    unused, geglu_backward_pull = jax.vjp(geglu, gate, up)
    grad_gate, grad_up = geglu_backward_pull(grad_inner)
    grad_gate = grad_gate.astype(BF16)
    grad_up = grad_up.astype(BF16)
    grad_normed_two = links.tp_sum(
        (contract_cols(grad_gate, wi0) + contract_cols(grad_up, wi1)).astype(BF16)
    )
    grad_gate_w = links.ctx_sum(links.shard_sums(normed_two, grad_gate))
    grad_up_w = links.ctx_sum(links.shard_sums(normed_two, grad_up))
    grad_ffn_gain = jnp.sum(grad_normed_two * hidden * scale_two, axis=0)
    grad_hidden = upstream + rms_back(hidden, scale_two, gain_two, grad_normed_two)
    branch_low = grad_hidden.astype(BF16)
    grad_attended = dot(branch_low, wo).astype(BF16)
    grad_output_w = links.ctx_sum(links.shard_sums(branch_low, attended))

    upstreams = [heads_of([grad_attended], d)[0] for d in range(n)]
    upstreams = [upstreams[0]] + [lax.ppermute(upstreams[d], "ctx", ring(n, d)) for d in range(1, n)]
    *grad_pieces, offset_grad = attend_back(where_am_i, offset_bias, *pieces, *upstreams, lse)
    grad_projected = heads_back(grad_pieces).reshape(3, rows, inner_width)
    grad_query, grad_key, grad_value = grad_projected[0], grad_projected[1], grad_projected[2]
    offset_grad = offset_grad.reshape(own_heads, 2 * reach)
    table_part = jnp.sum(jnp.where(indicator[:, None, :], offset_grad[None], 0.0), axis=-1)
    grad_table = lax.dynamic_update_slice(
        jnp.zeros((slots, heads), F32), table_part, (0, me * own_heads)
    )

    grad_normed = links.tp_sum(
        (contract_cols(grad_query, wq) + contract_cols(grad_key, wk) + contract_cols(grad_value, wv)).astype(BF16)
    )
    grad_query_w = links.ctx_sum(links.shard_sums(normed, grad_query))
    grad_key_w = links.ctx_sum(links.shard_sums(normed, grad_key))
    grad_value_w = links.ctx_sum(links.shard_sums(normed, grad_value))
    grad_norm_gain = jnp.sum(grad_normed * inputs * scale_one, axis=0)
    grad_inputs = grad_hidden + rms_back(inputs, scale_one, gain_one, grad_normed)
    small = links.small_sum(jnp.concatenate([grad_norm_gain, grad_ffn_gain, grad_table.reshape(-1)]))
    return (
        result,
        grad_inputs.reshape(seqs, part, width),
        grad_query_w,
        grad_key_w,
        grad_value_w,
        grad_output_w,
        grad_gate_w,
        grad_up_w,
        grad_down_w,
        small[:width],
        small[width : 2 * width],
        small[2 * width :].reshape(slots, heads),
    )


def solution(mesh):
    rows, weights = P("shard", "ctx", None), P("shard", "tp")
    return jax.shard_map(
        functools.partial(per_device, Links(mesh)),
        mesh=mesh,
        in_specs=(rows, rows, P("ctx", None)) + (weights,) * 7 + (P(), P(), P(None, "tp")),
        out_specs=(rows, rows) + (weights,) * 7 + (P(), P(), P(None, "tp")),
        check_vma=False,
    )
```

time: 2090 us -> 1430 us (0.68)
  waiting for transfers between devices: 1500 us -> 998 us
  matrix products: 321 us -> 172 us
  blocking collectives: 77.8 us -> 0 us
  starting transfers between devices: 1.1 us -> 75.4 us
  Pallas kernels: 0 us -> 68 us
  local copies, waits for them, and re-layouts: 76.4 us -> 14.7 us
    ppermute x0 -> x62, waiting for transfers between devices: none -> 863 us  [the longest x7 249 us: ctx_sum(): outward = lax.ppermute(whole, 'ctx', [(1, 0), (2, 3)])]
    psum x4 -> x0, waiting for transfers between devices: 565 us -> none  [the longest x1 331 us: per_device(): lax.psum(pieces[6].astype(jnp.bfloat16), 'ctx').astype(jnp.float32)]
    reduce_scatter x9 -> x0, waiting for transfers between devices: 531 us -> none  [the longest x1 87.9 us: per_device(): lax.psum_scatter(grad_gate_w.astype(jnp.bfloat16), 'shard', scatter_dimen...]
    all_gather x9 -> x7, waiting for transfers between devices: 400 us -> 131 us  [gathered(): return lax.all_gather(weight, 'shard', axis=0, tiled=True)]
    dot_general x24 -> x8, matrix products: 222 us -> 52.8 us  [the longest x7 52.6 us: dot(): return jnp.dot(left, right, preferred_element_type=F32)]
    psum x1 -> x0, blocking collectives: 77.8 us -> none  [per_device(): lax.psum((grad_norm_gain, grad_ffn_gain, grad_table), ('shard', 'ctx'))]
    ppermute x0 -> x62, starting transfers between devices: none -> 75.2 us  [the longest x7 21.8 us: ctx_sum(): inward = lax.ppermute(low, 'ctx', [(0, 1), (3, 2)])]
    pallas_call x0 -> x2, Pallas kernels: none -> 68 us  [the longest x1 41.6 us: per_device(): attend_back(where_am_i, offset_bias, *pieces, *upstreams, lse)]
  transfers between devices with their start and end apart: 22 -> 69, of which waited for: 20 -> 28; matrix products, arithmetic and copies ran while one was open for 11% -> 16% of each run, Pallas kernels for 0% -> 5%
where the time goes in v1:
time: 1430 us; the launch traced here: 1420 us
  waiting for transfers between devices  998 us (70%)
  matrix products  172 us (12%)
  other arithmetic  77 us (5%)
  starting transfers between devices  75.4 us (5%)
  Pallas kernels  68 us (5%)
  between operations  15.5 us (1%)
  local copies, waits for them, and re-layouts  14.7 us (1%)
    ppermute x7, waiting for transfers between devices, ctx_sum(): outward = lax.ppermute(whole, 'ctx', [(1, 0), (2, 3)])  249 us
    ppermute x7, waiting for transfers between devices, to_chip(): lax.ppermute(value, 'shard', [(i, (i + 2 * d) % n) for i in range(n)])  165 us
    all_gather x7, waiting for transfers between devices, gathered(): return lax.all_gather(weight, 'shard', axis=0, tiled=True)  131 us
    ppermute x7, waiting for transfers between devices, ctx_sum(): inward = lax.ppermute(low, 'ctx', [(0, 1), (3, 2)])  106 us
    ppermute x4, waiting for transfers between devices, small_sum(): value = value + lax.ppermute(value, axis, [(i, i ^ step) for i in range(n)])  102 us
    ppermute x4, waiting for transfers between devices, tp_sum(): other = lax.ppermute(value, 'tp', ring(2, 1))  95.8 us
    ppermute x6, waiting for transfers between devices, heads_back(): lax.ppermute(blocks[d], 'ctx', ring(n, n - d))  70.5 us
    dot_general x28, matrix products, contract_rows(): lax.dot_general(left, right, (((0,), (0,)), ((), ())), preferred_element_...  70.4 us
  transfers between devices with their start and end apart: 69, of which 28 were waited for; matrix products, arithmetic and copies ran while one was open for 16% of the time, Pallas kernels for 5%

profile of v1, /device:TPU:0, one launch (start us, length us, event | category | flops | bytes accessed | tf_op | source)
XLA Modules:
  0.0 1420.3 jit_solution(4036816653409929390)
XLA Ops:
  14.6 32.2 %all-gather.8.cloned.1.call-done = bf16[2048,1024]{1,0:T(8,128)(2,1)} async-done(((bf16[512,1024]{1,0:T(8,128)(2,1)}), bf16[2048,1024]{1,0:T(8,128)(2,1)}) %all-gather.8.cloned.1.call-update) | async-done | bytes 4194320 | tf_op jit(solution)/shard_map/all_gather | solution.py:312
  52.1 30.8 %all-gather.12.cloned.1.call-done = bf16[2048,1024]{1,0:T(8,128)(2,1)} async-done(((bf16[512,1024]{1,0:T(8,128)(2,1)}), bf16[2048,1024]{1,0:T(8,128)(2,1)}) %all-gather.12.cloned.1.call-update) | async-done | bytes 4194320 | tf_op jit(solution)/shard_map/all_gather | solution.py:312
  88.4 30.6 %all-gather.10.cloned.1.call-done = bf16[2048,1024]{1,0:T(8,128)(2,1)} async-done(((bf16[512,1024]{1,0:T(8,128)(2,1)}), bf16[2048,1024]{1,0:T(8,128)(2,1)}) %all-gather.10.cloned.1.call-update) | async-done | bytes 4194320 | tf_op jit(solution)/shard_map/all_gather | solution.py:312
  147.2 49.8 %collective-permute-done.1.refs_2_ = bf16[3,2,256,256]{3,2,1,0:T(8,128)(2,1)S(1)} collective-permute-done((bf16[3,2,256,256]{3,2,1,0:T(8,128)(2,1)}, bf16[3,2,256,256]{3,2,1,0:T(8,128)(2,1)S(1)}, u32[]{:S(2)}, u32[]{:S(2)}) %collective-permute-start.1) | collective-permute-done | bytes 786464 | tf_op jit(solution)/shard_map/ppermute | solution.py:349
  197.0 26.3 %attend.1 = (bf16[2,256,256]{2,1,0:T(8,128)(2,1)S(1)}, bf16[2,256,256]{2,1,0:T(8,128)(2,1)S(1)}, bf16[2,256,256]{2,1,0:T(8,128)(2,1)S(1)}, bf16[2,256,256]{2,1,0:T(8,128)(2,1)S(1)}, f32[2,2,4,256,128]{4,3,2,1,0:T(8,128)}) custom-call(s32[1]{0:T(128)} %bitcast.1.me_ref, f32[2,2,2048]{2,1,0:T(2,128)S(1)} %reshape.135.table_ref, ...), custom_call_target="tpu_custom_call" | custom-call | flops 8589934592 | bytes 8388608 | tf_op jit(solution)/shard_map/attend/pallas_call | solution.py:350
  231.1 18.7 %collective-permute-done.4 = bf16[2,256,256]{2,1,0:T(8,128)(2,1)S(1)} collective-permute-done((bf16[2,256,256]{2,1,0:T(8,128)(2,1)S(1)}, bf16[2,256,256]{2,1,0:T(8,128)(2,1)S(1)}, u32[]{:S(2)}, u32[]{:S(2)}) %collective-permute-start.4) | collective-permute-done | bytes 262176 | tf_op jit(solution)/shard_map/ppermute | solution.py:353
  259.0 45.8 %collective-permute-done.6 = bf16[512,2048]{1,0:T(8,128)(2,1)} collective-permute-done((bf16[512,2048]{1,0:T(8,128)(2,1)}, bf16[512,2048]{1,0:T(8,128)(2,1)}, u32[]{:S(2)}, u32[]{:S(2)}) %collective-permute-start.6) | collective-permute-done | bytes 2097184 | tf_op jit(solution)/shard_map/ppermute | solution.py:231
  332.8 37.2 %all-gather.16.cloned.1.call-done = bf16[2048,2560]{1,0:T(8,128)(2,1)} async-done(((bf16[512,2560]{1,0:T(8,128)(2,1)}), bf16[2048,2560]{1,0:T(8,128)(2,1)}) %all-gather.16.cloned.1.call-update) | async-done | bytes 10485776 | tf_op jit(solution)/shard_map/all_gather | solution.py:312
  453.0 42.7 %collective-permute-done.7 = bf16[512,2048]{1,0:T(8,128)(2,1)S(1)} collective-permute-done((bf16[512,2048]{1,0:T(8,128)(2,1)S(1)}, bf16[512,2048]{1,0:T(8,128)(2,1)S(1)}, u32[]{:S(2)}, u32[]{:S(2)}) %collective-permute-start.7) | collective-permute-done | bytes 2097184 | tf_op jit(solution)/shard_map/ppermute | solution.py:231
  529.9 41.6 %attend_back.1 = (bf16[3,2,256,256]{3,2,1,0:T(8,128)(2,1)S(1)}, bf16[3,2,256,256]{3,2,1,0:T(8,128)(2,1)}, bf16[3,2,256,256]{3,2,1,0:T(8,128)(2,1)S(1)}, bf16[3,2...) custom-call(s32[1]{0:T(128)} %bitcast.1.me_ref, f32[2,2,2048]{2,1,0:T(2,128)S(1)} %reshape.135.table_ref, ...), custom_call_target="tpu_custom_call" | custom-call | flops 21474836480 | bytes 16777216 | tf_op jit(solution)/shard_map/attend_back/pallas_call | solution.py:392
  597.3 49.2 %collective-permute-done.13 = bf16[3,2,256,256]{3,2,1,0:T(8,128)(2,1)S(1)} collective-permute-done((bf16[3,2,256,256]{3,2,1,0:T(8,128)(2,1)S(1)}, bf16[3,2,256,256]{3,2,1,0:T(8,128)(2,1)S(1)}, u32[]{:S(2)}, u32[]{:S(2)}) %collective-permute-start.13) | collective-permute-done | bytes 786464 | tf_op jit(solution)/shard_map/ppermute | solution.py:353
  676.6 50.8 %collective-permute-done.36 = bf16[512,1024]{1,0:T(8,128)(2,1)S(1)} collective-permute-done((bf16[512,1024]{1,0:T(8,128)(2,1)}, bf16[512,1024]{1,0:T(8,128)(2,1)S(1)}, u32[]{:S(2)}, u32[]{:S(2)}) %collective-permute-start.36) | collective-permute-done | bytes 1048608 | tf_op jit(solution)/shard_map/ppermute | solution.py:226
  749.5 44.7 %collective-permute-done.48 = bf16[512,2560]{1,0:T(8,128)(2,1)} collective-permute-done((bf16[512,2560]{1,0:T(8,128)(2,1)}, bf16[512,2560]{1,0:T(8,128)(2,1)}, u32[]{:S(2)}, u32[]{:S(2)}) %collective-permute-start.48) | collective-permute-done | bytes 2621472 | tf_op jit(solution)/shard_map/ppermute | solution.py:226
  801.9 48.5 %collective-permute-done.42 = bf16[512,2560]{1,0:T(8,128)(2,1)} collective-permute-done((bf16[512,2560]{1,0:T(8,128)(2,1)}, bf16[512,2560]{1,0:T(8,128)(2,1)}, u32[]{:S(2)}, u32[]{:S(2)}) %collective-permute-start.42) | collective-permute-done | bytes 2621472 | tf_op jit(solution)/shard_map/ppermute | solution.py:226
  856.8 15.9 %collective-permute-done.30 = bf16[512,1024]{1,0:T(8,128)(2,1)S(1)} collective-permute-done((bf16[512,1024]{1,0:T(8,128)(2,1)}, bf16[512,1024]{1,0:T(8,128)(2,1)S(1)}, u32[]{:S(2)}, u32[]{:S(2)}) %collective-permute-start.30) | collective-permute-done | bytes 1048608 | tf_op jit(solution)/shard_map/ppermute | solution.py:226
  874.8 20.4 %collective-permute-done.59 = f32[4608]{0:T(1024)S(1)} collective-permute-done((f32[4608]{0:T(1024)S(1)}, f32[4608]{0:T(1024)S(1)}, u32[]{:S(2)}, u32[]{:S(2)}) %collective-permute-start.59) | collective-permute-done | bytes 18464 | tf_op jit(solution)/shard_map/ppermute | solution.py:278
  921.4 81.7 %collective-permute-done.61 = f32[4608]{0:T(1024)S(1)} collective-permute-done((f32[4608]{0:T(1024)S(1)}, f32[4608]{0:T(1024)S(1)}, u32[]{:S(2)}, u32[]{:S(2)}) %collective-permute-start.61) | collective-permute-done | bytes 18464 | tf_op jit(solution)/shard_map/ppermute | solution.py:278
  1021.2 64.2 %collective-permute-done.19 = bf16[512,1024]{1,0:T(8,128)(2,1)S(1)} collective-permute-done((bf16[512,1024]{1,0:T(8,128)(2,1)}, bf16[512,1024]{1,0:T(8,128)(2,1)S(1)}, u32[]{:S(2)}, u32[]{:S(2)}) %collective-permute-start.19) | collective-permute-done | bytes 1048608 | tf_op jit(solution)/shard_map/ppermute | solution.py:238
  1097.0 41.6 %collective-permute-done.43 = bf16[512,2560]{1,0:T(8,128)(2,1)S(1)} collective-permute-done((bf16[512,2560]{1,0:T(8,128)(2,1)S(1)}, bf16[512,2560]{1,0:T(8,128)(2,1)S(1)}, u32[]{:S(2)}, u32[]{:S(2)}) %collective-permute-start.43) | collective-permute-done | bytes 2621472 | tf_op jit(solution)/shard_map/ppermute | solution.py:238
  1148.4 18.1 %collective-permute-done.33 = bf16[512,1024]{1,0:T(8,128)(2,1)S(1)} collective-permute-done((bf16[512,1024]{1,0:T(8,128)(2,1)S(1)}, bf16[512,1024]{1,0:T(8,128)(2,1)S(1)}, u32[]{:S(2)}, u32[]{:S(2)}) %collective-permute-start.33) | collective-permute-done | bytes 1048608 | tf_op jit(solution)/shard_map/ppermute | solution.py:242
  1186.8 25.3 %collective-permute-done.21 = bf16[512,1024]{1,0:T(8,128)(2,1)S(1)} collective-permute-done((bf16[512,1024]{1,0:T(8,128)(2,1)S(1)}, bf16[512,1024]{1,0:T(8,128)(2,1)S(1)}, u32[]{:S(2)}, u32[]{:S(2)}) %collective-permute-start.21) | collective-permute-done | bytes 1048608 | tf_op jit(solution)/shard_map/ppermute | solution.py:242
  1213.6 99.7 %collective-permute-done.57 = bf16[512,2560]{1,0:T(8,128)(2,1)S(1)} collective-permute-done((bf16[512,2560]{1,0:T(8,128)(2,1)S(1)}, bf16[512,2560]{1,0:T(8,128)(2,1)S(1)}, u32[]{:S(2)}, u32[]{:S(2)}) %collective-permute-start.57) | collective-permute-done | bytes 2621472 | tf_op jit(solution)/shard_map/ppermute | solution.py:242
  1316.0 53.5 %collective-permute-done.51 = bf16[512,2560]{1,0:T(8,128)(2,1)S(1)} collective-permute-done((bf16[512,2560]{1,0:T(8,128)(2,1)S(1)}, bf16[512,2560]{1,0:T(8,128)(2,1)S(1)}, u32[]{:S(2)}, u32[]{:S(2)}) %collective-permute-start.51) | collective-permute-done | bytes 2621472 | tf_op jit(solution)/shard_map/ppermute | solution.py:242
  1372.2 38.4 %collective-permute-done.45 = bf16[512,2560]{1,0:T(8,128)(2,1)S(1)} collective-permute-done((bf16[512,2560]{1,0:T(8,128)(2,1)S(1)}, bf16[512,2560]{1,0:T(8,128)(2,1)S(1)}, u32[]{:S(2)}, u32[]{:S(2)}) %collective-permute-start.45) | collective-permute-done | bytes 2621472 | tf_op jit(solution)/shard_map/ppermute | solution.py:242
  (366 shorter events, 397.2 us)
Async XLA Ops:
  8.7 110.3 %all-gather.10.cloned.1.call-start = ((), (), s32[]{:S(2)}) async-start(), calls=%async_computation.1 | async-start | bytes 5242880 | tf_op jit(solution)/shard_map/all_gather | solution.py:312
  9.4 241.7 %all-gather.14.cloned.1.call-start = ((), (), s32[]{:S(2)}) async-start(), calls=%async_computation.3 | async-start | bytes 5242880 | tf_op jit(solution)/shard_map/all_gather | solution.py:312
  10.0 301.2 %all-gather.18.cloned.1.call-start = ((), (), s32[]{:S(2)}) async-start(), calls=%async_computation.5 | async-start | bytes 13107200 | tf_op jit(solution)/shard_map/all_gather | solution.py:312
  10.6 311.8 %all-gather.20.cloned.1.call-start = ((), (), s32[]{:S(2)}) async-start(), calls=%async_computation.6 | async-start | bytes 13107200 | tf_op jit(solution)/shard_map/all_gather | solution.py:312
  11.2 358.8 %all-gather.16.cloned.1.call-start = ((), (), s32[]{:S(2)}) async-start(), calls=%async_computation.4 | async-start | bytes 13107200 | tf_op jit(solution)/shard_map/all_gather | solution.py:312
  431.9 142.7 %collective-permute-start.53 = (bf16[512,2560]{1,0:T(8,128)(2,1)}, bf16[512,2560]{1,0:T(8,128)(2,1)}, u32[]{:S(2)}, u32[]{:S(2)}) collective-permute-start(bf16[512,2560]{1,0:T(8,128)(2,1)} %convolution_convert_fusion), channel_id=1, source_target_pairs={{0,8},{8,0},{16,24},{24,16},{1,9},{9,1},{17,25},{25,17},{2,10},{10... | collective-permute-start | bytes 7864328 | tf_op jit(solution)/shard_map/ppermute | solution.py:222
  431.9 307.9 %collective-permute-start.52 = (bf16[512,2560]{1,0:T(8,128)(2,1)}, bf16[512,2560]{1,0:T(8,128)(2,1)}, u32[]{:S(2)}, u32[]{:S(2)}) collective-permute-start(bf16[512,2560]{1,0:T(8,128)(2,1)} %convolution_convert_fusion.1), channel_id=1, source_target_pairs={{0,8},{8,0},{16,24},{24,16},{1,9},{9,1},{17,25},{25,17},{2,10},{10... | collective-permute-start | bytes 7864328 | tf_op jit(solution)/shard_map/ppermute | solution.py:222
  596.7 78.3 %collective-permute-start.34 = (bf16[512,1024]{1,0:T(8,128)(2,1)S(1)}, bf16[512,1024]{1,0:T(8,128)(2,1)S(1)}, u32[]{:S(2)}, u32[]{:S(2)}) collective-permute-start(bf16[512,1024]{1,0:T(8,128)(2,1)S(1)} %copy-done.44), channel_id=1, source_target_pairs={{0,8},{8,0},{16,24},{24,16},{1,9},{9,1},{17,25},{25,17},{2,10},{10... | collective-permute-start | bytes 3145736 | tf_op jit(solution)/shard_map/ppermute | solution.py:222
  646.5 96.7 %collective-permute-start.54 = (bf16[512,2560]{1,0:T(8,128)(2,1)}, bf16[512,2560]{1,0:T(8,128)(2,1)}, u32[]{:S(2)}, u32[]{:S(2)}) collective-permute-start(bf16[512,2560]{1,0:T(8,128)(2,1)} %add_convert_fusion.3), channel_id=1, source_target_pairs={{0,16},{8,24},{16,0},{24,8},{1,17},{9,25},{17,1},{25,9},{2,18},{10... | collective-permute-start | bytes 7864328 | tf_op jit(solution)/shard_map/ppermute | solution.py:226
  740.0 110.4 %collective-permute-start.42 = (bf16[512,2560]{1,0:T(8,128)(2,1)}, bf16[512,2560]{1,0:T(8,128)(2,1)}, u32[]{:S(2)}, u32[]{:S(2)}) collective-permute-start(bf16[512,2560]{1,0:T(8,128)(2,1)} %add_convert_fusion.11), channel_id=1, source_target_pairs={{0,16},{8,24},{16,0},{24,8},{1,17},{9,25},{17,1},{25,9},{2,18},{10... | collective-permute-start | bytes 7864328 | tf_op jit(solution)/shard_map/ppermute | solution.py:226
  743.2 113.3 %collective-permute-start.28 = (bf16[512,1024]{1,0:T(8,128)(2,1)}, bf16[512,1024]{1,0:T(8,128)(2,1)S(1)}, u32[]{:S(2)}, u32[]{:S(2)}) collective-permute-start(bf16[512,1024]{1,0:T(8,128)(2,1)} %convolution_convert_fusion.11), channel_id=1, source_target_pairs={{0,8},{8,0},{16,24},{24,16},{1,9},{9,1},{17,25},{25,17},{2,10},{10... | collective-permute-start | bytes 3145736 | tf_op jit(solution)/shard_map/ppermute | solution.py:222
  748.9 149.6 %collective-permute-start.22 = (bf16[512,1024]{1,0:T(8,128)(2,1)}, bf16[512,1024]{1,0:T(8,128)(2,1)S(1)}, u32[]{:S(2)}, u32[]{:S(2)}) collective-permute-start(bf16[512,1024]{1,0:T(8,128)(2,1)} %convolution_convert_fusion.13), channel_id=1, source_target_pairs={{0,8},{8,0},{16,24},{24,16},{1,9},{9,1},{17,25},{25,17},{2,10},{10... | collective-permute-start | bytes 3145736 | tf_op jit(solution)/shard_map/ppermute | solution.py:222
  794.2 101.6 %collective-permute-start.37 = (bf16[512,1024]{1,0:T(8,128)(2,1)}, bf16[512,1024]{1,0:T(8,128)(2,1)S(1)}, u32[]{:S(2)}, u32[]{:S(2)}) collective-permute-start(bf16[512,1024]{1,0:T(8,128)(2,1)} %add_convert_fusion.17), channel_id=1, source_target_pairs={{0,2},{6,4},{1,3},{7,5},{8,10},{14,12},{9,11},{15,13},{16,18},{22,... | collective-permute-start | bytes 3145736 | tf_op jit(solution)/shard_map/ppermute | solution.py:238
  898.5 189.8 %collective-permute-start.55 = (bf16[512,2560]{1,0:T(8,128)(2,1)S(1)}, bf16[512,2560]{1,0:T(8,128)(2,1)}, u32[]{:S(2)}, u32[]{:S(2)}) collective-permute-start(bf16[512,2560]{1,0:T(8,128)(2,1)S(1)} %copy-done.18), channel_id=1, source_target_pairs={{0,2},{6,4},{1,3},{7,5},{8,10},{14,12},{9,11},{15,13},{16,18},{22,... | collective-permute-start | bytes 7864328 | tf_op jit(solution)/shard_map/ppermute | solution.py:238
  903.9 107.3 %collective-permute-start.38 = (bf16[512,1024]{1,0:T(8,128)(2,1)}, bf16[512,1024]{1,0:T(8,128)(2,1)}, u32[]{:S(2)}, u32[]{:S(2)}) collective-permute-start(bf16[512,1024]{1,0:T(8,128)(2,1)} %add_convert_fusion.16), channel_id=1, source_target_pairs={{2,4},{4,2},{3,5},{5,3},{10,12},{12,10},{11,13},{13,11},{18,20},{2... | collective-permute-start | bytes 3145736 | tf_op jit(solution)/shard_map/ppermute | solution.py:240
  905.5 102.1 %collective-permute-start.31 = (bf16[512,1024]{1,0:T(8,128)(2,1)}, bf16[512,1024]{1,0:T(8,128)(2,1)}, u32[]{:S(2)}, u32[]{:S(2)}) collective-permute-start(bf16[512,1024]{1,0:T(8,128)(2,1)} %add_convert_fusion.21), channel_id=1, source_target_pairs={{0,2},{6,4},{1,3},{7,5},{8,10},{14,12},{9,11},{15,13},{16,18},{22,... | collective-permute-start | bytes 3145736 | tf_op jit(solution)/shard_map/ppermute | solution.py:238
  912.9 101.6 %collective-permute-start.25 = (bf16[512,1024]{1,0:T(8,128)(2,1)}, bf16[512,1024]{1,0:T(8,128)(2,1)}, u32[]{:S(2)}, u32[]{:S(2)}) collective-permute-start(bf16[512,1024]{1,0:T(8,128)(2,1)} %add_convert_fusion.25), channel_id=1, source_target_pairs={{0,2},{6,4},{1,3},{7,5},{8,10},{14,12},{9,11},{15,13},{16,18},{22,... | collective-permute-start | bytes 3145736 | tf_op jit(solution)/shard_map/ppermute | solution.py:238
  919.9 83.2 %collective-permute-start.61 = (f32[4608]{0:T(1024)S(1)}, f32[4608]{0:T(1024)S(1)}, u32[]{:S(2)}, u32[]{:S(2)}) collective-permute-start(f32[4608]{0:T(1024)S(1)} %add.411), channel_id=1, source_target_pairs={{0,4},{2,6},{4,0},{6,2},{1,5},{3,7},{5,1},{7,3},{8,12},{10,14},{12... | collective-permute-start | bytes 55304 | tf_op jit(solution)/shard_map/ppermute | solution.py:278
  1003.1 88.4 %collective-permute-start.49 = (bf16[512,2560]{1,0:T(8,128)(2,1)}, bf16[512,2560]{1,0:T(8,128)(2,1)}, u32[]{:S(2)}, u32[]{:S(2)}) collective-permute-start(bf16[512,2560]{1,0:T(8,128)(2,1)} %add_convert_fusion.6), channel_id=1, source_target_pairs={{0,2},{6,4},{1,3},{7,5},{8,10},{14,12},{9,11},{15,13},{16,18},{22,... | collective-permute-start | bytes 7864328 | tf_op jit(solution)/shard_map/ppermute | solution.py:238
  1007.6 77.8 %collective-permute-start.19 = (bf16[512,1024]{1,0:T(8,128)(2,1)}, bf16[512,1024]{1,0:T(8,128)(2,1)S(1)}, u32[]{:S(2)}, u32[]{:S(2)}) collective-permute-start(bf16[512,1024]{1,0:T(8,128)(2,1)} %add_convert_fusion.29), channel_id=1, source_target_pairs={{0,2},{6,4},{1,3},{7,5},{8,10},{14,12},{9,11},{15,13},{16,18},{22,... | collective-permute-start | bytes 3145736 | tf_op jit(solution)/shard_map/ppermute | solution.py:238
  1014.6 124.0 %collective-permute-start.43 = (bf16[512,2560]{1,0:T(8,128)(2,1)S(1)}, bf16[512,2560]{1,0:T(8,128)(2,1)S(1)}, u32[]{:S(2)}, u32[]{:S(2)}) collective-permute-start(bf16[512,2560]{1,0:T(8,128)(2,1)S(1)} %copy-done.19), channel_id=1, source_target_pairs={{0,2},{6,4},{1,3},{7,5},{8,10},{14,12},{9,11},{15,13},{16,18},{22,... | collective-permute-start | bytes 7864328 | tf_op jit(solution)/shard_map/ppermute | solution.py:238
  1146.5 166.8 %collective-permute-start.57 = (bf16[512,2560]{1,0:T(8,128)(2,1)S(1)}, bf16[512,2560]{1,0:T(8,128)(2,1)S(1)}, u32[]{:S(2)}, u32[]{:S(2)}) collective-permute-start(bf16[512,2560]{1,0:T(8,128)(2,1)S(1)} %add_convert_fusion), channel_id=1, source_target_pairs={{2,0},{4,6},{3,1},{5,7},{10,8},{12,14},{11,9},{13,15},{18,16},{20,... | collective-permute-start | bytes 7864328 | tf_op jit(solution)/shard_map/ppermute | solution.py:242
  1166.6 202.9 %collective-permute-start.51 = (bf16[512,2560]{1,0:T(8,128)(2,1)S(1)}, bf16[512,2560]{1,0:T(8,128)(2,1)S(1)}, u32[]{:S(2)}, u32[]{:S(2)}) collective-permute-start(bf16[512,2560]{1,0:T(8,128)(2,1)S(1)} %add_convert_fusion.4), channel_id=1, source_target_pairs={{2,0},{4,6},{3,1},{5,7},{10,8},{12,14},{11,9},{13,15},{18,16},{20,... | collective-permute-start | bytes 7864328 | tf_op jit(solution)/shard_map/ppermute | solution.py:242
  1170.0 240.6 %collective-permute-start.45 = (bf16[512,2560]{1,0:T(8,128)(2,1)S(1)}, bf16[512,2560]{1,0:T(8,128)(2,1)S(1)}, u32[]{:S(2)}, u32[]{:S(2)}) collective-permute-start(bf16[512,2560]{1,0:T(8,128)(2,1)S(1)} %add_convert_fusion.8), channel_id=1, source_target_pairs={{2,0},{4,6},{3,1},{5,7},{10,8},{12,14},{11,9},{13,15},{18,16},{20,... | collective-permute-start | bytes 7864328 | tf_op jit(solution)/shard_map/ppermute | solution.py:242
  (97 other events, 3507.2 us)
Sparse Core Ops, SparseCore 0:
  9.6 37.1 all-gather.7
  48.4 34.4 all-gather.11
  84.4 34.4 all-gather.9
  120.4 34.4 all-gather.13
  156.3 70.1 all-gather.17
  227.9 70.1 all-gather.19
  299.7 70.1 all-gather.15

commit v2 on v1

--- a/solution.py
+++ b/solution.py
@@ -209,6 +209,314 @@
     return forward, backward
 
 
+MESH = pl.DeviceIdType.MESH
+
+
+class Spot:
+    def __init__(self, shards, ctx, tp):
+        self.shards, self.chips, self.n, self.tps = shards, shards // 2, ctx, tp
+        self.shard, self.me, self.half = (lax.axis_index(a) for a in ("shard", "ctx", "tp"))
+        self.chip, self.core = self.shard // 2, lax.rem(self.shard, 2)
+        self.mate = 2 * self.chip + 1 - self.core
+
+    def away(self, d):
+        return lax.rem(self.shard + 2 * d, self.shards)
+
+    def barrier(self):
+        peers = [{"shard": self.mate}] + [{"shard": self.away(d)} for d in range(1, self.chips)]
+        peers += [{"ctx": lax.rem(self.me + d, self.n)} for d in range(1, self.n)]
+        peers += [{"tp": 1 - self.half}]
+        semaphore = pltpu.get_barrier_semaphore()
+        for peer in peers:
+            pl.semaphore_signal(semaphore, inc=1, device_id=peer, device_id_type=MESH)
+        pl.semaphore_wait(semaphore, len(peers))
+
+
+def remote(src, dst, send, recv, peer):
+    return pltpu.make_async_remote_copy(
+        src_ref=src, dst_ref=dst, send_sem=send, recv_sem=recv, device_id=peer, device_id_type=MESH
+    )
+
+
+class Gather:
+    def __init__(self, spot, own, full, sems):
+        self.spot, self.own, self.full = spot, own, full
+        self.local, self.send, self.recv, self.on_send, self.on_recv = sems
+        spot_shard = spot.shard
+        self.keep = pltpu.make_async_copy(own, full.at[spot_shard], self.local)
+        self.far = [
+            remote(own, full.at[spot_shard], self.send.at[d], self.recv.at[d], {"shard": spot.away(d)})
+            for d in range(1, spot.chips)
+        ]
+        mate = {"shard": spot.mate}
+        self.near = [remote(own, full.at[spot_shard], self.on_send.at[0], self.on_recv.at[0], mate)]
+        for d in range(1, spot.chips):
+            at = full.at[lax.rem(spot.shard - 2 * d + spot.shards, spot.shards)]
+            self.near.append(remote(at, at, self.on_send.at[d], self.on_recv.at[d], mate))
+
+    def start_far(self):
+        for copy in self.far:
+            copy.start()
+
+    def start_near(self):
+        self.keep.start()
+        self.near[0].start()
+
+    def pass_on(self):
+        for d, copy in enumerate(self.far, 1):
+            copy.wait_recv()
+            self.near[d].start()
+
+    def wait_own(self):
+        self.keep.wait()
+        self.near[0].wait_recv()
+
+    def wait_near(self):
+        for copy in self.near[1:]:
+            copy.wait_recv()
+
+    def wait_sent(self):
+        for copy in self.far + self.near:
+            copy.wait_send()
+
+
+def forward_kernel(
+    dims, tokens, gains, table, wq, wk, wv, wo, wi0, wi1, wff,
+    normed, hidden, normed_two, attended, lse, pieces_out, full_q, full_k, full_v, full_o, full_0, full_1, full_2,
+    weights, acc, bias, staged, pieces, mixed, heads_in, branch, branch_in,
+    local_sem, far_send, far_recv, near_send, near_recv, head_send, head_recv, back_send, back_recv,
+    swap_send, swap_recv, out_sem,
+):
+    spot = Spot(*dims.mesh)
+    n, seqs, part, cols, head_dim = dims.n, dims.seqs, dims.part, dims.cols, dims.head_dim
+    me, shards = spot.me, spot.shards
+    shard_rows = weights.shape[2]
+    rows = seqs * part
+    lanes = 2 * head_dim
+    per = 2
+    spot.barrier()
+
+    def gather(i, own, full):
+        sems = [local_sem.at[i], far_send.at[i], far_recv.at[i], near_send.at[i], near_recv.at[i]]
+        return Gather(spot, own, full, sems)
+
+    loads = [gather(i, w, weights.at[i]) for i, w in enumerate((wq, wk, wv, wo))]
+    loads += [gather(4 + i, w, f) for i, (w, f) in enumerate(((wi0, full_0), (wi1, full_1), (wff, full_2)))]
+    for load in loads[:3]:
+        load.start_far()
+    for load in loads[:3]:
+        load.start_near()
+
+    @pl.loop(0, rows // 64)
+    def _(i):
+        at = pl.ds(pl.multiple_of(i * 64, 64), 64)
+        values = tokens[at, :].astype(F32)
+        normed[at, :] = (values * rms_scale(values) * gains[0:1, :]).astype(BF16)
+
+    for head in range(dims.own_heads):
+        bias_rows(table[head : head + 1, :], bias.at[head])
+
+    def term(i, shard):
+        at = pl.ds(pl.multiple_of(shard * shard_rows, 128), shard_rows)
+        return dot(normed[:, at], weights[i, shard])
+
+    moves = []
+    for i, load in enumerate(loads[:3]):
+        load.wait_own()
+        acc[...] = term(i, spot.shard)
+        acc[...] += term(i, spot.mate)
+        load.pass_on()
+        if i == 2:
+            for later in loads[3:]:
+                later.start_far()
+            for later in loads[3:]:
+                later.start_near()
+        for d in range(1, spot.chips):
+            acc[...] += term(i, lax.rem(spot.shard - 2 * d + shards, shards))
+        load.wait_near()
+        for d in range(1, spot.chips):
+            acc[...] += term(i, lax.rem(spot.mate - 2 * d + shards, shards))
+        for k in range(n):
+            for s in range(seqs):
+                staged[i, k, s] = acc[s * part : (s + 1) * part, k * cols : (k + 1) * cols].astype(BF16)
+        for d in range(1, n):
+            peer = lax.rem(me + d, n)
+            move = remote(
+                staged.at[i, peer], pieces.at[i, me], head_send.at[i, d], head_recv.at[i, d], {"ctx": peer}
+            )
+            move.start()
+            moves.append(move)
+        pieces[i, me] = staged[i, me]
+    outs = [
+        pltpu.make_async_copy(weights.at[i], full, out_sem.at[i])
+        for i, full in enumerate((full_q, full_k, full_v, full_o))
+    ]
+    for copy in outs[:3]:
+        copy.start()
+    for move in moves:
+        move.wait_recv()
+    loads[3].wait_own()
+    loads[3].pass_on()
+    outs.append(pltpu.make_async_copy(pieces, pieces_out, out_sem.at[4]))
+    outs[4].start()
+
+    def back(s, at, to):
+        return remote(mixed.at[s, at], heads_in.at[me, s], back_send.at[s, at], back_recv.at[s, me], {"ctx": to})
+
+    @pl.loop(0, seqs * n)
+    def _(step):
+        s, a = step // n, lax.rem(step, n)
+        lane = lax.broadcasted_iota(jnp.int32, (part, lanes), 1)
+        log_total = jnp.zeros((part, lanes), F32)
+        for group in range(cols // lanes):
+            span = slice(group * lanes, (group + 1) * lanes)
+            result = jnp.zeros((part, lanes), F32)
+            for j in range(per):
+                head = group * per + j
+                mask = (lane >= j * head_dim) & (lane < (j + 1) * head_dim)
+                query = jnp.where(mask, pieces[0, a, s, :, span], 0)
+                scores = jnp.concatenate(
+                    [
+                        contract_cols(query, pieces[1, b, s, :, span])
+                        + bias[head, :, pl.ds(pl.multiple_of((n + b - a) * part, part), part)]
+                        for b in range(n)
+                    ],
+                    axis=1,
+                )
+                peak = jnp.max(scores, axis=1, keepdims=True)
+                expo = jnp.exp(scores - peak)
+                total = jnp.sum(expo, axis=1, keepdims=True)
+                probs = (expo * (1.0 / total)).astype(BF16)
+                summed = sum(
+                    dot(probs[:, b * part : (b + 1) * part], pieces[2, b, s, :, span]) for b in range(n)
+                )
+                result = jnp.where(mask, summed, result)
+                log_total = jnp.where(lane == head, peak + jnp.log(total), log_total)
+            mixed[s, a, :, span] = result.astype(BF16)
+        lse[s, a] = log_total
+
+        @pl.when(a != me)
+        def _():
+            back(s, a, a).start()
+
+        @pl.when(a == me)
+        def _():
+            heads_in[a, s] = mixed[s, a]
+
+    loads[3].wait_near()
+    outs[3].start()
+    swaps = []
+    for s in range(seqs):
+        at = slice(s * part, (s + 1) * part)
+        for d in range(1, n):
+            peer = lax.rem(me + d, n)
+            remote(
+                mixed.at[s, 0], heads_in.at[peer, s], back_send.at[s, peer], back_recv.at[s, peer], {"ctx": peer}
+            ).wait_recv()
+        for k in range(n):
+            attended[at, k * cols : (k + 1) * cols] = heads_in[k, s]
+        for j in range(shards):
+            branch[s, :, j * shard_rows : (j + 1) * shard_rows] = contract_cols(
+                attended[at, :], weights[3, j]
+            ).astype(BF16)
+        swap = remote(branch.at[s], branch_in.at[s], swap_send.at[s], swap_recv.at[s], {"tp": 1 - spot.half})
+        swap.start()
+        swaps.append(swap)
+    loads[4].wait_own()
+    loads[4].pass_on()
+    for s in range(seqs):
+        swaps[s].wait_recv()
+
+        @pl.loop(0, part // 64)
+        def _(i):
+            here = pl.ds(pl.multiple_of(i * 64, 64), 64)
+            at = pl.ds(pl.multiple_of(s * part + i * 64, 64), 64)
+            values = tokens[at, :].astype(F32) + (
+                branch[s, here, :].astype(F32) + branch_in[s, here, :].astype(F32)
+            )
+            hidden[at, :] = values
+            normed_two[at, :] = (values * rms_scale(values) * gains[1:2, :]).astype(BF16)
+
+    for load in loads[5:]:
+        load.wait_own()
+        load.pass_on()
+    for load in loads[4:]:
+        load.wait_near()
+    for load in loads:
+        load.wait_sent()
+    for move in moves + swaps:
+        move.wait_send()
+    for s in range(seqs):
+        for d in range(1, n):
+            peer = lax.rem(me + d, n)
+            back(s, peer, peer).wait_send()
+    for copy in outs:
+        copy.wait()
+
+
+class Dims:
+    def __init__(self, links, seqs, part, width, inner_width, units, heads):
+        self.mesh = (links.shard, links.ctx, links.tp)
+        self.n, self.seqs, self.part, self.width = links.ctx, seqs, part, width
+        self.inner_width, self.units = inner_width, units
+        self.head_dim = inner_width // heads
+        self.cols, self.own_heads = inner_width // links.ctx, heads // links.ctx
+        self.shards, self.shard_rows = links.shard, width // links.shard
+
+
+def forward_call(dims):
+    rows, width, n, part, seqs = dims.seqs * dims.part, dims.width, dims.n, dims.part, dims.seqs
+    shards, shard_rows, inner, units = dims.shards, dims.shard_rows, dims.inner_width, dims.units
+    lanes, span = 2 * dims.head_dim, 2 * n * part
+    vmem, anywhere = pl.BlockSpec(memory_space=pltpu.VMEM), pl.BlockSpec(memory_space=pl.ANY)
+    shape = jax.ShapeDtypeStruct
+    dma = pltpu.SemaphoreType.DMA
+    chips = shards // 2
+    block = (seqs, part, dims.cols)
+    return pl.pallas_call(
+        functools.partial(forward_kernel, dims),
+        in_specs=[vmem] * 3 + [anywhere] * 7,
+        out_specs=[vmem] * 5 + [anywhere] * 8,
+        out_shape=[
+            shape((rows, width), BF16),
+            shape((rows, width), F32),
+            shape((rows, width), BF16),
+            shape((rows, inner), BF16),
+            shape((seqs, n, part, lanes), F32),
+            shape((3, n) + block, BF16),
+        ]
+        + [shape((shards, shard_rows, inner), BF16)] * 4
+        + [shape((shards, shard_rows, units), BF16)] * 3,
+        scratch_shapes=[
+            pltpu.VMEM((4, shards, shard_rows, inner), BF16),
+            pltpu.VMEM((rows, inner), F32),
+            pltpu.VMEM((dims.own_heads, part, span), F32),
+            pltpu.VMEM((3, n) + block, BF16),
+            pltpu.VMEM((3, n) + block, BF16),
+            pltpu.VMEM((seqs, n, part, dims.cols), BF16),
+            pltpu.VMEM((n,) + block, BF16),
+            pltpu.VMEM((seqs, part, width), BF16),
+            pltpu.VMEM((seqs, part, width), BF16),
+            dma((7,)),
+            dma((7, chips)),
+            dma((7, chips)),
+            dma((7, chips)),
+            dma((7, chips)),
+            dma((3, n)),
+            dma((3, n)),
+            dma((seqs, n)),
+            dma((seqs, n)),
+            dma((seqs,)),
+            dma((seqs,)),
+            dma((5,)),
+        ],
+        compiler_params=pltpu.CompilerParams(
+            vmem_limit_bytes=60 * 2**20, collective_id=0, has_side_effects=True
+        ),
+        name="forward",
+    )
+
+
 def ring(n, d):
     return [(i, (i + d) % n) for i in range(n)]
 
@@ -333,21 +641,22 @@
     groups = cols // (2 * head_dim)
     offset_bias = offset_bias.reshape(groups, 2, 2 * reach)
     where_am_i = me.astype(jnp.int32).reshape(1)
-    attend, attend_back = attention_calls(n, seqs, part, cols, head_dim)
-
-    wq, wk, wv = gathered(query_weight), gathered(key_weight), gathered(value_weight)
+    unused_attend, attend_back = attention_calls(n, seqs, part, cols, head_dim)
+
+    dims = Dims(links, seqs, part, width, inner_width, gate_weight.shape[1], heads)
+    normed, hidden, normed_two, attended, lse, pieces, *full = forward_call(dims)(
+        tokens.reshape(rows, width),
+        jnp.stack([gain_one, gain_two]),
+        offset_bias.reshape(own_heads, 2 * reach),
+        query_weight, key_weight, value_weight, output_weight, gate_weight, up_weight, down_weight,
+    )
+    wq, wk, wv, wo, wi0, wi1, wff = (w.reshape(width, w.shape[2]) for w in full)
     inputs = tokens.reshape(rows, width).astype(F32)
-    scale_one = rms_scale(inputs)
-    normed = (inputs * scale_one * gain_one).astype(BF16)
-    projected = [dot(normed, w).astype(BF16) for w in (wq, wk, wv)]
+    scale_one, scale_two = rms_scale(inputs), rms_scale(hidden)
 
     def heads_of(values, d):
         start = at_ctx(d) * cols
         return [lax.dynamic_slice_in_dim(v, start, cols, 1).reshape(seqs, part, cols) for v in values]
-
-    pieces = [jnp.stack(heads_of(projected, d)) for d in range(n)]
-    pieces = [pieces[0]] + [lax.ppermute(pieces[d], "ctx", ring(n, d)) for d in range(1, n)]
-    *mixed, lse = attend(where_am_i, offset_bias, *pieces)
 
     def heads_back(blocks):
         blocks = [blocks[0]] + [lax.ppermute(blocks[d], "ctx", ring(n, n - d)) for d in range(1, n)]
@@ -355,13 +664,10 @@
         twice = jnp.concatenate([around, around], axis=-1)
         return lax.dynamic_slice_in_dim(twice, (n - me) * cols, n * cols, around.ndim - 1)
 
-    attended = heads_back(mixed).reshape(rows, inner_width)
-    wo = gathered(output_weight)
-    branch = links.tp_sum(contract_cols(attended, wo).astype(BF16))
-    hidden = inputs + branch
-    wi0, wi1, wff = gathered(gate_weight), gathered(up_weight), gathered(down_weight)
-    scale_two = rms_scale(hidden)
-    normed_two = (hidden * scale_two * gain_two).astype(BF16)
+    pieces = [lax.dynamic_index_in_dim(pieces, at_ctx(-d), 1, keepdims=False) for d in range(n)]
+    lse = jnp.stack([lax.dynamic_index_in_dim(lse, at_ctx(-d), 1, keepdims=False) for d in range(n)], axis=1)
+    lse = jnp.stack([lse[..., 2 * g : 2 * g + 2] for g in range(groups)])
+    lse = jnp.pad(lse, ((0, 0),) * 4 + ((0, 2 * head_dim - 2),))
     gate = dot(normed_two, wi0)
     up = dot(normed_two, wi1)
     inner = geglu(gate, up).astype(BF16)

time: 1430 us -> 1410 us (0.986)
  Pallas kernels: 68 us -> 367 us
  waiting for transfers between devices: 998 us -> 709 us
    pallas_call x1, Pallas kernels: 26.3 us -> 325 us  [per_device(): forward_call(dims)]
    all_gather x7 -> x0, waiting for transfers between devices: 131 us -> none  [gathered(): return lax.all_gather(weight, 'shard', axis=0, tiled=True)]
    ppermute x4 -> x3, waiting for transfers between devices: 95.8 us -> 31.5 us  [tp_sum(): other = lax.ppermute(value, 'tp', ring(2, 1))]
    ppermute x3 -> x0, waiting for transfers between devices: 59.9 us -> none  [per_device(): lax.ppermute(pieces[d], 'ctx', ring(n, d))]
    ppermute x7, waiting for transfers between devices: 165 us -> 198 us  [to_chip(): lax.ppermute(value, 'shard', [(i, (i + 2 * d) % n) for i in range(n)])]
    ppermute x7, waiting for transfers between devices: 106 us -> 84.2 us  [ctx_sum(): inward = lax.ppermute(low, 'ctx', [(0, 1), (3, 2)])]
    ppermute x6 -> x3, waiting for transfers between devices: 70.5 us -> 49.9 us  [heads_back(): lax.ppermute(blocks[d], 'ctx', ring(n, n - d))]
    ppermute x7, waiting for transfers between devices: 249 us -> 231 us  [ctx_sum(): outward = lax.ppermute(whole, 'ctx', [(1, 0), (2, 3)])]
  transfers between devices with their start and end apart: 69 -> 55, of which waited for: 28 -> 20; matrix products, arithmetic and copies ran while one was open for 16% -> 13% of each run, Pallas kernels for 5% -> 3%
where the time goes in v2:
time: 1410 us; the launch traced here: 1400 us
  waiting for transfers between devices  709 us (50%)
  Pallas kernels  367 us (26%)
  matrix products  160 us (11%)
  other arithmetic  76.6 us (5%)
  starting transfers between devices  69.2 us (5%)
  local copies, waits for them, and re-layouts  18.5 us (1%)
    pallas_call x1, Pallas kernels, per_device(): forward_call(dims)  325 us
    ppermute x7, waiting for transfers between devices, ctx_sum(): outward = lax.ppermute(whole, 'ctx', [(1, 0), (2, 3)])  231 us
    ppermute x7, waiting for transfers between devices, to_chip(): lax.ppermute(value, 'shard', [(i, (i + 2 * d) % n) for i in range(n)])  198 us
    ppermute x4, waiting for transfers between devices, small_sum(): value = value + lax.ppermute(value, axis, [(i, i ^ step) for i in range(n)])  100 us
    ppermute x7, waiting for transfers between devices, ctx_sum(): inward = lax.ppermute(low, 'ctx', [(0, 1), (3, 2)])  84.2 us
    dot_general x28, matrix products, contract_rows(): lax.dot_general(left, right, (((0,), (0,)), ((), ())), preferred_element_...  79.1 us
    ppermute x3, waiting for transfers between devices, heads_back(): lax.ppermute(blocks[d], 'ctx', ring(n, n - d))  49.9 us
    dot_general x6, matrix products, contract_cols(): lax.dot_general(left, right, (((1,), (1,)), ((), ())), preferred_element_...  45.6 us
  transfers between devices with their start and end apart: 55, of which 20 were waited for; matrix products, arithmetic and copies ran while one was open for 13% of the time, Pallas kernels for 3%

profile of v2, /device:TPU:0, one launch (start us, length us, event | category | flops | bytes accessed | tf_op | source)
XLA Modules:
  0.0 1403.3 jit_solution(7370200619512113487)
XLA Ops:
  8.1 325.3 %forward.1 = (bf16[512,2048]{1,0:T(8,128)(2,1)}, f32[512,2048]{1,0:T(8,128)}, bf16[512,2048]{1,0:T(8,128)(2,1)}, bf16[512,1024]{1,0:T(8,128)(2,1)}, f32[2,4,256,...) custom-call(bf16[512,2048]{1,0:T(8,128)(2,1)} %bitcast.101, ...), custom_call_target="tpu_custom_call" | custom-call | tf_op jit(solution)/shard_map/forward/pallas_call | solution.py:647
  333.4 12.2 fusion.97
  353.0 13.0 fusion.7
  366.0 12.4 fusion.99
  378.4 11.6 add_convert_fusion.13
  451.7 31.5 %collective-permute-done = bf16[512,2048]{1,0:T(8,128)(2,1)} collective-permute-done((bf16[512,2048]{1,0:T(8,128)(2,1)}, bf16[512,2048]{1,0:T(8,128)(2,1)}, u32[]{:S(2)}, u32[]{:S(2)}) %collective-permute-start) | collective-permute-done | bytes 2097184 | tf_op jit(solution)/shard_map/ppermute | solution.py:539
  518.8 42.1 %attend_back.1 = (bf16[3,2,256,256]{3,2,1,0:T(8,128)(2,1)S(1)}, bf16[3,2,256,256]{3,2,1,0:T(8,128)(2,1)}, bf16[3,2,256,256]{3,2,1,0:T(8,128)(2,1)S(1)}, bf16[3,2...) custom-call(s32[1]{0:T(128)} %bitcast.12.me_ref, f32[2,2,2048]{2,1,0:T(2,128)S(1)} %reshape.160.table_ref, ...), custom_call_target="tpu_custom_call" | custom-call | flops 21474836480 | bytes 16777216 | tf_op jit(solution)/shard_map/attend_back/pallas_call | solution.py:698
  586.5 49.9 %collective-permute-done.6 = bf16[3,2,256,256]{3,2,1,0:T(8,128)(2,1)S(1)} collective-permute-done((bf16[3,2,256,256]{3,2,1,0:T(8,128)(2,1)}, bf16[3,2,256,256]{3,2,1,0:T(8,128)(2,1)S(1)}, u32[]{:S(2)}, u32[]{:S(2)}) %collective-permute-start.6) | collective-permute-done | bytes 786464 | tf_op jit(solution)/shard_map/ppermute | solution.py:662
  672.4 70.9 %collective-permute-done.29 = bf16[512,1024]{1,0:T(8,128)(2,1)S(1)} collective-permute-done((bf16[512,1024]{1,0:T(8,128)(2,1)S(1)}, bf16[512,1024]{1,0:T(8,128)(2,1)S(1)}, u32[]{:S(2)}, u32[]{:S(2)}) %collective-permute-start.29) | collective-permute-done | bytes 1048608 | tf_op jit(solution)/shard_map/ppermute | solution.py:534
  758.9 44.6 %collective-permute-done.41 = bf16[512,2560]{1,0:T(8,128)(2,1)} collective-permute-done((bf16[512,2560]{1,0:T(8,128)(2,1)}, bf16[512,2560]{1,0:T(8,128)(2,1)}, u32[]{:S(2)}, u32[]{:S(2)}) %collective-permute-start.41) | collective-permute-done | bytes 2621472 | tf_op jit(solution)/shard_map/ppermute | solution.py:534
  809.4 50.3 %collective-permute-done.47 = bf16[512,2560]{1,0:T(8,128)(2,1)} collective-permute-done((bf16[512,2560]{1,0:T(8,128)(2,1)}, bf16[512,2560]{1,0:T(8,128)(2,1)}, u32[]{:S(2)}, u32[]{:S(2)}) %collective-permute-start.47) | collective-permute-done | bytes 2621472 | tf_op jit(solution)/shard_map/ppermute | solution.py:534
  867.0 15.0 %collective-permute-done.11 = bf16[512,1024]{1,0:T(8,128)(2,1)S(1)} collective-permute-done((bf16[512,1024]{1,0:T(8,128)(2,1)S(1)}, bf16[512,1024]{1,0:T(8,128)(2,1)S(1)}, u32[]{:S(2)}, u32[]{:S(2)}) %collective-permute-start.11) | collective-permute-done | bytes 1048608 | tf_op jit(solution)/shard_map/ppermute | solution.py:534
  887.6 16.9 %collective-permute-done.17 = bf16[512,1024]{1,0:T(8,128)(2,1)S(1)} collective-permute-done((bf16[512,1024]{1,0:T(8,128)(2,1)}, bf16[512,1024]{1,0:T(8,128)(2,1)S(1)}, u32[]{:S(2)}, u32[]{:S(2)}) %collective-permute-start.17) | collective-permute-done | bytes 1048608 | tf_op jit(solution)/shard_map/ppermute | solution.py:534
  913.4 12.1 collective-permute-done.52
  935.7 72.2 %collective-permute-done.53 = f32[4608]{0:T(1024)S(1)} collective-permute-done((f32[4608]{0:T(1024)S(1)}, f32[4608]{0:T(1024)S(1)}, u32[]{:S(2)}, u32[]{:S(2)}) %collective-permute-start.53) | collective-permute-done | bytes 18464 | tf_op jit(solution)/shard_map/ppermute | solution.py:586
  1015.1 15.7 %collective-permute-done.54 = f32[4608]{0:T(1024)S(1)} collective-permute-done((f32[4608]{0:T(1024)S(1)}, f32[4608]{0:T(1024)S(1)}, u32[]{:S(2)}, u32[]{:S(2)}) %collective-permute-start.54) | collective-permute-done | bytes 18464 | tf_op jit(solution)/shard_map/ppermute | solution.py:586
  1059.9 37.9 %collective-permute-done.42 = bf16[512,2560]{1,0:T(8,128)(2,1)S(1)} collective-permute-done((bf16[512,2560]{1,0:T(8,128)(2,1)}, bf16[512,2560]{1,0:T(8,128)(2,1)S(1)}, u32[]{:S(2)}, u32[]{:S(2)}) %collective-permute-start.42) | collective-permute-done | bytes 2621472 | tf_op jit(solution)/shard_map/ppermute | solution.py:546
  1100.6 46.3 %collective-permute-done.48 = bf16[512,2560]{1,0:T(8,128)(2,1)S(1)} collective-permute-done((bf16[512,2560]{1,0:T(8,128)(2,1)S(1)}, bf16[512,2560]{1,0:T(8,128)(2,1)S(1)}, u32[]{:S(2)}, u32[]{:S(2)}) %collective-permute-start.48) | collective-permute-done | bytes 2621472 | tf_op jit(solution)/shard_map/ppermute | solution.py:546
  1156.9 18.0 %collective-permute-done.14 = bf16[512,1024]{1,0:T(8,128)(2,1)S(1)} collective-permute-done((bf16[512,1024]{1,0:T(8,128)(2,1)S(1)}, bf16[512,1024]{1,0:T(8,128)(2,1)S(1)}, u32[]{:S(2)}, u32[]{:S(2)}) %collective-permute-start.14) | collective-permute-done | bytes 1048608 | tf_op jit(solution)/shard_map/ppermute | solution.py:550
  1179.5 17.8 %collective-permute-done.20 = bf16[512,1024]{1,0:T(8,128)(2,1)S(1)} collective-permute-done((bf16[512,1024]{1,0:T(8,128)(2,1)S(1)}, bf16[512,1024]{1,0:T(8,128)(2,1)S(1)}, u32[]{:S(2)}, u32[]{:S(2)}) %collective-permute-start.20) | collective-permute-done | bytes 1048608 | tf_op jit(solution)/shard_map/ppermute | solution.py:550
  1198.8 13.2 collective-permute-done.26
  1213.4 89.0 %collective-permute-done.38 = bf16[512,2560]{1,0:T(8,128)(2,1)S(1)} collective-permute-done((bf16[512,2560]{1,0:T(8,128)(2,1)S(1)}, bf16[512,2560]{1,0:T(8,128)(2,1)S(1)}, u32[]{:S(2)}, u32[]{:S(2)}) %collective-permute-start.38) | collective-permute-done | bytes 2621472 | tf_op jit(solution)/shard_map/ppermute | solution.py:550
  1305.1 53.5 %collective-permute-done.44 = bf16[512,2560]{1,0:T(8,128)(2,1)S(1)} collective-permute-done((bf16[512,2560]{1,0:T(8,128)(2,1)S(1)}, bf16[512,2560]{1,0:T(8,128)(2,1)S(1)}, u32[]{:S(2)}, u32[]{:S(2)}) %collective-permute-start.44) | collective-permute-done | bytes 2621472 | tf_op jit(solution)/shard_map/ppermute | solution.py:550
  1361.2 39.2 %collective-permute-done.50 = bf16[512,2560]{1,0:T(8,128)(2,1)S(1)} collective-permute-done((bf16[512,2560]{1,0:T(8,128)(2,1)S(1)}, bf16[512,2560]{1,0:T(8,128)(2,1)S(1)}, u32[]{:S(2)}, u32[]{:S(2)}) %collective-permute-start.50) | collective-permute-done | bytes 2621472 | tf_op jit(solution)/shard_map/ppermute | solution.py:550
  (319 shorter events, 291.0 us)
Async XLA Ops:
  398.5 84.7 %collective-permute-start = (bf16[512,2048]{1,0:T(8,128)(2,1)}, bf16[512,2048]{1,0:T(8,128)(2,1)}, u32[]{:S(2)}, u32[]{:S(2)}) collective-permute-start(bf16[512,2048]{1,0:T(8,128)(2,1)} %convolution_convert_fusion.6), channel_id=1, source_target_pairs={{0,1},{1,0},{2,3},{3,2},{4,5},{5,4},{6,7},{7,6},{8,9},{9,8},{10,11... | collective-permute-start | bytes 6291464 | tf_op jit(solution)/shard_map/ppermute | solution.py:539
  403.3 164.4 %collective-permute-start.34 = (bf16[512,2560]{1,0:T(8,128)(2,1)}, bf16[512,2560]{1,0:T(8,128)(2,1)}, u32[]{:S(2)}, u32[]{:S(2)}) collective-permute-start(bf16[512,2560]{1,0:T(8,128)(2,1)} %convolution_convert_fusion.4), channel_id=1, source_target_pairs={{0,8},{8,0},{16,24},{24,16},{1,9},{9,1},{17,25},{25,17},{2,10},{10... | collective-permute-start | bytes 7864328 | tf_op jit(solution)/shard_map/ppermute | solution.py:530
  408.4 340.4 %collective-permute-start.33 = (bf16[512,2560]{1,0:T(8,128)(2,1)}, bf16[512,2560]{1,0:T(8,128)(2,1)}, u32[]{:S(2)}, u32[]{:S(2)}) collective-permute-start(bf16[512,2560]{1,0:T(8,128)(2,1)} %convolution_convert_fusion.5), channel_id=1, source_target_pairs={{0,8},{8,0},{16,24},{24,16},{1,9},{9,1},{17,25},{25,17},{2,10},{10... | collective-permute-start | bytes 7864328 | tf_op jit(solution)/shard_map/ppermute | solution.py:530
  580.8 81.0 %collective-permute-start.28 = (bf16[512,1024]{1,0:T(8,128)(2,1)S(1)}, bf16[512,1024]{1,0:T(8,128)(2,1)S(1)}, u32[]{:S(2)}, u32[]{:S(2)}) collective-permute-start(bf16[512,1024]{1,0:T(8,128)(2,1)S(1)} %copy-done.41), channel_id=1, source_target_pairs={{0,8},{8,0},{16,24},{24,16},{1,9},{9,1},{17,25},{25,17},{2,10},{10... | collective-permute-start | bytes 3145736 | tf_op jit(solution)/shard_map/ppermute | solution.py:530
  585.9 78.2 %collective-permute-start.27 = (bf16[512,1024]{1,0:T(8,128)(2,1)S(1)}, bf16[512,1024]{1,0:T(8,128)(2,1)S(1)}, u32[]{:S(2)}, u32[]{:S(2)}) collective-permute-start(bf16[512,1024]{1,0:T(8,128)(2,1)S(1)} %copy-done.42), channel_id=1, source_target_pairs={{0,8},{8,0},{16,24},{24,16},{1,9},{9,1},{17,25},{25,17},{2,10},{10... | collective-permute-start | bytes 3145736 | tf_op jit(solution)/shard_map/ppermute | solution.py:530
  661.9 90.4 %collective-permute-start.35 = (bf16[512,2560]{1,0:T(8,128)(2,1)}, bf16[512,2560]{1,0:T(8,128)(2,1)S(1)}, u32[]{:S(2)}, u32[]{:S(2)}) collective-permute-start(bf16[512,2560]{1,0:T(8,128)(2,1)} %add_convert_fusion.11), channel_id=1, source_target_pairs={{0,16},{8,24},{16,0},{24,8},{1,17},{9,25},{17,1},{25,9},{2,18},{10... | collective-permute-start | bytes 7864328 | tf_op jit(solution)/shard_map/ppermute | solution.py:534
  664.2 84.7 %collective-permute-start.8 = (bf16[512,2048]{1,0:T(8,128)(2,1)S(1)}, bf16[512,2048]{1,0:T(8,128)(2,1)S(1)}, u32[]{:S(2)}, u32[]{:S(2)}) collective-permute-start(bf16[512,2048]{1,0:T(8,128)(2,1)S(1)} %add_convert_fusion.12), channel_id=1, source_target_pairs={{0,1},{1,0},{2,3},{3,2},{4,5},{5,4},{6,7},{7,6},{8,9},{9,8},{10,11... | collective-permute-start | bytes 6291464 | tf_op jit(solution)/shard_map/ppermute | solution.py:539
  665.7 77.6 %collective-permute-start.29 = (bf16[512,1024]{1,0:T(8,128)(2,1)S(1)}, bf16[512,1024]{1,0:T(8,128)(2,1)S(1)}, u32[]{:S(2)}, u32[]{:S(2)}) collective-permute-start(bf16[512,1024]{1,0:T(8,128)(2,1)S(1)} %add_convert_fusion.18), channel_id=1, source_target_pairs={{0,16},{8,24},{16,0},{24,8},{1,17},{9,25},{17,1},{25,9},{2,18},{10... | collective-permute-start | bytes 3145736 | tf_op jit(solution)/shard_map/ppermute | solution.py:534
  672.3 86.4 %collective-permute-start.39 = (bf16[512,2560]{1,0:T(8,128)(2,1)}, bf16[512,2560]{1,0:T(8,128)(2,1)}, u32[]{:S(2)}, u32[]{:S(2)}) collective-permute-start(bf16[512,2560]{1,0:T(8,128)(2,1)} %convolution_convert_fusion.3), channel_id=1, source_target_pairs={{0,8},{8,0},{16,24},{24,16},{1,9},{9,1},{17,25},{25,17},{2,10},{10... | collective-permute-start | bytes 7864328 | tf_op jit(solution)/shard_map/ppermute | solution.py:530
  748.9 110.8 %collective-permute-start.47 = (bf16[512,2560]{1,0:T(8,128)(2,1)}, bf16[512,2560]{1,0:T(8,128)(2,1)}, u32[]{:S(2)}, u32[]{:S(2)}) collective-permute-start(bf16[512,2560]{1,0:T(8,128)(2,1)} %add_convert_fusion.3), channel_id=1, source_target_pairs={{0,16},{8,24},{16,0},{24,8},{1,17},{9,25},{17,1},{25,9},{2,18},{10... | collective-permute-start | bytes 7864328 | tf_op jit(solution)/shard_map/ppermute | solution.py:534
  753.8 111.6 %collective-permute-start.9 = (bf16[512,1024]{1,0:T(8,128)(2,1)}, bf16[512,1024]{1,0:T(8,128)(2,1)}, u32[]{:S(2)}, u32[]{:S(2)}) collective-permute-start(bf16[512,1024]{1,0:T(8,128)(2,1)} %convolution_convert_fusion.14), channel_id=1, source_target_pairs={{0,8},{8,0},{16,24},{24,16},{1,9},{9,1},{17,25},{25,17},{2,10},{10... | collective-permute-start | bytes 3145736 | tf_op jit(solution)/shard_map/ppermute | solution.py:530
  758.7 128.9 %collective-permute-start.15 = (bf16[512,1024]{1,0:T(8,128)(2,1)}, bf16[512,1024]{1,0:T(8,128)(2,1)}, u32[]{:S(2)}, u32[]{:S(2)}) collective-permute-start(bf16[512,1024]{1,0:T(8,128)(2,1)} %convolution_convert_fusion.12), channel_id=1, source_target_pairs={{0,8},{8,0},{16,24},{24,16},{1,9},{9,1},{17,25},{25,17},{2,10},{10... | collective-permute-start | bytes 3145736 | tf_op jit(solution)/shard_map/ppermute | solution.py:530
  803.5 107.6 %collective-permute-start.21 = (bf16[512,1024]{1,0:T(8,128)(2,1)}, bf16[512,1024]{1,0:T(8,128)(2,1)}, u32[]{:S(2)}, u32[]{:S(2)}) collective-permute-start(bf16[512,1024]{1,0:T(8,128)(2,1)} %convolution_convert_fusion.10), channel_id=1, source_target_pairs={{0,8},{8,0},{16,24},{24,16},{1,9},{9,1},{17,25},{25,17},{2,10},{10... | collective-permute-start | bytes 3145736 | tf_op jit(solution)/shard_map/ppermute | solution.py:530
  882.0 131.3 %collective-permute-start.30 = (bf16[512,1024]{1,0:T(8,128)(2,1)S(1)}, bf16[512,1024]{1,0:T(8,128)(2,1)S(1)}, u32[]{:S(2)}, u32[]{:S(2)}) collective-permute-start(bf16[512,1024]{1,0:T(8,128)(2,1)S(1)} %copy-done.25), channel_id=1, source_target_pairs={{0,2},{6,4},{1,3},{7,5},{8,10},{14,12},{9,11},{15,13},{16,18},{22,... | collective-permute-start | bytes 3145736 | tf_op jit(solution)/shard_map/ppermute | solution.py:546
  907.8 125.5 %collective-permute-start.12 = (bf16[512,1024]{1,0:T(8,128)(2,1)}, bf16[512,1024]{1,0:T(8,128)(2,1)}, u32[]{:S(2)}, u32[]{:S(2)}) collective-permute-start(bf16[512,1024]{1,0:T(8,128)(2,1)} %add_convert_fusion.29), channel_id=1, source_target_pairs={{0,2},{6,4},{1,3},{7,5},{8,10},{14,12},{9,11},{15,13},{16,18},{22,... | collective-permute-start | bytes 3145736 | tf_op jit(solution)/shard_map/ppermute | solution.py:546
  911.0 131.3 %collective-permute-start.18 = (bf16[512,1024]{1,0:T(8,128)(2,1)}, bf16[512,1024]{1,0:T(8,128)(2,1)}, u32[]{:S(2)}, u32[]{:S(2)}) collective-permute-start(bf16[512,1024]{1,0:T(8,128)(2,1)} %add_convert_fusion.25), channel_id=1, source_target_pairs={{0,2},{6,4},{1,3},{7,5},{8,10},{14,12},{9,11},{15,13},{16,18},{22,... | collective-permute-start | bytes 3145736 | tf_op jit(solution)/shard_map/ppermute | solution.py:546
  925.5 130.4 %collective-permute-start.36 = (bf16[512,2560]{1,0:T(8,128)(2,1)S(1)}, bf16[512,2560]{1,0:T(8,128)(2,1)}, u32[]{:S(2)}, u32[]{:S(2)}) collective-permute-start(bf16[512,2560]{1,0:T(8,128)(2,1)S(1)} %add_convert_fusion.10), channel_id=1, source_target_pairs={{0,2},{6,4},{1,3},{7,5},{8,10},{14,12},{9,11},{15,13},{16,18},{22,... | collective-permute-start | bytes 7864328 | tf_op jit(solution)/shard_map/ppermute | solution.py:546
  932.9 75.0 %collective-permute-start.53 = (f32[4608]{0:T(1024)S(1)}, f32[4608]{0:T(1024)S(1)}, u32[]{:S(2)}, u32[]{:S(2)}) collective-permute-start(f32[4608]{0:T(1024)S(1)} %add.435), channel_id=1, source_target_pairs={{0,2},{2,0},{4,6},{6,4},{1,3},{3,1},{5,7},{7,5},{8,10},{10,8},{12,... | collective-permute-start | bytes 55304 | tf_op jit(solution)/shard_map/ppermute | solution.py:586
  1045.6 101.2 %collective-permute-start.48 = (bf16[512,2560]{1,0:T(8,128)(2,1)S(1)}, bf16[512,2560]{1,0:T(8,128)(2,1)S(1)}, u32[]{:S(2)}, u32[]{:S(2)}) collective-permute-start(bf16[512,2560]{1,0:T(8,128)(2,1)S(1)} %copy-done.18), channel_id=1, source_target_pairs={{0,2},{6,4},{1,3},{7,5},{8,10},{14,12},{9,11},{15,13},{16,18},{22,... | collective-permute-start | bytes 7864328 | tf_op jit(solution)/shard_map/ppermute | solution.py:546
  1054.8 94.0 %collective-permute-start.25 = (bf16[512,1024]{1,0:T(8,128)(2,1)S(1)}, bf16[512,1024]{1,0:T(8,128)(2,1)S(1)}, u32[]{:S(2)}, u32[]{:S(2)}) collective-permute-start(bf16[512,1024]{1,0:T(8,128)(2,1)S(1)} %add_convert_fusion.20), channel_id=1, source_target_pairs={{2,4},{4,2},{3,5},{5,3},{10,12},{12,10},{11,13},{13,11},{18,20},{2... | collective-permute-start | bytes 3145736 | tf_op jit(solution)/shard_map/ppermute | solution.py:548
  1055.9 94.1 %collective-permute-start.32 = (bf16[512,1024]{1,0:T(8,128)(2,1)S(1)}, bf16[512,1024]{1,0:T(8,128)(2,1)S(1)}, u32[]{:S(2)}, u32[]{:S(2)}) collective-permute-start(bf16[512,1024]{1,0:T(8,128)(2,1)S(1)} %add_convert_fusion.15), channel_id=1, source_target_pairs={{2,0},{4,6},{3,1},{5,7},{10,8},{12,14},{11,9},{13,15},{18,16},{20,... | collective-permute-start | bytes 3145736 | tf_op jit(solution)/shard_map/ppermute | solution.py:550
  1154.9 147.4 %collective-permute-start.38 = (bf16[512,2560]{1,0:T(8,128)(2,1)S(1)}, bf16[512,2560]{1,0:T(8,128)(2,1)S(1)}, u32[]{:S(2)}, u32[]{:S(2)}) collective-permute-start(bf16[512,2560]{1,0:T(8,128)(2,1)S(1)} %add_convert_fusion.8), channel_id=1, source_target_pairs={{2,0},{4,6},{3,1},{5,7},{10,8},{12,14},{11,9},{13,15},{18,16},{20,... | collective-permute-start | bytes 7864328 | tf_op jit(solution)/shard_map/ppermute | solution.py:550
  1174.8 183.7 %collective-permute-start.44 = (bf16[512,2560]{1,0:T(8,128)(2,1)S(1)}, bf16[512,2560]{1,0:T(8,128)(2,1)S(1)}, u32[]{:S(2)}, u32[]{:S(2)}) collective-permute-start(bf16[512,2560]{1,0:T(8,128)(2,1)S(1)} %add_convert_fusion.4), channel_id=1, source_target_pairs={{2,0},{4,6},{3,1},{5,7},{10,8},{12,14},{11,9},{13,15},{18,16},{20,... | collective-permute-start | bytes 7864328 | tf_op jit(solution)/shard_map/ppermute | solution.py:550
  1178.2 222.2 %collective-permute-start.50 = (bf16[512,2560]{1,0:T(8,128)(2,1)S(1)}, bf16[512,2560]{1,0:T(8,128)(2,1)S(1)}, u32[]{:S(2)}, u32[]{:S(2)}) collective-permute-start(bf16[512,2560]{1,0:T(8,128)(2,1)S(1)} %add_convert_fusion), channel_id=1, source_target_pairs={{2,0},{4,6},{3,1},{5,7},{10,8},{12,14},{11,9},{13,15},{18,16},{20,... | collective-permute-start | bytes 7864328 | tf_op jit(solution)/shard_map/ppermute | solution.py:550
  (84 other events, 2501.3 us)

commit v3 on v2

--- a/solution.py
+++ b/solution.py
@@ -55,158 +55,6 @@
         rows //= 2
         total = total[:rows] + pltpu.roll(total[rows:], span - rows, 1)
     return total
-
-
-def head_mask(shape, head, head_dim):
-    lane = lax.broadcasted_iota(jnp.int32, shape, 1)
-    return (lane >= head * head_dim) & (lane < (head + 1) * head_dim)
-
-
-def window(me, n, part, query, key):
-    q_at = lax.rem(me - query + n, n)
-    k_at = lax.rem(me - key + n, n)
-    return pl.multiple_of((n + k_at - q_at) * part, part)
-
-
-def attend_kernel(n, head_dim, me_ref, table_ref, *refs):
-    pieces, outs, lse_ref, bias, keys, values = (
-        refs[:n], refs[n : 2 * n], refs[2 * n], refs[2 * n + 1], refs[2 * n + 2], refs[2 * n + 3],
-    )
-    part, lanes = pieces[0].shape[2:]
-    per = lanes // head_dim
-    me = me_ref[0]
-
-    @pl.when(pl.program_id(1) == 0)
-    def _():
-        for head in range(per):
-            bias_rows(table_ref[0, head : head + 1, :], bias.at[head])
-
-    for b in range(n):
-        keys[b * part : (b + 1) * part, :] = pieces[b][1, 0]
-        values[b * part : (b + 1) * part, :] = pieces[b][2, 0]
-    for a in range(n):
-        lse = jnp.zeros((part, lanes), F32)
-        mixed = jnp.zeros((part, lanes), F32)
-        lane = lax.broadcasted_iota(jnp.int32, (part, lanes), 1)
-        for head in range(per):
-            mask = head_mask((part, lanes), head, head_dim)
-            query = jnp.where(mask, pieces[a][0, 0], 0)
-            scores = contract_cols(query, keys[...])
-            scores = scores + jnp.concatenate(
-                [bias[head, :, pl.ds(window(me, n, part, a, b), part)] for b in range(n)], axis=1
-            )
-            peak = jnp.max(scores, axis=1, keepdims=True)
-            expo = jnp.exp(scores - peak)
-            total = jnp.sum(expo, axis=1, keepdims=True)
-            probs = (expo * (1.0 / total)).astype(BF16)
-            mixed = jnp.where(mask, dot(probs, values[...]), mixed)
-            lse = jnp.where(lane == head, peak + jnp.log(total), lse)
-        outs[a][0] = mixed.astype(BF16)
-        lse_ref[0, 0, a] = lse
-
-
-def attend_back_kernel(n, head_dim, me_ref, table_ref, *refs):
-    pieces, grads, lse_ref = refs[:n], refs[n : 2 * n], refs[2 * n]
-    outs, table_out = refs[2 * n + 1 : 3 * n + 1], refs[3 * n + 1]
-    bias, sums, keys, values, grad_k, grad_v = refs[3 * n + 2 :]
-    part, lanes = pieces[0].shape[2:]
-    per = lanes // head_dim
-    me = me_ref[0]
-
-    @pl.when(pl.program_id(1) == 0)
-    def _():
-        for head in range(per):
-            bias_rows(table_ref[0, head : head + 1, :], bias.at[head])
-        sums[...] = jnp.zeros_like(sums)
-
-    for b in range(n):
-        keys[b * part : (b + 1) * part, :] = pieces[b][1, 0]
-        values[b * part : (b + 1) * part, :] = pieces[b][2, 0]
-    grad_k[...] = jnp.zeros_like(grad_k)
-    grad_v[...] = jnp.zeros_like(grad_v)
-    for a in range(n):
-        grad_q = jnp.zeros((part, lanes), F32)
-        for head in range(per):
-            mask = head_mask((part, lanes), head, head_dim)
-            query = jnp.where(mask, pieces[a][0, 0], 0)
-            upstream = jnp.where(mask, grads[a][0], 0)
-            starts = [window(me, n, part, a, b) for b in range(n)]
-            scores = contract_cols(query, keys[...])
-            scores = scores + jnp.concatenate(
-                [bias[head, :, pl.ds(start, part)] for start in starts], axis=1
-            )
-            probs = jnp.exp(scores - lse_ref[0, 0, a][:, head : head + 1])
-            grad_probs = contract_cols(upstream, values[...])
-            delta = jnp.sum(grad_probs * probs, axis=1, keepdims=True)
-            grad_scores = (probs * (grad_probs - delta)).astype(BF16)
-            for b, start in enumerate(starts):
-                sums[head, :, pl.ds(start, part)] += grad_scores[:, b * part : (b + 1) * part].astype(F32)
-            grad_q = jnp.where(mask, dot(grad_scores, keys[...]), grad_q)
-            grad_k[...] += contract_rows(grad_scores, query)
-            grad_v[...] += contract_rows(probs.astype(BF16), upstream)
-        outs[a][0, 0] = grad_q.astype(BF16)
-    for b in range(n):
-        outs[b][1, 0] = grad_k[b * part : (b + 1) * part, :].astype(BF16)
-        outs[b][2, 0] = grad_v[b * part : (b + 1) * part, :].astype(BF16)
-
-    @pl.when(pl.program_id(1) == pl.num_programs(1) - 1)
-    def _():
-        for head in range(per):
-            table_out[0, head : head + 1, :] = diagonal_sums(sums.at[head])
-
-
-def attention_calls(n, seqs, part, cols, head_dim):
-    lanes = 2 * head_dim
-    groups, per, span = cols // lanes, lanes // head_dim, 2 * n * part
-    smem = pl.BlockSpec(memory_space=pltpu.SMEM)
-    table_spec = pl.BlockSpec((1, per, span), lambda g, s: (g, 0, 0))
-    three = pl.BlockSpec((3, 1, part, lanes), lambda g, s: (0, s, 0, g))
-    one = pl.BlockSpec((1, part, lanes), lambda g, s: (s, 0, g))
-    lse_spec = pl.BlockSpec((1, 1, n, part, lanes), lambda g, s: (g, s, 0, 0, 0))
-    piece = jax.ShapeDtypeStruct((3, seqs, part, cols), BF16)
-    single = jax.ShapeDtypeStruct((seqs, part, cols), BF16)
-    lse = jax.ShapeDtypeStruct((groups, seqs, n, part, lanes), F32)
-    table = jax.ShapeDtypeStruct((groups, per, span), F32)
-    length = n * part
-    pairs = seqs * (cols // head_dim) * length * length
-    forward = pl.pallas_call(
-        functools.partial(attend_kernel, n, head_dim),
-        grid=(groups, seqs),
-        in_specs=[smem, table_spec] + [three] * n,
-        out_specs=[one] * n + [lse_spec],
-        out_shape=[single] * n + [lse],
-        scratch_shapes=[
-            pltpu.VMEM((per, part, span), F32),
-            pltpu.VMEM((length, lanes), BF16),
-            pltpu.VMEM((length, lanes), BF16),
-        ],
-        compiler_params=pltpu.CompilerParams(vmem_limit_bytes=VMEM_LIMIT),
-        cost_estimate=pl.CostEstimate(
-            flops=4 * pairs * 256, bytes_accessed=2**23, transcendentals=pairs
-        ),
-        name="attend",
-    )
-    backward = pl.pallas_call(
-        functools.partial(attend_back_kernel, n, head_dim),
-        grid=(groups, seqs),
-        in_specs=[smem, table_spec] + [three] * n + [one] * n + [lse_spec],
-        out_specs=[three] * n + [table_spec],
-        out_shape=[piece] * n + [table],
-        scratch_shapes=[
-            pltpu.VMEM((per, part, span), F32),
-            pltpu.VMEM((per, part, span), F32),
-            pltpu.VMEM((length, lanes), BF16),
-            pltpu.VMEM((length, lanes), BF16),
-            pltpu.VMEM((length, lanes), F32),
-            pltpu.VMEM((length, lanes), F32),
-        ],
-        compiler_params=pltpu.CompilerParams(vmem_limit_bytes=VMEM_LIMIT),
-        cost_estimate=pl.CostEstimate(
-            flops=10 * pairs * 256, bytes_accessed=2**24, transcendentals=pairs
-        ),
-        name="attend_back",
-    )
-    return forward, backward
 
 
 MESH = pl.DeviceIdType.MESH
@@ -517,6 +365,549 @@
     )
 
 
+CHUNK = 512
+SLOTS = 4
+
+
+class Pump:
+    def __init__(self, dims, spot, left, right, sources, from_heads, outs, buffers, sems, credits):
+        self.dims, self.spot, self.left, self.right = dims, spot, left, right
+        self.sources, self.from_heads, self.outs = sources, from_heads, outs
+        self.core_out, self.core_in, self.far_out, self.far_in, self.line, self.line_in, self.across_in, self.done = buffers
+        (
+            self.right_sem, self.core_send, self.core_recv, self.far_send, self.far_recv, self.in_send, self.in_recv,
+            self.across_send, self.across_recv, self.out_send, self.out_recv, self.fin_sem,
+        ) = sems
+        self.core_credit, self.far_credit, self.in_credit, self.across_credit, self.out_credit = credits
+        units, heads = dims.units // CHUNK, dims.inner_width // CHUNK
+        self.units, self.heads = units, heads
+        self.early = 3 * units + heads
+        self.total = 3 * units + 4 * heads
+        self.bases = [(i * units, units) for i in range(3)]
+        self.bases += [(3 * units + i * heads, heads) for i in range(4)]
+        me, n = spot.me, dims.n
+        middle = n // 2
+        self.is_middle = (me == middle - 1) | (me == middle)
+        self.is_end = (me == 0) | (me == n - 1)
+        self.has_outer, self.has_inner = jnp.logical_not(self.is_end), jnp.logical_not(self.is_middle)
+        low_side = me < middle
+        self.facing = jnp.where(low_side, middle, middle - 1)
+        toward, away = jnp.where(low_side, me + 1, me - 1), jnp.where(low_side, me - 1, me + 1)
+        self.inner = jnp.where(self.is_middle, self.facing, toward)
+        self.outer = jnp.where(self.is_end, self.inner, away)
+        self.last = self.total + 10
+
+    def core(self, c, k):
+        return remote(
+            self.core_out.at[lax.rem(c, 2)], self.core_in.at[k], self.core_send.at[lax.rem(c, 2)],
+            self.core_recv.at[k], {"shard": self.spot.mate},
+        )
+
+    def far(self, k, d):
+        return remote(
+            self.far_out.at[k, d - 1], self.far_in.at[k, d - 1], self.far_send.at[k, d - 1],
+            self.far_recv.at[k, d - 1], {"shard": self.spot.away(d)},
+        )
+
+    def inward(self, k):
+        return remote(
+            self.line.at[k], self.line_in.at[k], self.in_send.at[k], self.in_recv.at[k], {"ctx": self.inner}
+        )
+
+    def across(self, k):
+        return remote(
+            self.line.at[k], self.across_in.at[k], self.across_send.at[k], self.across_recv.at[k],
+            {"ctx": self.facing},
+        )
+
+    def outward(self, k):
+        return remote(
+            self.done.at[k], self.done.at[k], self.out_send.at[k], self.out_recv.at[k], {"ctx": self.outer}
+        )
+
+    def spend(self, c, credit):
+        @pl.when(c >= SLOTS)
+        def _():
+            pl.semaphore_wait(credit, 1)
+
+    def give(self, c, credit, peer):
+        @pl.when(c + SLOTS < self.total)
+        def _():
+            pl.semaphore_signal(credit, inc=1, device_id=peer, device_id_type=MESH)
+
+    def term(self, c, shard, k):
+        one = lambda b: jnp.where(c >= b, 1, 0)
+        which = one(self.units) + one(3 * self.units) + one(self.early)
+        rows = self.dims.shard_rows
+        return dot(self.left[which, pl.ds(pl.multiple_of(shard * rows, rows), rows), :], self.right[k])
+
+    def fetch(self, c):
+        k = lax.rem(c, SLOTS)
+        for (base, count), source in zip(self.bases, self.sources):
+            @pl.when((c >= base) & (c < base + count))
+            def _():
+                at = pl.ds(pl.multiple_of((c - base) * CHUNK, CHUNK), CHUNK)
+                pltpu.make_async_copy(source.at[:, at], self.right.at[k], self.right_sem.at[k]).start()
+
+        @pl.when((c >= self.early) & (c < self.total))
+        def _():
+            dims = self.dims
+            which, piece = (c - self.early) // self.heads, lax.rem(c - self.early, self.heads)
+            per = CHUNK // dims.cols
+            for i in range(per):
+                for s in range(dims.seqs):
+                    self.right[k, s * dims.part : (s + 1) * dims.part, i * dims.cols : (i + 1) * dims.cols] = (
+                        self.from_heads[which, piece * per + i, s]
+                    )
+
+    def save(self, c, k):
+        for (base, count), out in zip(self.bases, self.outs):
+            @pl.when((c >= base) & (c < base + count))
+            def _():
+                at = pl.ds(pl.multiple_of((c - base) * CHUNK, CHUNK), CHUNK)
+                pltpu.make_async_copy(self.done.at[k], out.at[:, at], self.fin_sem.at[k]).start()
+
+    def settle(self, c, k):
+        pltpu.make_async_copy(self.done.at[k], self.outs[0].at[:, pl.ds(0, CHUNK)], self.fin_sem.at[k]).wait()
+
+        @pl.when(self.has_outer)
+        def _():
+            self.outward(k).wait_send()
+
+        @pl.when(self.has_inner)
+        def _():
+            self.give(c, self.out_credit, {"ctx": self.inner})
+
+    def deliver(self, c, k):
+        @pl.when(self.has_inner)
+        def _():
+            self.outward(k).wait_recv()
+            self.save(c, k)
+
+            @pl.when(self.has_outer)
+            def _():
+                self.spend(c, self.out_credit)
+                self.outward(k).start()
+
+    def finish(self, c, k):
+        @pl.when(self.is_middle)
+        def _():
+            self.across(k).wait_recv()
+            self.across(k).wait_send()
+            self.done[k] = (self.line[k].astype(F32) + self.across_in[k].astype(F32)).astype(BF16)
+            self.give(c, self.across_credit, {"ctx": self.facing})
+            self.save(c, k)
+
+            @pl.when(self.has_outer)
+            def _():
+                self.spend(c, self.out_credit)
+                self.outward(k).start()
+
+        @pl.when(self.has_inner)
+        def _():
+            self.inward(k).wait_send()
+
+    def collect(self, c, k):
+        @pl.when(self.has_outer)
+        def _():
+            self.inward(k).wait_recv()
+            self.line[k] = (self.line[k].astype(F32) + self.line_in[k].astype(F32)).astype(BF16)
+            self.give(c, self.in_credit, {"ctx": self.outer})
+
+        @pl.when(self.is_middle)
+        def _():
+            self.spend(c, self.across_credit)
+            self.across(k).start()
+
+        @pl.when(self.has_outer & self.has_inner)
+        def _():
+            self.spend(c, self.in_credit)
+            self.inward(k).start()
+
+    def own(self, c, k):
+        total = self.term(c, self.spot.shard, k) + self.core_in[k, self.spot.chips - 1].astype(F32)
+        for d in range(1, self.spot.chips):
+            self.far(k, d).wait_send()
+            self.far(k, d).wait_recv()
+            total = total + self.far_in[k, d - 1].astype(F32)
+        self.line[k] = total.astype(BF16)
+        self.give(c, self.core_credit, {"shard": self.spot.mate})
+        for d in range(1, self.spot.chips):
+            sender = lax.rem(self.spot.shard - 2 * d + self.spot.shards, self.spot.shards)
+            self.give(c, self.far_credit.at[d - 1], {"shard": sender})
+
+        @pl.when(self.is_end & self.has_inner)
+        def _():
+            self.spend(c, self.in_credit)
+            self.inward(k).start()
+
+    def to_chips(self, c, k):
+        self.core(c, k).wait_recv()
+        self.core(c, k).wait_send()
+        for d in range(1, self.spot.chips):
+            pair = self.term(c, self.spot.away(d), k) + self.core_in[k, d - 1].astype(F32)
+            self.far_out[k, d - 1] = pair.astype(BF16)
+            self.spend(c, self.far_credit.at[d - 1])
+            self.far(k, d).start()
+
+    def to_core(self, c, k):
+        @pl.when(c < self.early)
+        def _():
+            pltpu.make_async_copy(
+                self.sources[0].at[:, pl.ds(0, CHUNK)], self.right.at[k], self.right_sem.at[k]
+            ).wait()
+
+        chips, half = self.spot.chips, lax.rem(c, 2)
+        for d in range(1, chips + 1):
+            shard = 2 * lax.rem(self.spot.chip + d, chips) + 1 - self.spot.core
+            self.core_out[half, d - 1] = self.term(c, shard, k).astype(BF16)
+        self.spend(c, self.core_credit)
+        self.core(c, k).start()
+
+    def step(self, t):
+        def at(lag, stage):
+            c = t - lag
+
+            @pl.when((c >= 0) & (c < self.total))
+            def _():
+                stage(c, lax.rem(c, SLOTS))
+
+        at(10, self.settle)
+        at(9, self.deliver)
+        at(7, self.finish)
+        at(5, self.collect)
+        at(3, self.own)
+
+        @pl.when(t + 1 < self.total)
+        def _():
+            self.fetch(t + 1)
+
+        at(1, self.to_chips)
+        at(0, self.to_core)
+
+    def steps(self, first, last):
+        @pl.loop(first, last)
+        def _(t):
+            self.step(t)
+
+
+def backward_kernel(
+    dims, gain_two, table, lse, pieces,
+    term, ffn_term, left_g, left_two, left_one, inner, grad_gate, grad_up, attended, hidden, cotangent,
+    wo, wq, wk, wv,
+    down_out, gate_out, up_out, o_out, q_out, k_out, v_out,
+    grad_hidden, ffn_other, term_one, other_one, ffn_gain, table_out,
+    left, right, core_out, core_in, far_out, far_in, line, line_in, across_in, done,
+    swap_in, staged, grads, grads_out, grads_in,
+    right_sem, core_send, core_recv, far_send, far_recv, in_send, in_recv, across_send, across_recv,
+    out_send, out_recv, fin_sem, swap_send, swap_recv, head_send, head_recv, back_send, back_recv,
+    one_send, one_recv, ffn_sem, local_sem,
+    core_credit, far_credit, in_credit, across_credit, out_credit,
+):
+    spot = Spot(*dims.mesh)
+    n, seqs, part, cols, head_dim, width = dims.n, dims.seqs, dims.part, dims.cols, dims.head_dim, dims.width
+    me, shards, shard_rows = spot.me, spot.shards, dims.shard_rows
+    lanes, per = 2 * head_dim, 2
+    groups = cols // lanes
+    span = table.shape[1]
+    other_half = {"tp": 1 - spot.half}
+    pump = Pump(
+        dims, spot, left, right, (inner, grad_gate, grad_up, attended), grads_in,
+        (down_out, gate_out, up_out, o_out, q_out, k_out, v_out),
+        (core_out, core_in, far_out, far_in, line, line_in, across_in, done),
+        (
+            right_sem, core_send, core_recv, far_send, far_recv, in_send, in_recv, across_send, across_recv,
+            out_send, out_recv, fin_sem,
+        ),
+        (core_credit, far_credit, in_credit, across_credit, out_credit),
+    )
+    loads = [
+        pltpu.make_async_copy(source, left.at[i], local_sem.at[i])
+        for i, source in ((0, left_g), (1, left_two), (3, left_one))
+    ]
+    for load in loads:
+        load.start()
+    pump.fetch(0)
+    spot.barrier()
+    swaps = [
+        remote(term.at[s], swap_in.at[s], swap_send.at[s], swap_recv.at[s], other_half) for s in range(seqs)
+    ]
+    for swap in swaps:
+        swap.start()
+    for load in loads:
+        load.wait()
+    ffn_gain[...] = jnp.zeros_like(ffn_gain)
+    table_out[...] = jnp.zeros_like(table_out)
+    pump.steps(0, 4)
+
+    def head_move(s, peer):
+        return remote(
+            staged.at[peer, s], grads.at[me, s], head_send.at[s, peer], head_recv.at[s, me], {"ctx": peer}
+        )
+
+    def head_wait(s, peer):
+        remote(
+            staged.at[peer, s], grads.at[peer, s], head_send.at[s, peer], head_recv.at[s, peer], {"ctx": peer}
+        ).wait_recv()
+
+    def second_norm(s, weights, values, given, own, result, sem):
+        at = pl.ds(s * part, part)
+        copies = [
+            pltpu.make_async_copy(hidden.at[at, :], values, sem.at[0]),
+            pltpu.make_async_copy(cotangent.at[at, :], given, sem.at[1]),
+            pltpu.make_async_copy(term.at[s], own, sem.at[2]),
+        ]
+        for copy in copies:
+            copy.start()
+        for copy in copies:
+            copy.wait()
+        swaps[s].wait_recv()
+
+        @pl.loop(0, part // 64)
+        def _(i):
+            here = pl.ds(pl.multiple_of(i * 64, 64), 64)
+            h = values[here, :]
+            grad = own[here, :].astype(F32) + swap_in[s, here, :].astype(F32)
+            scale = rms_scale(h)
+            ffn_gain[...] += jnp.sum(grad * h * scale, axis=0, keepdims=True)
+            total = given[here, :].astype(F32) + rms_back(h, scale, gain_two[...], grad)
+            result[here, :] = total
+            own[here, :] = total.astype(BF16)
+
+        saved = pltpu.make_async_copy(result, grad_hidden.at[at, :], sem.at[0])
+        saved.start()
+        total = dot(own[:, :shard_rows], weights[0])
+        for j in range(1, shards):
+            total += dot(own[:, j * shard_rows : (j + 1) * shard_rows], weights[j])
+        for k in range(n):
+            staged[k, s] = total[:, k * cols : (k + 1) * cols].astype(BF16)
+        for d in range(1, n):
+            head_move(s, lax.rem(me + d, n)).start()
+        grads[me, s] = staged[me, s]
+        left[2, :, s * part : (s + 1) * part] = own[...].T
+        saved.wait()
+
+    def second_norms(weights, values, given, own, result, sem):
+        load = pltpu.make_async_copy(wo, weights, sem.at[3])
+        load.start()
+        load.wait()
+        for s in range(seqs):
+            second_norm(s, weights, values, given, own, result, sem)
+            if s == 0:
+                pump.steps(4, 5)
+
+    pl.run_scoped(
+        second_norms,
+        pltpu.VMEM((shards, shard_rows, dims.inner_width), BF16),
+        pltpu.VMEM((part, width), F32),
+        pltpu.VMEM((part, width), BF16),
+        pltpu.VMEM((part, width), BF16),
+        pltpu.VMEM((part, width), F32),
+        pltpu.SemaphoreType.DMA((4,)),
+    )
+    ffn_swap = remote(ffn_term, ffn_other, ffn_sem.at[0], ffn_sem.at[1], other_half)
+    ffn_swap.start()
+    pump.steps(5, 7)
+
+    def back_move(j, s, peer):
+        return remote(
+            grads_out.at[j, peer, s], grads_in.at[j, me, s], back_send.at[j, s, peer], back_recv.at[j, s, me],
+            {"ctx": peer},
+        )
+
+    def back_wait(j, s, peer):
+        remote(
+            grads_out.at[j, peer, s], grads_in.at[j, peer, s], back_send.at[j, s, peer], back_recv.at[j, s, peer],
+            {"ctx": peer},
+        ).wait_recv()
+
+    def attention(bias, sums, grad_k, grad_v):
+        @pl.loop(0, seqs * groups * n)
+        def _(i):
+            a, group, s = lax.rem(i, n), lax.rem(i // n, groups), i // (n * groups)
+            at = pl.ds(pl.multiple_of(group * lanes, lanes), lanes)
+
+            @pl.when((a == 0) & (group == 0))
+            def _():
+                for d in range(1, n):
+                    head_wait(s, lax.rem(me + d, n))
+
+            @pl.when(a == 0)
+            def _():
+                for j in range(per):
+                    bias_rows(table[pl.ds(group * per + j, 1), :], bias.at[j])
+                sums[...] = jnp.zeros_like(sums)
+                grad_k[...] = jnp.zeros_like(grad_k)
+                grad_v[...] = jnp.zeros_like(grad_v)
+
+            lane = lax.broadcasted_iota(jnp.int32, (part, lanes), 1)
+            result = jnp.zeros((part, lanes), F32)
+            for j in range(per):
+                mask = (lane >= j * head_dim) & (lane < (j + 1) * head_dim)
+                query = jnp.where(mask, pieces[0, a, s, :, at], 0)
+                upstream = jnp.where(mask, grads[a, s, :, at], 0)
+                log_total = jnp.sum(jnp.where(lane == group * per + j, lse[s, a], 0.0), axis=1, keepdims=True)
+                windows = [pl.ds(pl.multiple_of((n + b - a) * part, part), part) for b in range(n)]
+                probs, grad_probs = [], []
+                for b in range(n):
+                    scores = contract_cols(query, pieces[1, b, s, :, at]) + bias[j, :, windows[b]]
+                    probs.append(jnp.exp(scores - log_total))
+                    grad_probs.append(contract_cols(upstream, pieces[2, b, s, :, at]))
+                delta = sum(jnp.sum(g * p, axis=1, keepdims=True) for g, p in zip(grad_probs, probs))
+                summed = None
+                for b in range(n):
+                    grad_scores = (probs[b] * (grad_probs[b] - delta)).astype(BF16)
+                    sums[j, :, windows[b]] += grad_scores.astype(F32)
+                    product = dot(grad_scores, pieces[1, b, s, :, at])
+                    summed = product if summed is None else summed + product
+                    grad_k[b] += contract_rows(grad_scores, query)
+                    grad_v[b] += contract_rows(probs[b].astype(BF16), upstream)
+                result = jnp.where(mask, summed, result)
+            grads_out[0, a, s, :, at] = result.astype(BF16)
+
+            @pl.when(a == n - 1)
+            def _():
+                for b in range(n):
+                    grads_out[1, b, s, :, at] = grad_k[b].astype(BF16)
+                    grads_out[2, b, s, :, at] = grad_v[b].astype(BF16)
+                for j in range(per):
+                    table_out[pl.ds(group * per + j, 1), :] += diagonal_sums(sums.at[j])
+
+            @pl.when((a == n - 1) & (group == groups - 1))
+            def _():
+                for j in range(3):
+                    for d in range(1, n):
+                        back_move(j, s, lax.rem(me + d, n)).start()
+                    grads_in[j, me, s] = grads_out[j, me, s]
+
+            @pl.when(a == n - 1)
+            def _():
+                pump.step(7 + i // n)
+
+    pl.run_scoped(
+        attention,
+        pltpu.VMEM((per, part, span), F32),
+        pltpu.VMEM((per, part, span), F32),
+        pltpu.VMEM((n, part, lanes), F32),
+        pltpu.VMEM((n, part, lanes), F32),
+    )
+    after = 7 + seqs * groups
+    pump.steps(after, after + 1)
+    for s in range(seqs):
+        for j in range(3):
+            for d in range(1, n):
+                back_wait(j, s, lax.rem(me + d, n))
+
+    def first_norm_terms(weights, values, sem):
+        def load(shard):
+            return [
+                pltpu.make_async_copy(w.at[shard], weights.at[shard % 2, j], sem.at[shard % 2, j])
+                for j, w in enumerate((wq, wk, wv))
+            ]
+
+        for copy in load(0):
+            copy.start()
+        for j in range(3):
+            for s in range(seqs):
+                for k in range(n):
+                    values[j, s * part : (s + 1) * part, k * cols : (k + 1) * cols] = grads_in[j, k, s]
+        for shard in range(shards):
+            if shard + 1 < shards:
+                for copy in load(shard + 1):
+                    copy.start()
+            for copy in load(shard):
+                copy.wait()
+            total = contract_cols(values[0], weights[shard % 2, 0])
+            total += contract_cols(values[1], weights[shard % 2, 1])
+            total += contract_cols(values[2], weights[shard % 2, 2])
+            for s in range(seqs):
+                term_one[s, :, shard * shard_rows : (shard + 1) * shard_rows] = (
+                    total[s * part : (s + 1) * part].astype(BF16)
+                )
+
+    pl.run_scoped(
+        first_norm_terms,
+        pltpu.VMEM((2, 3, shard_rows, dims.inner_width), BF16),
+        pltpu.VMEM((3, seqs * part, dims.inner_width), BF16),
+        pltpu.SemaphoreType.DMA((2, 3)),
+    )
+    ones = [
+        remote(term_one.at[s], other_one.at[s], one_send.at[s], one_recv.at[s], other_half) for s in range(seqs)
+    ]
+    for swap in ones:
+        swap.start()
+    pump.steps(after + 1, pump.last)
+    for swap in swaps:
+        swap.wait_send()
+    for copy in ones + [ffn_swap]:
+        copy.wait_recv()
+        copy.wait_send()
+    for s in range(seqs):
+        for d in range(1, n):
+            peer = lax.rem(me + d, n)
+            head_move(s, peer).wait_send()
+            for j in range(3):
+                back_move(j, s, peer).wait_send()
+
+
+def backward_call(dims):
+    rows, width, n, part, seqs = dims.seqs * dims.part, dims.width, dims.n, dims.part, dims.seqs
+    shards, shard_rows, inner, units, cols = dims.shards, dims.shard_rows, dims.inner_width, dims.units, dims.cols
+    span, chips = 2 * n * part, dims.shards // 2
+    vmem, anywhere = pl.BlockSpec(memory_space=pltpu.VMEM), pl.BlockSpec(memory_space=pl.ANY)
+    shape, dma, regular = jax.ShapeDtypeStruct, pltpu.SemaphoreType.DMA, pltpu.SemaphoreType.REGULAR
+    far = max(chips - 1, 1)
+    block = (shard_rows, CHUNK)
+    return pl.pallas_call(
+        functools.partial(backward_kernel, dims),
+        in_specs=[vmem] * 4 + [anywhere] * 15,
+        out_specs=[anywhere] * 9 + [vmem, anywhere, vmem, vmem],
+        out_shape=[shape((shard_rows, units), BF16)] * 3
+        + [shape((shard_rows, inner), BF16)] * 4
+        + [
+            shape((rows, width), F32),
+            shape((rows, width), BF16),
+            shape((seqs, part, width), BF16),
+            shape((seqs, part, width), BF16),
+            shape((1, width), F32),
+            shape((dims.own_heads, span), F32),
+        ],
+        scratch_shapes=[
+            pltpu.VMEM((4, width, rows), BF16),
+            pltpu.VMEM((SLOTS, rows, CHUNK), BF16),
+            pltpu.VMEM((2, chips) + block, BF16),
+            pltpu.VMEM((SLOTS, chips) + block, BF16),
+            pltpu.VMEM((SLOTS, far) + block, BF16),
+            pltpu.VMEM((SLOTS, far) + block, BF16),
+            pltpu.VMEM((SLOTS,) + block, BF16),
+            pltpu.VMEM((SLOTS,) + block, BF16),
+            pltpu.VMEM((SLOTS,) + block, BF16),
+            pltpu.VMEM((SLOTS,) + block, BF16),
+            pltpu.VMEM((seqs, part, width), BF16),
+            pltpu.VMEM((n, seqs, part, cols), BF16),
+            pltpu.VMEM((n, seqs, part, cols), BF16),
+            pltpu.VMEM((3, n, seqs, part, cols), BF16),
+            pltpu.VMEM((3, n, seqs, part, cols), BF16),
+            dma((SLOTS,)),
+            dma((2,)),
+            dma((SLOTS,)),
+            dma((SLOTS, far)),
+            dma((SLOTS, far)),
+        ]
+        + [dma((SLOTS,))] * 7
+        + [dma((seqs,))] * 2
+        + [dma((seqs, n))] * 2
+        + [dma((3, seqs, n))] * 2
+        + [dma((seqs,))] * 2
+        + [dma((2,)), dma((4,))]
+        + [regular, regular((far,)), regular, regular, regular],
+        compiler_params=pltpu.CompilerParams(
+            vmem_limit_bytes=62 * 2**20, collective_id=1, has_side_effects=True
+        ),
+        name="backward",
+    )
+
+
 def ring(n, d):
     return [(i, (i + d) % n) for i in range(n)]
 
@@ -640,8 +1031,6 @@
     )
     groups = cols // (2 * head_dim)
     offset_bias = offset_bias.reshape(groups, 2, 2 * reach)
-    where_am_i = me.astype(jnp.int32).reshape(1)
-    unused_attend, attend_back = attention_calls(n, seqs, part, cols, head_dim)
 
     dims = Dims(links, seqs, part, width, inner_width, gate_weight.shape[1], heads)
     normed, hidden, normed_two, attended, lse, pieces, *full = forward_call(dims)(
@@ -650,66 +1039,37 @@
         offset_bias.reshape(own_heads, 2 * reach),
         query_weight, key_weight, value_weight, output_weight, gate_weight, up_weight, down_weight,
     )
-    wq, wk, wv, wo, wi0, wi1, wff = (w.reshape(width, w.shape[2]) for w in full)
+    wi0, wi1, wff = (w.reshape(width, w.shape[2]) for w in full[4:])
     inputs = tokens.reshape(rows, width).astype(F32)
-    scale_one, scale_two = rms_scale(inputs), rms_scale(hidden)
-
-    def heads_of(values, d):
-        start = at_ctx(d) * cols
-        return [lax.dynamic_slice_in_dim(v, start, cols, 1).reshape(seqs, part, cols) for v in values]
-
-    def heads_back(blocks):
-        blocks = [blocks[0]] + [lax.ppermute(blocks[d], "ctx", ring(n, n - d)) for d in range(1, n)]
-        around = jnp.concatenate(blocks, axis=-1)
-        twice = jnp.concatenate([around, around], axis=-1)
-        return lax.dynamic_slice_in_dim(twice, (n - me) * cols, n * cols, around.ndim - 1)
-
-    pieces = [lax.dynamic_index_in_dim(pieces, at_ctx(-d), 1, keepdims=False) for d in range(n)]
-    lse = jnp.stack([lax.dynamic_index_in_dim(lse, at_ctx(-d), 1, keepdims=False) for d in range(n)], axis=1)
-    lse = jnp.stack([lse[..., 2 * g : 2 * g + 2] for g in range(groups)])
-    lse = jnp.pad(lse, ((0, 0),) * 4 + ((0, 2 * head_dim - 2),))
+    scale_one = rms_scale(inputs)
+
     gate = dot(normed_two, wi0)
     up = dot(normed_two, wi1)
     inner = geglu(gate, up).astype(BF16)
-    ffn_out = links.tp_sum(contract_cols(inner, wff).astype(BF16))
-    result = (hidden + ffn_out).astype(BF16).reshape(seqs, part, width)
-
-    upstream = cotangent.reshape(rows, width).astype(F32)
+    ffn_term = contract_cols(inner, wff).astype(BF16)
     upstream_low = cotangent.reshape(rows, width)
-    grad_down_w = links.ctx_sum(links.shard_sums(upstream_low, inner))
     grad_inner = dot(upstream_low, wff)
     unused, geglu_backward_pull = jax.vjp(geglu, gate, up)
     grad_gate, grad_up = geglu_backward_pull(grad_inner)
     grad_gate = grad_gate.astype(BF16)
     grad_up = grad_up.astype(BF16)
-    grad_normed_two = links.tp_sum(
-        (contract_cols(grad_gate, wi0) + contract_cols(grad_up, wi1)).astype(BF16)
-    )
-    grad_gate_w = links.ctx_sum(links.shard_sums(normed_two, grad_gate))
-    grad_up_w = links.ctx_sum(links.shard_sums(normed_two, grad_up))
-    grad_ffn_gain = jnp.sum(grad_normed_two * hidden * scale_two, axis=0)
-    grad_hidden = upstream + rms_back(hidden, scale_two, gain_two, grad_normed_two)
-    branch_low = grad_hidden.astype(BF16)
-    grad_attended = dot(branch_low, wo).astype(BF16)
-    grad_output_w = links.ctx_sum(links.shard_sums(branch_low, attended))
-
-    upstreams = [heads_of([grad_attended], d)[0] for d in range(n)]
-    upstreams = [upstreams[0]] + [lax.ppermute(upstreams[d], "ctx", ring(n, d)) for d in range(1, n)]
-    *grad_pieces, offset_grad = attend_back(where_am_i, offset_bias, *pieces, *upstreams, lse)
-    grad_projected = heads_back(grad_pieces).reshape(3, rows, inner_width)
-    grad_query, grad_key, grad_value = grad_projected[0], grad_projected[1], grad_projected[2]
-    offset_grad = offset_grad.reshape(own_heads, 2 * reach)
+    term_two = (contract_cols(grad_gate, wi0) + contract_cols(grad_up, wi1)).astype(BF16)
+    *weight_grads, grad_hidden, ffn_other, term_one, other_one, grad_ffn_gain, offset_grad = backward_call(dims)(
+        gain_two.reshape(1, width), offset_bias.reshape(own_heads, 2 * reach), lse, pieces,
+        term_two.reshape(seqs, part, width), ffn_term, upstream_low.T, normed_two.T, normed.T,
+        inner, grad_gate, grad_up, attended, hidden, upstream_low,
+        full[3], full[0], full[1], full[2],
+    )
+    grad_down_w, grad_gate_w, grad_up_w, grad_output_w, grad_query_w, grad_key_w, grad_value_w = (
+        g.astype(F32) for g in weight_grads
+    )
+    result = (hidden + (ffn_term.astype(F32) + ffn_other.astype(F32))).astype(BF16).reshape(seqs, part, width)
+    grad_ffn_gain = grad_ffn_gain[0]
     table_part = jnp.sum(jnp.where(indicator[:, None, :], offset_grad[None], 0.0), axis=-1)
     grad_table = lax.dynamic_update_slice(
         jnp.zeros((slots, heads), F32), table_part, (0, me * own_heads)
     )
-
-    grad_normed = links.tp_sum(
-        (contract_cols(grad_query, wq) + contract_cols(grad_key, wk) + contract_cols(grad_value, wv)).astype(BF16)
-    )
-    grad_query_w = links.ctx_sum(links.shard_sums(normed, grad_query))
-    grad_key_w = links.ctx_sum(links.shard_sums(normed, grad_key))
-    grad_value_w = links.ctx_sum(links.shard_sums(normed, grad_value))
+    grad_normed = (term_one.astype(F32) + other_one.astype(F32)).reshape(rows, width)
     grad_norm_gain = jnp.sum(grad_normed * inputs * scale_one, axis=0)
     grad_inputs = grad_hidden + rms_back(inputs, scale_one, gain_one, grad_normed)
     small = links.small_sum(jnp.concatenate([grad_norm_gain, grad_ffn_gain, grad_table.reshape(-1)]))

time: 1410 us -> 865 us (0.61)
  waiting for transfers between devices: 709 us -> 4.29 us
  Pallas kernels: 367 us -> 734 us
  matrix products: 160 us -> 65.1 us
  starting transfers between devices: 69.2 us -> 2.72 us
  other arithmetic: 76.6 us -> 31.4 us
    ppermute x51 -> x0, waiting for transfers between devices: 609 us -> none  [the longest x7 231 us: ctx_sum(): outward = lax.ppermute(whole, 'ctx', [(1, 0), (2, 3)])]
    pallas_call x1, Pallas kernels: 42.1 us -> 409 us  [per_device(): backward_call(dims)]
    ppermute x4, waiting for transfers between devices: 100 us -> 4.29 us  [small_sum(): value = value + lax.ppermute(value, axis, [(i, i ^ step) for i in range(n)])]
    dot_general x28 -> x0, matrix products: 79.1 us -> none  [contract_rows(): lax.dot_general(left, right, (((0,), (0,)), ((), ())), preferred_element_...]
    ppermute x51 -> x0, starting transfers between devices: 68.2 us -> none  [the longest x7 28.8 us: ctx_sum(): inward = lax.ppermute(low, 'ctx', [(0, 1), (3, 2)])]
    convert_element_type x30 -> x8, other arithmetic: 63.3 us -> 17.9 us  [the longest x7 15.4 us: per_device(): g.astype(F32)]
    dot_general x6 -> x3, matrix products: 45.6 us -> 30.6 us  [contract_cols(): lax.dot_general(left, right, (((1,), (1,)), ((), ())), preferred_element_...]
    dot_general x4 -> x3, matrix products: 34.9 us -> 33.8 us  [dot(): return jnp.dot(left, right, preferred_element_type=F32)]
  transfers between devices with their start and end apart: 55 -> 4, of which waited for: 20 -> 2; matrix products, arithmetic and copies ran while one was open for 13% -> 3% of each run, Pallas kernels for 3% -> 0%
where the time goes in v3:
time: 865 us; the launch traced here: 856 us
  Pallas kernels  734 us (85%)
  matrix products  65.1 us (8%)
  other arithmetic  31.4 us (4%)
  local copies, waits for them, and re-layouts  17 us (2%)
    pallas_call x1, Pallas kernels, per_device(): backward_call(dims)  409 us
    pallas_call x1, Pallas kernels, per_device(): forward_call(dims)  325 us
    dot_general x3, matrix products, dot(): return jnp.dot(left, right, preferred_element_type=F32)  33.8 us
    dot_general x3, matrix products, contract_cols(): lax.dot_general(left, right, (((1,), (1,)), ((), ())), preferred_element_...  30.6 us
  transfers between devices with their start and end apart: 4, of which 2 were waited for; matrix products, arithmetic and copies ran while one was open for 3% of the time, Pallas kernels for 0%

profile of v3, /device:TPU:0, one launch (start us, length us, event | category | flops | bytes accessed | tf_op | source)
XLA Modules:
  0.0 856.2 jit_solution(2395087001538319222)
XLA Ops:
  4.0 2.1 fusion.8
  10.2 325.3 %forward.1 = (bf16[512,2048]{1,0:T(8,128)(2,1)}, f32[512,2048]{1,0:T(8,128)}, bf16[512,2048]{1,0:T(8,128)(2,1)}, bf16[512,1024]{1,0:T(8,128)(2,1)}, f32[2,4,256,...) custom-call(bf16[512,2048]{1,0:T(8,128)(2,1)} %bitcast.53, ...), custom_call_target="tpu_custom_call" | custom-call | tf_op jit(solution)/shard_map/forward/pallas_call | solution.py:1036
  335.5 3.9 copy.35
  339.5 11.1 %fusion.21 = f32[512,2560]{1,0:T(8,128)} fusion(bf16[512,2048]{1,0:T(8,128)(2,1)} %get-tuple-element.39, bf16[2048,2560]{1,0:T(8,128)(2,1)} %bitcast.73), kind=kOutput, calls=%fused_computation.44 | convolution fusion | flops 5368709120 | bytes 17825792 | tf_op jit(solution)/shard_map/dot_general | solution.py:24
  350.6 7.3 fusion.23
  357.9 15.4 %multiply_convert_fusion = (bf16[512,2560]{1,0:T(8,128)(2,1)S(1)}, bf16[512,2560]{1,0:T(8,128)(2,1)S(1)}, bf16[512,2560]{1,0:T(8,128)(2,1)}) fusion(f32[512,2560]{1,0:T(8,128)} %fusion.21, f32[2560,512]{0,1:T(8,128)} %fusion.23, bf16[512,2048]{1,0:T(8,128)(2,1)S(1)} %copy-done.13, bf16[2048,2560]{1,0:T(8,128)(2,1)} %bitcast.71), kind=kOutput, calls=%fused_computation.15 | convolution fusion | flops 5402787840 | bytes 30932992 | tf_op jit(solution)/shard_map/dot_general | solution.py:24
  373.3 12.7 %convolution_convert_fusion.ffn_term = bf16[512,2048]{1,0:T(8,128)(2,1)} fusion(bf16[512,2560]{1,0:T(8,128)(2,1)S(1)} %get-tuple-element.90.inner, bf16[2048,2560]{1,0:T(8,128)(2,1)} %bitcast.77), kind=kOutput, calls=%fused_computation.28 | convolution fusion | flops 5369757696 | bytes 15204352 | tf_op jit(solution)/shard_map/dot_general | solution.py:20
  386.0 7.1 fusion.22
  393.2 3.9 copy.36
  397.1 2.7 copy.37.left_g
  399.8 10.7 %add_convert_fusion.1 = bf16[512,2048]{1,0:T(8,128)(2,1)} fusion(f32[512,2048]{1,0:T(8,128)} %fusion.22, bf16[512,2560]{1,0:T(8,128)(2,1)} %get-tuple-element.92.grad_up, bf16[2048,2560]{1,0:T(8,128)(2,1)} %bitcast.72), kind=kOutput, calls=%fused_computation.27 | convolution fusion | flops 5370806272 | bytes 19398656 | tf_op jit(solution)/shard_map/dot_general | solution.py:20
  410.5 409.0 %backward.1 = (bf16[512,2560]{1,0:T(8,128)(2,1)}, bf16[512,2560]{1,0:T(8,128)(2,1)}, bf16[512,2560]{1,0:T(8,128)(2,1)}, bf16[512,1024]{1,0:T(8,128)(2,1)}, bf16[...) custom-call(f32[1,2048]{1,0:T(1,128)} %bitcast.64, ...), custom_call_target="tpu_custom_call" | custom-call | tf_op jit(solution)/shard_map/backward/pallas_call | solution.py:1057
  820.9 4.7 fusion.11
  827.5 3.1 collective-permute-done.1
  830.7 3.7 fusion.14
  834.4 2.0 collective-permute-start.3
  836.4 2.5 add_convert_fusion
  838.9 3.0 convert_element_type.81
  842.0 3.0 convert_element_type.82
  845.0 3.0 convert_element_type.83
  848.1 1.6 convert_element_type.77
  849.6 1.6 convert_element_type.78
  851.2 1.6 convert_element_type.79
  852.8 1.6 convert_element_type.80
  (86 shorter events, 12.2 us)
Async XLA Ops:
  0.6 8.2 copy-start
  4.0 331.5 %copy-start.18 = (f32[2048]{0:T(1024)}, f32[2048]{0:T(1024)S(1)}, u32[]{:S(2)}) copy-start(f32[2048]{0:T(1024)S(1)} %stack.15) | copy-start | bytes 24580
  339.4 11.1 %copy-start.5 = (bf16[2,256,2048]{2,1,0:T(8,128)(2,1)S(1)}, bf16[2,256,2048]{2,1,0:T(8,128)(2,1)}, u32[]{:S(2)}) copy-start(bf16[2,256,2048]{2,1,0:T(8,128)(2,1)} %param.14) | copy-start | bytes 6291460
  339.5 11.1 %copy-start.20 = (bf16[4,512,2560]{2,1,0:T(8,128)(2,1)S(1)}, bf16[4,512,2560]{2,1,0:T(8,128)(2,1)}, u32[]{:S(2)}) copy-start(bf16[4,512,2560]{2,1,0:T(8,128)(2,1)} %get-tuple-element.42) | copy-start | bytes 31457284
  350.6 7.3 copy-start.13
  357.9 28.1 %slice-start = ((s8[10485760]{0:T(1024)(128)(4,1)}), s8[2097152]{0:T(1024)(128)(4,1)S(1)}, s32[]{:S(2)}) async-start(s8[10485760]{0:T(1024)(128)(4,1)} %bitcast.74), calls=%async_computation | async-start | bytes 4194304
  357.9 28.1 %slice-start.1 = ((s8[10485760]{0:T(1024)(128)(4,1)}), s8[4194304]{0:T(1024)(128)(4,1)S(1)}, s32[]{:S(2)}) async-start(s8[10485760]{0:T(1024)(128)(4,1)} %bitcast.74), calls=%async_computation.1 | async-start | bytes 8388608
  373.3 12.7 %copy-start.7 = (bf16[512,2560]{1,0:T(8,128)(2,1)}, bf16[512,2560]{1,0:T(8,128)(2,1)S(1)}, u32[]{:S(2)}) copy-start(bf16[512,2560]{1,0:T(8,128)(2,1)S(1)} %get-tuple-element.90.inner) | copy-start | bytes 7864324
  373.3 12.7 %copy-start.8 = (bf16[512,2560]{1,0:T(8,128)(2,1)}, bf16[512,2560]{1,0:T(8,128)(2,1)S(1)}, u32[]{:S(2)}) copy-start(bf16[512,2560]{1,0:T(8,128)(2,1)S(1)} %get-tuple-element.91.grad_gate) | copy-start | bytes 7864324
  373.3 12.7 %slice-start.2 = ((s8[10485760]{0:T(1024)(128)(4,1)}), s8[4194304]{0:T(1024)(128)(4,1)S(1)}, s32[]{:S(2)}) async-start(s8[10485760]{0:T(1024)(128)(4,1)} %bitcast.74), calls=%async_computation.2 | async-start | bytes 8388608
  820.9 4.7 copy-start.19
  820.9 9.8 %copy-start.2 = (bf16[2,256,2048]{2,1,0:T(8,128)(2,1)S(1)}, bf16[2,256,2048]{2,1,0:T(8,128)(2,1)}, u32[]{:S(2)}) copy-start(bf16[2,256,2048]{2,1,0:T(8,128)(2,1)} %param.13) | copy-start | bytes 6291460
  820.9 9.8 %copy-start.6 = (f32[512,2048]{1,0:T(8,128)S(1)}, f32[512,2048]{1,0:T(8,128)}, u32[]{:S(2)}) copy-start(f32[512,2048]{1,0:T(8,128)} %get-tuple-element.52) | copy-start | bytes 12582916
  825.6 1.3 collective-permute-start
  826.9 3.8 collective-permute-start.1
  830.6 3.8 collective-permute-start.2
  830.7 5.8 copy-start.3
  830.7 5.7 copy-start.4
  830.7 5.7 copy-start.12
  834.4 19.9 %collective-permute-start.3 = (f32[4608]{0:T(1024)S(1)}, f32[4608]{0:T(1024)S(1)}, u32[]{:S(2)}, u32[]{:S(2)}) collective-permute-start(f32[4608]{0:T(1024)S(1)} %add.69), channel_id=1, source_target_pairs={{0,4},{2,6},{4,0},{6,2},{1,5},{3,7},{5,1},{7,3},{8,12},{10,14},{12... | collective-permute-start | bytes 55304 | tf_op jit(solution)/shard_map/ppermute | solution.py:977
  845.0 4.6 copy-start.16
  848.0 3.2 copy-start.15
  848.0 4.7 copy-start.14
  849.6 6.1 copy-start.1
  (4 other events, 11.6 us)

commit v4 on v3

--- a/solution.py
+++ b/solution.py
@@ -86,12 +86,36 @@
     )
 
 
+class Keep:
+    def __init__(self, jobs, room, sem):
+        self.halves = []
+        for i, (own, full) in enumerate(jobs):
+            self.halves.append(pltpu.make_async_copy(own, room, sem.at[0]))
+            self.halves.append(pltpu.make_async_copy(room, full, sem.at[1]))
+        self.at = 0
+        self.halves[0].start()
+
+    def step(self):
+        if self.at < len(self.halves):
+            self.halves[self.at].wait()
+            self.at += 1
+            if self.at < len(self.halves):
+                self.halves[self.at].start()
+
+    def start(self):
+        pass
+
+    def wait(self):
+        while self.at < len(self.halves):
+            self.step()
+
+
 class Gather:
-    def __init__(self, spot, own, full, sems):
+    def __init__(self, spot, own, full, sems, keep=None):
         self.spot, self.own, self.full = spot, own, full
         self.local, self.send, self.recv, self.on_send, self.on_recv = sems
         spot_shard = spot.shard
-        self.keep = pltpu.make_async_copy(own, full.at[spot_shard], self.local)
+        self.keep = keep or pltpu.make_async_copy(own, full.at[spot_shard], self.local)
         self.far = [
             remote(own, full.at[spot_shard], self.send.at[d], self.recv.at[d], {"shard": spot.away(d)})
             for d in range(1, spot.chips)
@@ -128,12 +152,113 @@
             copy.wait_send()
 
 
+class Spread:
+    def __init__(self, spot, own, full, keep, sems):
+        self.spot, self.own, self.full, self.keep = spot, own, full, keep
+        (
+            self.far_send, self.far_recv, self.right_send, self.right_recv, self.left_send, self.left_recv,
+            self.mate_send, self.mate_recv,
+        ) = sems
+        self.part = full.shape[1] // spot.n
+        n, me = spot.n, spot.me
+        self.near = remote(
+            own, full.at[spot.shard], self.mate_send.at[0, 0], self.mate_recv.at[0, 0], {"shard": spot.mate}
+        )
+        mine = pl.ds(pl.multiple_of(me * self.part, self.part), self.part)
+        self.far = [
+            remote(
+                own.at[mine], full.at[spot.shard, mine], self.far_send.at[d], self.far_recv.at[d],
+                {"shard": spot.away(d)},
+            )
+            for d in range(1, spot.chips)
+        ]
+        self.can_right, self.can_left = me + 1 < n, me > 0
+
+    def piece(self, d, z):
+        source = lax.rem(self.spot.shard - 2 * d + self.spot.shards, self.spot.shards)
+        return self.full.at[source, pl.ds(pl.multiple_of(z * self.part, self.part), self.part)]
+
+    def tell(self, d, z):
+        at = self.piece(d, z)
+        return remote(at, at, self.mate_send.at[d, z], self.mate_recv.at[d, z], {"shard": self.spot.mate})
+
+    def right(self, d, h, z):
+        at, to = self.piece(d, z), {"ctx": lax.rem(self.spot.me + 1, self.spot.n)}
+        return remote(at, at, self.right_send.at[d, h], self.right_recv.at[d, h], to)
+
+    def left(self, d, h, z):
+        at, to = self.piece(d, z), {"ctx": lax.rem(self.spot.me - 1 + self.spot.n, self.spot.n)}
+        return remote(at, at, self.left_send.at[d, h], self.left_recv.at[d, h], to)
+
+    def pairs(self):
+        return range(1, self.spot.chips)
+
+    def start(self):
+        for copy in self.far:
+            copy.start()
+
+    def start_near(self):
+        self.keep.start()
+        self.near.start()
+
+    def send_on(self, d, h, z, right, left):
+        self.tell(d, z).start()
+        if right:
+            @pl.when(self.can_right)
+            def _():
+                self.right(d, h, z).start()
+
+        if left:
+            @pl.when(self.can_left)
+            def _():
+                self.left(d, h, z).start()
+
+    def arrived(self):
+        for d in self.pairs():
+            self.far[d - 1].wait_recv()
+            self.send_on(d, 1, self.spot.me, True, True)
+
+    def hop(self, h):
+        me, n = self.spot.me, self.spot.n
+        for d in self.pairs():
+            @pl.when(me - h >= 0)
+            def _():
+                self.right(d, h, me - h).wait_recv()
+                self.send_on(d, h + 1, me - h, h + 1 < n, False)
+
+            @pl.when(me + h < n)
+            def _():
+                self.left(d, h, me + h).wait_recv()
+                self.send_on(d, h + 1, me + h, False, h + 1 < n)
+
+    def wait(self):
+        me, n = self.spot.me, self.spot.n
+        self.keep.wait()
+        self.near.wait_recv()
+        self.near.wait_send()
+        for d in self.pairs():
+            self.far[d - 1].wait_send()
+            for z in range(n):
+                self.tell(d, z).wait_recv()
+                self.tell(d, z).wait_send()
+            for h in range(1, n):
+                @pl.when((me - h + 1 >= 0) & self.can_right)
+                def _():
+                    self.right(d, h, me - h + 1).wait_send()
+
+                @pl.when((me + h - 1 < n) & self.can_left)
+                def _():
+                    self.left(d, h, me + h - 1).wait_send()
+
+
 def forward_kernel(
-    dims, tokens, gains, table, wq, wk, wv, wo, wi0, wi1, wff,
-    normed, hidden, normed_two, attended, lse, pieces_out, full_q, full_k, full_v, full_o, full_0, full_1, full_2,
-    weights, acc, bias, staged, pieces, mixed, heads_in, branch, branch_in,
+    dims, tokens, cotangent, gains, table, wq, wk, wv, wo, wi0, wi1, wff,
+    hidden, normed_two, attended, lse, pieces_out, left_g, left_one, left_two,
+    full_q, full_k, full_v, full_o, full_0, full_1, full_2,
+    normed, flipped, weights, acc, bias, staged, pieces, mixed, heads_in, rolled, branch_in,
     local_sem, far_send, far_recv, near_send, near_recv, head_send, head_recv, back_send, back_recv,
-    swap_send, swap_recv, out_sem,
+    room, keep_sem,
+    swap_send, swap_recv, out_sem, *spread_sems,
 ):
     spot = Spot(*dims.mesh)
     n, seqs, part, cols, head_dim = dims.n, dims.seqs, dims.part, dims.cols, dims.head_dim
@@ -144,14 +269,29 @@
     per = 2
     spot.barrier()
 
-    def gather(i, own, full):
+    def gather(i, own, full, keep=None):
         sems = [local_sem.at[i], far_send.at[i], far_recv.at[i], near_send.at[i], near_recv.at[i]]
-        return Gather(spot, own, full, sems)
+        return Gather(spot, own, full, sems, keep)
 
     loads = [gather(i, w, weights.at[i]) for i, w in enumerate((wq, wk, wv, wo))]
-    loads += [gather(4 + i, w, f) for i, (w, f) in enumerate(((wi0, full_0), (wi1, full_1), (wff, full_2)))]
-    for load in loads[:3]:
-        load.start_far()
+    keep = Keep(
+        [(w, full.at[spot.shard]) for w, full in ((wi0, full_0), (wi1, full_1), (wff, full_2))], room, keep_sem
+    )
+    loads.append(gather(4, wi0, full_0, keep))
+    spreads = [
+        Spread(spot, own, full, keep, [sem.at[i] for sem in spread_sems])
+        for i, (own, full) in enumerate(((wi1, full_1), (wff, full_2)))
+    ]
+    flips = []
+
+    def flip(value, out):
+        if flips:
+            flips[-1].wait()
+        flipped[...] = value.T
+        flips.append(pltpu.make_async_copy(flipped, out, out_sem.at[5]))
+        flips[-1].start()
+
+    loads[0].start_far()
     for load in loads[:3]:
         load.start_near()
 
@@ -162,7 +302,8 @@
         normed[at, :] = (values * rms_scale(values) * gains[0:1, :]).astype(BF16)
 
     for head in range(dims.own_heads):
-        bias_rows(table[head : head + 1, :], bias.at[head])
+        bias_rows(table[head : head + 1, :], rolled)
+        bias[head] = rolled[...].astype(BF16)
 
     def term(i, shard):
         at = pl.ds(pl.multiple_of(shard * shard_rows, 128), shard_rows)
@@ -173,12 +314,16 @@
         load.wait_own()
         acc[...] = term(i, spot.shard)
         acc[...] += term(i, spot.mate)
+        keep.step()
         load.pass_on()
-        if i == 2:
-            for later in loads[3:]:
-                later.start_far()
-            for later in loads[3:]:
+        if i < 2:
+            loads[i + 1].start_far()
+        else:
+            for spread in spreads:
+                spread.start()
+            for later in loads[3:] + spreads:
                 later.start_near()
+        keep.step()
         for d in range(1, spot.chips):
             acc[...] += term(i, lax.rem(spot.shard - 2 * d + shards, shards))
         load.wait_near()
@@ -201,10 +346,14 @@
     ]
     for copy in outs[:3]:
         copy.start()
+    flip(normed[...], left_one)
+    spreads[0].arrived()
+    spreads[1].arrived()
+    loads[3].start_far()
+    flip(cotangent[...], left_g)
     for move in moves:
         move.wait_recv()
     loads[3].wait_own()
-    loads[3].pass_on()
     outs.append(pltpu.make_async_copy(pieces, pieces_out, out_sem.at[4]))
     outs[4].start()
 
@@ -226,7 +375,7 @@
                 scores = jnp.concatenate(
                     [
                         contract_cols(query, pieces[1, b, s, :, span])
-                        + bias[head, :, pl.ds(pl.multiple_of((n + b - a) * part, part), part)]
+                        + bias[head, :, pl.ds(pl.multiple_of((n + b - a) * part, part), part)].astype(F32)
                         for b in range(n)
                     ],
                     axis=1,
@@ -251,11 +400,26 @@
         def _():
             heads_in[a, s] = mixed[s, a]
 
+        @pl.when(step == 2)
+        def _():
+            spreads[0].hop(1)
+
+        @pl.when(step == 4)
+        def _():
+            loads[3].pass_on()
+            loads[4].start_far()
+
+        @pl.when(step == 5)
+        def _():
+            spreads[1].hop(1)
+
+    if n > 2:
+        spreads[0].hop(2)
     loads[3].wait_near()
     outs[3].start()
     swaps = []
     for s in range(seqs):
-        at = slice(s * part, (s + 1) * part)
+        at = pl.ds(s * part, part)
         for d in range(1, n):
             peer = lax.rem(me + d, n)
             remote(
@@ -264,12 +428,17 @@
         for k in range(n):
             attended[at, k * cols : (k + 1) * cols] = heads_in[k, s]
         for j in range(shards):
-            branch[s, :, j * shard_rows : (j + 1) * shard_rows] = contract_cols(
+            normed[at, j * shard_rows : (j + 1) * shard_rows] = contract_cols(
                 attended[at, :], weights[3, j]
             ).astype(BF16)
-        swap = remote(branch.at[s], branch_in.at[s], swap_send.at[s], swap_recv.at[s], {"tp": 1 - spot.half})
+        swap = remote(normed.at[at], branch_in.at[s], swap_send.at[s], swap_recv.at[s], {"tp": 1 - spot.half})
         swap.start()
         swaps.append(swap)
+    if n > 2:
+        spreads[1].hop(2)
+    for h in range(3, n):
+        for spread in spreads:
+            spread.hop(h)
     loads[4].wait_own()
     loads[4].pass_on()
     for s in range(seqs):
@@ -280,16 +449,15 @@
             here = pl.ds(pl.multiple_of(i * 64, 64), 64)
             at = pl.ds(pl.multiple_of(s * part + i * 64, 64), 64)
             values = tokens[at, :].astype(F32) + (
-                branch[s, here, :].astype(F32) + branch_in[s, here, :].astype(F32)
+                normed[at, :].astype(F32) + branch_in[s, here, :].astype(F32)
             )
             hidden[at, :] = values
             normed_two[at, :] = (values * rms_scale(values) * gains[1:2, :]).astype(BF16)
 
-    for load in loads[5:]:
-        load.wait_own()
-        load.pass_on()
-    for load in loads[4:]:
-        load.wait_near()
+    flip(normed_two[...], left_two)
+    loads[4].wait_near()
+    for spread in spreads:
+        spread.wait()
     for load in loads:
         load.wait_sent()
     for move in moves + swaps:
@@ -298,7 +466,7 @@
         for d in range(1, n):
             peer = lax.rem(me + d, n)
             back(s, peer, peer).wait_send()
-    for copy in outs:
+    for copy in outs + flips[-1:]:
         copy.wait()
 
 
@@ -323,27 +491,29 @@
     block = (seqs, part, dims.cols)
     return pl.pallas_call(
         functools.partial(forward_kernel, dims),
-        in_specs=[vmem] * 3 + [anywhere] * 7,
-        out_specs=[vmem] * 5 + [anywhere] * 8,
+        in_specs=[vmem] * 4 + [anywhere] * 7,
+        out_specs=[vmem] * 4 + [anywhere] * 11,
         out_shape=[
-            shape((rows, width), BF16),
             shape((rows, width), F32),
             shape((rows, width), BF16),
             shape((rows, inner), BF16),
             shape((seqs, n, part, lanes), F32),
             shape((3, n) + block, BF16),
         ]
+        + [shape((width, rows), BF16)] * 3
         + [shape((shards, shard_rows, inner), BF16)] * 4
         + [shape((shards, shard_rows, units), BF16)] * 3,
         scratch_shapes=[
+            pltpu.VMEM((rows, width), BF16),
+            pltpu.VMEM((width, rows), BF16),
             pltpu.VMEM((4, shards, shard_rows, inner), BF16),
             pltpu.VMEM((rows, inner), F32),
-            pltpu.VMEM((dims.own_heads, part, span), F32),
+            pltpu.VMEM((dims.own_heads, part, span), BF16),
             pltpu.VMEM((3, n) + block, BF16),
             pltpu.VMEM((3, n) + block, BF16),
             pltpu.VMEM((seqs, n, part, dims.cols), BF16),
             pltpu.VMEM((n,) + block, BF16),
-            pltpu.VMEM((seqs, part, width), BF16),
+            pltpu.VMEM((part, span), F32),
             pltpu.VMEM((seqs, part, width), BF16),
             dma((7,)),
             dma((7, chips)),
@@ -354,10 +524,14 @@
             dma((3, n)),
             dma((seqs, n)),
             dma((seqs, n)),
+            pltpu.VMEM((shard_rows, units), BF16),
+            dma((2,)),
             dma((seqs,)),
             dma((seqs,)),
-            dma((5,)),
-        ],
+            dma((6,)),
+        ]
+        + [dma((2, chips))] * 2
+        + [dma((2, chips, n))] * 6,
         compiler_params=pltpu.CompilerParams(
             vmem_limit_bytes=60 * 2**20, collective_id=0, has_side_effects=True
         ),
@@ -372,7 +546,8 @@
 class Pump:
     def __init__(self, dims, spot, left, right, sources, from_heads, outs, buffers, sems, credits):
         self.dims, self.spot, self.left, self.right = dims, spot, left, right
-        self.sources, self.from_heads, self.outs = sources, from_heads, outs
+        self.fed, self.attended = sources
+        self.from_heads, self.outs = from_heads, outs
         self.core_out, self.core_in, self.far_out, self.far_in, self.line, self.line_in, self.across_in, self.done = buffers
         (
             self.right_sem, self.core_send, self.core_recv, self.far_send, self.far_recv, self.in_send, self.in_recv,
@@ -405,19 +580,20 @@
 
     def far(self, k, d):
         return remote(
-            self.far_out.at[k, d - 1], self.far_in.at[k, d - 1], self.far_send.at[k, d - 1],
+            self.far_out.at[lax.rem(k, 2), d - 1], self.far_in.at[k, d - 1], self.far_send.at[k, d - 1],
             self.far_recv.at[k, d - 1], {"shard": self.spot.away(d)},
         )
 
     def inward(self, k):
+        half = k
         return remote(
-            self.line.at[k], self.line_in.at[k], self.in_send.at[k], self.in_recv.at[k], {"ctx": self.inner}
+            self.line.at[k], self.line_in.at[half], self.in_send.at[k], self.in_recv.at[half], {"ctx": self.inner}
         )
 
     def across(self, k):
         return remote(
-            self.line.at[k], self.across_in.at[k], self.across_send.at[k], self.across_recv.at[k],
-            {"ctx": self.facing},
+            self.line.at[k], self.across_in.at[k], self.across_send.at[k],
+            self.across_recv.at[k], {"ctx": self.facing},
         )
 
     def outward(self, k):
@@ -425,29 +601,34 @@
             self.done.at[k], self.done.at[k], self.out_send.at[k], self.out_recv.at[k], {"ctx": self.outer}
         )
 
-    def spend(self, c, credit):
-        @pl.when(c >= SLOTS)
+    def spend(self, c, credit, slots=SLOTS):
+        @pl.when(c >= slots)
         def _():
             pl.semaphore_wait(credit, 1)
 
-    def give(self, c, credit, peer):
-        @pl.when(c + SLOTS < self.total)
+    def give(self, c, credit, peer, slots=SLOTS):
+        @pl.when(c + slots < self.total)
         def _():
             pl.semaphore_signal(credit, inc=1, device_id=peer, device_id_type=MESH)
 
     def term(self, c, shard, k):
         one = lambda b: jnp.where(c >= b, 1, 0)
-        which = one(self.units) + one(3 * self.units) + one(self.early)
+        which = one(self.units) + one(3 * self.units) - 2 * one(self.early)
         rows = self.dims.shard_rows
         return dot(self.left[which, pl.ds(pl.multiple_of(shard * rows, rows), rows), :], self.right[k])
 
     def fetch(self, c):
-        k = lax.rem(c, SLOTS)
-        for (base, count), source in zip(self.bases, self.sources):
-            @pl.when((c >= base) & (c < base + count))
-            def _():
-                at = pl.ds(pl.multiple_of((c - base) * CHUNK, CHUNK), CHUNK)
-                pltpu.make_async_copy(source.at[:, at], self.right.at[k], self.right_sem.at[k]).start()
+        k, fed = lax.rem(c, SLOTS), 3 * self.units
+
+        @pl.when(c < fed)
+        def _():
+            source = self.fed.at[c // self.units, lax.rem(c, self.units)]
+            pltpu.make_async_copy(source, self.right.at[k], self.right_sem.at[k]).start()
+
+        @pl.when((c >= fed) & (c < self.early))
+        def _():
+            at = pl.ds(pl.multiple_of((c - fed) * CHUNK, CHUNK), CHUNK)
+            pltpu.make_async_copy(self.attended.at[:, at], self.right.at[k], self.right_sem.at[k]).start()
 
         @pl.when((c >= self.early) & (c < self.total))
         def _():
@@ -546,16 +727,14 @@
         self.core(c, k).wait_send()
         for d in range(1, self.spot.chips):
             pair = self.term(c, self.spot.away(d), k) + self.core_in[k, d - 1].astype(F32)
-            self.far_out[k, d - 1] = pair.astype(BF16)
+            self.far_out[lax.rem(k, 2), d - 1] = pair.astype(BF16)
             self.spend(c, self.far_credit.at[d - 1])
             self.far(k, d).start()
 
     def to_core(self, c, k):
         @pl.when(c < self.early)
         def _():
-            pltpu.make_async_copy(
-                self.sources[0].at[:, pl.ds(0, CHUNK)], self.right.at[k], self.right_sem.at[k]
-            ).wait()
+            pltpu.make_async_copy(self.fed.at[0, 0], self.right.at[k], self.right_sem.at[k]).wait()
 
         chips, half = self.spot.chips, lax.rem(c, 2)
         for d in range(1, chips + 1):
@@ -572,16 +751,16 @@
             def _():
                 stage(c, lax.rem(c, SLOTS))
 
+        @pl.when(t < self.total)
+        def _():
+            self.fetch(t)
+
         at(10, self.settle)
         at(9, self.deliver)
         at(7, self.finish)
         at(5, self.collect)
         at(3, self.own)
 
-        @pl.when(t + 1 < self.total)
-        def _():
-            self.fetch(t + 1)
-
         at(1, self.to_chips)
         at(0, self.to_core)
 
@@ -591,14 +770,27 @@
             self.step(t)
 
 
+UNITS = 256
+
+
+def geglu_both(gate, up, upstream):
+    root, cube = 0.7978845608028654, 0.044715
+    square = gate * gate
+    bent = jnp.tanh(root * gate * (1.0 + cube * square))
+    half = 0.5 * (1.0 + bent)
+    gelu = gate * half
+    slope = half + 0.5 * gate * (1.0 - bent * bent) * (root * (1.0 + 3.0 * cube * square))
+    return gelu * up, upstream * up * slope, upstream * gelu
+
+
 def backward_kernel(
-    dims, gain_two, table, lse, pieces,
-    term, ffn_term, left_g, left_two, left_one, inner, grad_gate, grad_up, attended, hidden, cotangent,
-    wo, wq, wk, wv,
+    dims, gain_two, table,
+    lse_from, pieces_from, left_g, left_two, left_one, normed_two, attended, hidden, cotangent,
+    wo, wq, wk, wv, wi0, wi1, wff,
     down_out, gate_out, up_out, o_out, q_out, k_out, v_out,
-    grad_hidden, ffn_other, term_one, other_one, ffn_gain, table_out,
+    grad_hidden, ffn_term, ffn_other, term_one, other_one, ffn_gain, table_out,
     left, right, core_out, core_in, far_out, far_in, line, line_in, across_in, done,
-    swap_in, staged, grads, grads_out, grads_in,
+    fed, term, swap_in, grads, grads_out, grads_in,
     right_sem, core_send, core_recv, far_send, far_recv, in_send, in_recv, across_send, across_recv,
     out_send, out_recv, fin_sem, swap_send, swap_recv, head_send, head_recv, back_send, back_recv,
     one_send, one_recv, ffn_sem, local_sem,
@@ -606,13 +798,14 @@
 ):
     spot = Spot(*dims.mesh)
     n, seqs, part, cols, head_dim, width = dims.n, dims.seqs, dims.part, dims.cols, dims.head_dim, dims.width
-    me, shards, shard_rows = spot.me, spot.shards, dims.shard_rows
+    me, shards, shard_rows, units = spot.me, spot.shards, dims.shard_rows, dims.units
+    rows = seqs * part
     lanes, per = 2 * head_dim, 2
     groups = cols // lanes
     span = table.shape[1]
     other_half = {"tp": 1 - spot.half}
     pump = Pump(
-        dims, spot, left, right, (inner, grad_gate, grad_up, attended), grads_in,
+        dims, spot, left, right, (fed, attended), grads_in,
         (down_out, gate_out, up_out, o_out, q_out, k_out, v_out),
         (core_out, core_in, far_out, far_in, line, line_in, across_in, done),
         (
@@ -621,41 +814,151 @@
         ),
         (core_credit, far_credit, in_credit, across_credit, out_credit),
     )
-    loads = [
+    lefts = [
         pltpu.make_async_copy(source, left.at[i], local_sem.at[i])
-        for i, source in ((0, left_g), (1, left_two), (3, left_one))
+        for i, source in ((0, left_g), (1, left_two), (0, left_one))
     ]
-    for load in loads:
-        load.start()
-    pump.fetch(0)
     spot.barrier()
+    ffn_gain[...] = jnp.zeros_like(ffn_gain)
+    table_out[...] = jnp.zeros_like(table_out)
+
+    def feed(weights, values, given, sem, value_sem):
+        inputs = [
+            pltpu.make_async_copy(normed_two, values, value_sem.at[0]),
+            pltpu.make_async_copy(cotangent, given, value_sem.at[1]),
+        ]
+
+        def load(u):
+            slot = lax.rem(u, 2)
+            at = pl.ds(pl.multiple_of(u * UNITS, UNITS), UNITS)
+            return [
+                pltpu.make_async_copy(w.at[:, :, at], weights.at[slot, j], sem.at[slot, j])
+                for j, w in enumerate((wi0, wi1, wff))
+            ]
+
+        for copy in load(0) + inputs + lefts[:2]:
+            copy.start()
+        for copy in inputs:
+            copy.wait()
+        each = CHUNK // UNITS
+
+        @pl.loop(0, units // CHUNK)
+        def _(c):
+            for i in range(each):
+                u = c * each + i
+
+                @pl.when(u + 1 < units // UNITS)
+                def _():
+                    for copy in load(u + 1):
+                        copy.start()
+
+                for copy in load(u):
+                    copy.wait()
+                slot = lax.rem(u, 2)
+                gate = dot(values[...], weights[slot, 0].reshape(width, UNITS))
+                up = dot(values[...], weights[slot, 1].reshape(width, UNITS))
+                upstream = dot(given[...], weights[slot, 2].reshape(width, UNITS))
+                for j, made in enumerate(geglu_both(gate, up, upstream)):
+                    fed[j, c, :, i * UNITS : (i + 1) * UNITS] = made.astype(BF16)
+
+            @pl.when(c == 0)
+            def _():
+                for copy in lefts[:2]:
+                    copy.wait()
+
+            pump.step(c)
+
+    pl.run_scoped(
+        feed,
+        pltpu.VMEM((2, 3, shards, shard_rows, UNITS), BF16),
+        pltpu.VMEM((rows, width), BF16),
+        pltpu.VMEM((rows, width), BF16),
+        pltpu.SemaphoreType.DMA((2, 3)),
+        pltpu.SemaphoreType.DMA((2,)),
+    )
+    fed_steps = units // CHUNK
+
+    def feed_terms(weights, block, sem, block_sem):
+        def load(j, w, slot):
+            return pltpu.make_async_copy(w.at[j], weights.at[slot], sem.at[slot])
+
+        def product(slot, which):
+            total = None
+            for c in range(units // CHUNK):
+                at = slice(c * CHUNK, (c + 1) * CHUNK)
+                made = contract_cols(fed[which, c], weights[slot, :, at])
+                total = made if total is None else total + made
+            return total
+
+        def columns(j):
+            return pl.ds(pl.multiple_of(j * shard_rows, shard_rows), shard_rows)
+
+        load(0, wi0, 0).start()
+        load(0, wi1, 1).start()
+
+        @pl.loop(0, shards)
+        def _(j):
+            total = None
+            for slot, w in enumerate((wi0, wi1)):
+                load(j, w, slot).wait()
+                made = product(slot, 1 + slot)
+                total = made if total is None else total + made
+
+                @pl.when(j + 1 < shards)
+                def _():
+                    load(j + 1, w, slot).start()
+
+            for s in range(seqs):
+                term[s, :, columns(j)] = total[s * part : (s + 1) * part].astype(BF16)
+
+        for swap in swaps:
+            swap.start()
+        load(0, wff, 0).start()
+        pump.steps(fed_steps, fed_steps + 1)
+
+        @pl.loop(0, shards)
+        def _(j):
+            slot = lax.rem(j, 2)
+
+            @pl.when(j + 1 < shards)
+            def _():
+                load(j + 1, wff, 1 - slot).start()
+
+            load(j, wff, slot).wait()
+            block[...] = product(slot, 0).astype(BF16)
+            copy = pltpu.make_async_copy(block, ffn_term.at[:, columns(j)], block_sem.at[0])
+            copy.start()
+            copy.wait()
+
+        pump.steps(fed_steps + 1, fed_steps + 2)
+
     swaps = [
         remote(term.at[s], swap_in.at[s], swap_send.at[s], swap_recv.at[s], other_half) for s in range(seqs)
     ]
-    for swap in swaps:
-        swap.start()
-    for load in loads:
-        load.wait()
-    ffn_gain[...] = jnp.zeros_like(ffn_gain)
-    table_out[...] = jnp.zeros_like(table_out)
-    pump.steps(0, 4)
+    pl.run_scoped(
+        feed_terms,
+        pltpu.VMEM((2, shard_rows, units), BF16),
+        pltpu.VMEM((rows, shard_rows), BF16),
+        pltpu.SemaphoreType.DMA((2,)),
+        pltpu.SemaphoreType.DMA((1,)),
+    )
+    so_far = fed_steps + 2
 
     def head_move(s, peer):
         return remote(
-            staged.at[peer, s], grads.at[me, s], head_send.at[s, peer], head_recv.at[s, me], {"ctx": peer}
+            grads_out.at[0, peer, s], grads.at[me, s], head_send.at[s, peer], head_recv.at[s, me], {"ctx": peer}
         )
 
     def head_wait(s, peer):
         remote(
-            staged.at[peer, s], grads.at[peer, s], head_send.at[s, peer], head_recv.at[s, peer], {"ctx": peer}
+            grads_out.at[0, peer, s], grads.at[peer, s], head_send.at[s, peer], head_recv.at[s, peer], {"ctx": peer}
         ).wait_recv()
 
-    def second_norm(s, weights, values, given, own, result, sem):
+    def second_norm(s, weights, values, given, own, sem):
         at = pl.ds(s * part, part)
         copies = [
             pltpu.make_async_copy(hidden.at[at, :], values, sem.at[0]),
             pltpu.make_async_copy(cotangent.at[at, :], given, sem.at[1]),
-            pltpu.make_async_copy(term.at[s], own, sem.at[2]),
         ]
         for copy in copies:
             copy.start()
@@ -667,34 +970,34 @@
         def _(i):
             here = pl.ds(pl.multiple_of(i * 64, 64), 64)
             h = values[here, :]
-            grad = own[here, :].astype(F32) + swap_in[s, here, :].astype(F32)
+            grad = term[s, here, :].astype(F32) + swap_in[s, here, :].astype(F32)
             scale = rms_scale(h)
             ffn_gain[...] += jnp.sum(grad * h * scale, axis=0, keepdims=True)
             total = given[here, :].astype(F32) + rms_back(h, scale, gain_two[...], grad)
-            result[here, :] = total
+            values[here, :] = total
             own[here, :] = total.astype(BF16)
 
-        saved = pltpu.make_async_copy(result, grad_hidden.at[at, :], sem.at[0])
+        saved = pltpu.make_async_copy(values, grad_hidden.at[at, :], sem.at[0])
         saved.start()
         total = dot(own[:, :shard_rows], weights[0])
         for j in range(1, shards):
             total += dot(own[:, j * shard_rows : (j + 1) * shard_rows], weights[j])
         for k in range(n):
-            staged[k, s] = total[:, k * cols : (k + 1) * cols].astype(BF16)
+            grads_out[0, k, s] = total[:, k * cols : (k + 1) * cols].astype(BF16)
         for d in range(1, n):
             head_move(s, lax.rem(me + d, n)).start()
-        grads[me, s] = staged[me, s]
+        grads[me, s] = grads_out[0, me, s]
         left[2, :, s * part : (s + 1) * part] = own[...].T
         saved.wait()
 
-    def second_norms(weights, values, given, own, result, sem):
+    def second_norms(weights, values, given, own, sem):
         load = pltpu.make_async_copy(wo, weights, sem.at[3])
         load.start()
         load.wait()
         for s in range(seqs):
-            second_norm(s, weights, values, given, own, result, sem)
+            second_norm(s, weights, values, given, own, sem)
             if s == 0:
-                pump.steps(4, 5)
+                pump.steps(so_far, so_far + 1)
 
     pl.run_scoped(
         second_norms,
@@ -702,12 +1005,12 @@
         pltpu.VMEM((part, width), F32),
         pltpu.VMEM((part, width), BF16),
         pltpu.VMEM((part, width), BF16),
-        pltpu.VMEM((part, width), F32),
         pltpu.SemaphoreType.DMA((4,)),
     )
     ffn_swap = remote(ffn_term, ffn_other, ffn_sem.at[0], ffn_sem.at[1], other_half)
     ffn_swap.start()
-    pump.steps(5, 7)
+    pump.steps(so_far + 1, so_far + 2)
+    so_far += 2
 
     def back_move(j, s, peer):
         return remote(
@@ -721,7 +1024,7 @@
             {"ctx": peer},
         ).wait_recv()
 
-    def attention(bias, sums, grad_k, grad_v):
+    def attention(pieces, lse, bias, sums, grad_k, grad_v, sem):
         @pl.loop(0, seqs * groups * n)
         def _(i):
             a, group, s = lax.rem(i, n), lax.rem(i // n, groups), i // (n * groups)
@@ -729,13 +1032,23 @@
 
             @pl.when((a == 0) & (group == 0))
             def _():
+                here = [
+                    pltpu.make_async_copy(pieces_from.at[:, :, s], pieces, sem.at[0]),
+                    pltpu.make_async_copy(lse_from.at[s], lse, sem.at[1]),
+                ]
+                for copy in here:
+                    copy.start()
+                for copy in here:
+                    copy.wait()
                 for d in range(1, n):
                     head_wait(s, lax.rem(me + d, n))
+                    head_move(s, lax.rem(me + d, n)).wait_send()
 
             @pl.when(a == 0)
             def _():
                 for j in range(per):
-                    bias_rows(table[pl.ds(group * per + j, 1), :], bias.at[j])
+                    bias_rows(table[pl.ds(group * per + j, 1), :], sums.at[j])
+                bias[...] = sums[...].astype(BF16)
                 sums[...] = jnp.zeros_like(sums)
                 grad_k[...] = jnp.zeros_like(grad_k)
                 grad_v[...] = jnp.zeros_like(grad_v)
@@ -744,21 +1057,21 @@
             result = jnp.zeros((part, lanes), F32)
             for j in range(per):
                 mask = (lane >= j * head_dim) & (lane < (j + 1) * head_dim)
-                query = jnp.where(mask, pieces[0, a, s, :, at], 0)
+                query = jnp.where(mask, pieces[0, a, :, at], 0)
                 upstream = jnp.where(mask, grads[a, s, :, at], 0)
-                log_total = jnp.sum(jnp.where(lane == group * per + j, lse[s, a], 0.0), axis=1, keepdims=True)
+                log_total = jnp.sum(jnp.where(lane == group * per + j, lse[a], 0.0), axis=1, keepdims=True)
                 windows = [pl.ds(pl.multiple_of((n + b - a) * part, part), part) for b in range(n)]
                 probs, grad_probs = [], []
                 for b in range(n):
-                    scores = contract_cols(query, pieces[1, b, s, :, at]) + bias[j, :, windows[b]]
+                    scores = contract_cols(query, pieces[1, b, :, at]) + bias[j, :, windows[b]].astype(F32)
                     probs.append(jnp.exp(scores - log_total))
-                    grad_probs.append(contract_cols(upstream, pieces[2, b, s, :, at]))
+                    grad_probs.append(contract_cols(upstream, pieces[2, b, :, at]))
                 delta = sum(jnp.sum(g * p, axis=1, keepdims=True) for g, p in zip(grad_probs, probs))
                 summed = None
                 for b in range(n):
                     grad_scores = (probs[b] * (grad_probs[b] - delta)).astype(BF16)
                     sums[j, :, windows[b]] += grad_scores.astype(F32)
-                    product = dot(grad_scores, pieces[1, b, s, :, at])
+                    product = dot(grad_scores, pieces[1, b, :, at])
                     summed = product if summed is None else summed + product
                     grad_k[b] += contract_rows(grad_scores, query)
                     grad_v[b] += contract_rows(probs[b].astype(BF16), upstream)
@@ -782,17 +1095,23 @@
 
             @pl.when(a == n - 1)
             def _():
-                pump.step(7 + i // n)
+                pump.step(so_far + i // n)
 
     pl.run_scoped(
         attention,
-        pltpu.VMEM((per, part, span), F32),
+        pltpu.VMEM((3, n, part, cols), BF16),
+        pltpu.VMEM((n, part, lanes), F32),
+        pltpu.VMEM((per, part, span), BF16),
         pltpu.VMEM((per, part, span), F32),
         pltpu.VMEM((n, part, lanes), F32),
         pltpu.VMEM((n, part, lanes), F32),
-    )
-    after = 7 + seqs * groups
-    pump.steps(after, after + 1)
+        pltpu.SemaphoreType.DMA((2,)),
+    )
+    so_far += seqs * groups
+    lefts[2].start()
+    lefts[2].wait()
+    pump.steps(so_far, so_far + 3)
+    so_far += 3
     for s in range(seqs):
         for j in range(3):
             for d in range(1, n):
@@ -836,7 +1155,7 @@
     ]
     for swap in ones:
         swap.start()
-    pump.steps(after + 1, pump.last)
+    pump.steps(so_far, pump.last)
     for swap in swaps:
         swap.wait_send()
     for copy in ones + [ffn_swap]:
@@ -845,7 +1164,6 @@
     for s in range(seqs):
         for d in range(1, n):
             peer = lax.rem(me + d, n)
-            head_move(s, peer).wait_send()
             for j in range(3):
                 back_move(j, s, peer).wait_send()
 
@@ -860,12 +1178,13 @@
     block = (shard_rows, CHUNK)
     return pl.pallas_call(
         functools.partial(backward_kernel, dims),
-        in_specs=[vmem] * 4 + [anywhere] * 15,
-        out_specs=[anywhere] * 9 + [vmem, anywhere, vmem, vmem],
+        in_specs=[vmem] * 2 + [anywhere] * 16,
+        out_specs=[anywhere] * 10 + [vmem, anywhere, vmem, vmem],
         out_shape=[shape((shard_rows, units), BF16)] * 3
         + [shape((shard_rows, inner), BF16)] * 4
         + [
             shape((rows, width), F32),
+            shape((rows, width), BF16),
             shape((rows, width), BF16),
             shape((seqs, part, width), BF16),
             shape((seqs, part, width), BF16),
@@ -873,18 +1192,19 @@
             shape((dims.own_heads, span), F32),
         ],
         scratch_shapes=[
-            pltpu.VMEM((4, width, rows), BF16),
+            pltpu.VMEM((3, width, rows), BF16),
             pltpu.VMEM((SLOTS, rows, CHUNK), BF16),
             pltpu.VMEM((2, chips) + block, BF16),
             pltpu.VMEM((SLOTS, chips) + block, BF16),
-            pltpu.VMEM((SLOTS, far) + block, BF16),
+            pltpu.VMEM((2, far) + block, BF16),
             pltpu.VMEM((SLOTS, far) + block, BF16),
             pltpu.VMEM((SLOTS,) + block, BF16),
             pltpu.VMEM((SLOTS,) + block, BF16),
             pltpu.VMEM((SLOTS,) + block, BF16),
             pltpu.VMEM((SLOTS,) + block, BF16),
+            pltpu.VMEM((3, units // CHUNK, rows, CHUNK), BF16),
             pltpu.VMEM((seqs, part, width), BF16),
-            pltpu.VMEM((n, seqs, part, cols), BF16),
+            pltpu.VMEM((seqs, part, width), BF16),
             pltpu.VMEM((n, seqs, part, cols), BF16),
             pltpu.VMEM((3, n, seqs, part, cols), BF16),
             pltpu.VMEM((3, n, seqs, part, cols), BF16),
@@ -1033,33 +1353,20 @@
     offset_bias = offset_bias.reshape(groups, 2, 2 * reach)
 
     dims = Dims(links, seqs, part, width, inner_width, gate_weight.shape[1], heads)
-    normed, hidden, normed_two, attended, lse, pieces, *full = forward_call(dims)(
-        tokens.reshape(rows, width),
-        jnp.stack([gain_one, gain_two]),
-        offset_bias.reshape(own_heads, 2 * reach),
+    token_rows, upstream = tokens.reshape(rows, width), cotangent.reshape(rows, width)
+    bias_table = offset_bias.reshape(own_heads, 2 * reach)
+    hidden, normed_two, attended, lse, pieces, *lefts_and_weights = forward_call(dims)(
+        token_rows, upstream, jnp.stack([gain_one, gain_two]), bias_table,
         query_weight, key_weight, value_weight, output_weight, gate_weight, up_weight, down_weight,
     )
-    wi0, wi1, wff = (w.reshape(width, w.shape[2]) for w in full[4:])
-    inputs = tokens.reshape(rows, width).astype(F32)
+    left_g, left_one, left_two, wq, wk, wv, wo, wi0, wi1, wff = lefts_and_weights
+    *weight_grads, grad_hidden, ffn_term, ffn_other, term_one, other_one, grad_ffn_gain, offset_grad = backward_call(dims)(
+        gain_two.reshape(1, width), bias_table,
+        lse, pieces, left_g, left_two, left_one, normed_two, attended, hidden, upstream,
+        wo, wq, wk, wv, wi0, wi1, wff,
+    )
+    inputs = token_rows.astype(F32)
     scale_one = rms_scale(inputs)
-
-    gate = dot(normed_two, wi0)
-    up = dot(normed_two, wi1)
-    inner = geglu(gate, up).astype(BF16)
-    ffn_term = contract_cols(inner, wff).astype(BF16)
-    upstream_low = cotangent.reshape(rows, width)
-    grad_inner = dot(upstream_low, wff)
-    unused, geglu_backward_pull = jax.vjp(geglu, gate, up)
-    grad_gate, grad_up = geglu_backward_pull(grad_inner)
-    grad_gate = grad_gate.astype(BF16)
-    grad_up = grad_up.astype(BF16)
-    term_two = (contract_cols(grad_gate, wi0) + contract_cols(grad_up, wi1)).astype(BF16)
-    *weight_grads, grad_hidden, ffn_other, term_one, other_one, grad_ffn_gain, offset_grad = backward_call(dims)(
-        gain_two.reshape(1, width), offset_bias.reshape(own_heads, 2 * reach), lse, pieces,
-        term_two.reshape(seqs, part, width), ffn_term, upstream_low.T, normed_two.T, normed.T,
-        inner, grad_gate, grad_up, attended, hidden, upstream_low,
-        full[3], full[0], full[1], full[2],
-    )
     grad_down_w, grad_gate_w, grad_up_w, grad_output_w, grad_query_w, grad_key_w, grad_value_w = (
         g.astype(F32) for g in weight_grads
     )

time: 865 us -> 718 us (0.83)
  Pallas kernels: 734 us -> 661 us
  matrix products: 65.1 us -> 0.78 us
  local copies, waits for them, and re-layouts: 17 us -> 6.45 us
    pallas_call x1, Pallas kernels: 325 us -> 213 us  [per_device(): forward_call(dims)]
    dot_general x6 -> x0, matrix products: 64.4 us -> none  [the longest x3 33.8 us: dot(): return jnp.dot(left, right, preferred_element_type=F32)]
    pallas_call x1, Pallas kernels: 409 us -> 448 us  [per_device(): backward_call(dims)]
where the time goes in v4:
time: 718 us; the launch traced here: 708 us
  Pallas kernels  661 us (92%)
  other arithmetic  31.4 us (4%)
    pallas_call x1, Pallas kernels, per_device(): backward_call(dims)  448 us
    pallas_call x1, Pallas kernels, per_device(): forward_call(dims)  213 us
    convert_element_type x7, other arithmetic, per_device(): g.astype(F32)  15.4 us
  transfers between devices with their start and end apart: 4, of which 2 were waited for; matrix products, arithmetic and copies ran while one was open for 3% of the time, Pallas kernels for 0%

profile of v4, /device:TPU:0, one launch (start us, length us, event | category | flops | bytes accessed | tf_op | source)
XLA Modules:
  0.0 708.1 jit_solution(1166244956600302316)
XLA Ops:
  0.7 0.7 constant_dynamic-slice_fusion
  1.4 1.1 dynamic-slice_reduce_fusion
  2.6 0.7 convert_element_type.49
  3.3 0.7 stack.15
  4.0 2.1 fusion
  6.1 1.3 constant_dynamic-slice_fusion.1
  8.8 0.8 fusion.7.table
  10.3 213.0 %forward.1 = (f32[512,2048]{1,0:T(8,128)}, bf16[512,2048]{1,0:T(8,128)(2,1)}, bf16[512,1024]{1,0:T(8,128)(2,1)}, f32[2,4,256,128]{3,2,1,0:T(8,128)}, bf16[3,4,2,...) custom-call(bf16[512,2048]{1,0:T(8,128)(2,1)} %bitcast.26, ...), custom_call_target="tpu_custom_call" | custom-call | tf_op jit(solution)/shard_map/forward/pallas_call | solution.py:1358
  223.2 448.5 %backward.1 = (bf16[512,2560]{1,0:T(8,128)(2,1)}, bf16[512,2560]{1,0:T(8,128)(2,1)}, bf16[512,2560]{1,0:T(8,128)(2,1)}, bf16[512,1024]{1,0:T(8,128)(2,1)}, bf16[...) custom-call(f32[1,2048]{1,0:T(1,128)} %bitcast.33, ...), custom_call_target="tpu_custom_call" | custom-call | tf_op jit(solution)/shard_map/backward/pallas_call | solution.py:1363
  671.7 0.9 select_reduce_fusion
  673.1 4.7 fusion.3
  677.9 1.2 collective-permute-done
  679.1 1.3 collective-permute-start.1
  680.3 2.5 collective-permute-done.1
  682.9 3.7 fusion.6
  686.6 1.8 collective-permute-start.3
  688.4 2.5 add_convert_fusion
  690.9 3.0 convert_element_type.61
  694.0 3.0 convert_element_type.62
  697.0 3.0 convert_element_type.63
  700.1 1.6 convert_element_type.57
  701.6 1.6 convert_element_type.58
  703.2 1.6 convert_element_type.59
  704.8 1.6 convert_element_type.60
  (60 shorter events, 4.1 us)
Async XLA Ops:
  0.6 8.2 %copy-start = (bf16[32,16]{0,1:T(8,128)(2,1)S(1)}, bf16[32,16]{0,1:T(8,128)(2,1)}, u32[]{:S(2)}) copy-start(bf16[32,16]{0,1:T(8,128)(2,1)} %param.25) | copy-start | bytes 3076
  4.0 219.2 %copy-start.14 = (f32[2048]{0:T(1024)}, f32[2048]{0:T(1024)S(1)}, u32[]{:S(2)}) copy-start(f32[2048]{0:T(1024)S(1)} %stack.15) | copy-start | bytes 24580
  673.1 4.7 copy-start.15
  673.1 9.8 %copy-start.2 = (bf16[2,256,2048]{2,1,0:T(8,128)(2,1)S(1)}, bf16[2,256,2048]{2,1,0:T(8,128)(2,1)}, u32[]{:S(2)}) copy-start(bf16[2,256,2048]{2,1,0:T(8,128)(2,1)} %param.13) | copy-start | bytes 6291460
  673.1 9.8 %copy-start.4 = (f32[512,2048]{1,0:T(8,128)S(1)}, f32[512,2048]{1,0:T(8,128)}, u32[]{:S(2)}) copy-start(f32[512,2048]{1,0:T(8,128)} %get-tuple-element.58) | copy-start | bytes 12582916
  677.8 1.3 collective-permute-start
  679.1 3.8 collective-permute-start.1
  682.8 3.8 collective-permute-start.2
  682.9 5.6 copy-start.3
  682.9 5.6 copy-start.8
  682.9 5.6 copy-start.9
  686.6 19.7 %collective-permute-start.3 = (f32[4608]{0:T(1024)S(1)}, f32[4608]{0:T(1024)S(1)}, u32[]{:S(2)}, u32[]{:S(2)}) collective-permute-start(f32[4608]{0:T(1024)S(1)} %add.54), channel_id=1, source_target_pairs={{0,4},{2,6},{4,0},{6,2},{1,5},{3,7},{5,1},{7,3},{8,12},{10,14},{12... | collective-permute-start | bytes 55304 | tf_op jit(solution)/shard_map/ppermute | solution.py:1297
  688.4 2.5 copy-start.7
  690.9 3.1 copy-start.6
  694.0 3.0 copy-start.5
  697.0 3.0 copy-start.13
  697.0 4.6 copy-start.12
  700.1 3.2 copy-start.11
  700.1 4.7 copy-start.10
  701.6 6.1 copy-start.1

commit v5 on v4

--- a/solution.py
+++ b/solution.py
@@ -153,30 +153,58 @@
 
 
 class Spread:
-    def __init__(self, spot, own, full, keep, sems):
-        self.spot, self.own, self.full, self.keep = spot, own, full, keep
+    def __init__(self, spot, own, full, keep, sems, direct=0):
+        self.spot, self.own, self.full, self.keep, self.direct = spot, own, full, keep, direct
         (
             self.far_send, self.far_recv, self.right_send, self.right_recv, self.left_send, self.left_recv,
             self.mate_send, self.mate_recv,
         ) = sems
-        self.part = full.shape[1] // spot.n
+        self.part = (full.shape[1] - direct) // spot.n
         n, me = spot.n, spot.me
         self.near = remote(
             own, full.at[spot.shard], self.mate_send.at[0, 0], self.mate_recv.at[0, 0], {"shard": spot.mate}
         )
-        mine = pl.ds(pl.multiple_of(me * self.part, self.part), self.part)
+        mine = self.at(me)
         self.far = [
             remote(
-                own.at[mine], full.at[spot.shard, mine], self.far_send.at[d], self.far_recv.at[d],
+                own.at[mine], full.at[spot.shard, mine], self.far_send.at[d, 0], self.far_recv.at[d, 0],
                 {"shard": spot.away(d)},
             )
             for d in range(1, spot.chips)
         ]
+        whole = pl.ds(0, direct)
+        self.far_direct = [
+            remote(
+                own.at[whole], full.at[spot.shard, whole], self.far_send.at[d, 1], self.far_recv.at[d, 1],
+                {"shard": spot.away(d)},
+            )
+            for d in range(1, spot.chips)
+            if direct
+        ]
         self.can_right, self.can_left = me + 1 < n, me > 0
 
+    def at(self, z):
+        return pl.ds(pl.multiple_of(self.direct + z * self.part, 16), self.part)
+
+    def source(self, d):
+        return lax.rem(self.spot.shard - 2 * d + self.spot.shards, self.spot.shards)
+
     def piece(self, d, z):
-        source = lax.rem(self.spot.shard - 2 * d + self.spot.shards, self.spot.shards)
-        return self.full.at[source, pl.ds(pl.multiple_of(z * self.part, self.part), self.part)]
+        return self.full.at[self.source(d), self.at(z)]
+
+    def tell_direct(self, d):
+        at = self.full.at[self.source(d), pl.ds(0, self.direct)]
+        n = self.spot.n
+        return remote(at, at, self.mate_send.at[d, n], self.mate_recv.at[d, n], {"shard": self.spot.mate})
+
+    def start_direct(self):
+        for copy in self.far_direct:
+            copy.start()
+
+    def pass_on(self):
+        for d, copy in enumerate(self.far_direct, 1):
+            copy.wait_recv()
+            self.tell_direct(d).start()
 
     def tell(self, d, z):
         at = self.piece(d, z)
@@ -198,7 +226,6 @@
             copy.start()
 
     def start_near(self):
-        self.keep.start()
         self.near.start()
 
     def send_on(self, d, h, z, right, left):
@@ -236,6 +263,10 @@
         self.keep.wait()
         self.near.wait_recv()
         self.near.wait_send()
+        for d, copy in enumerate(self.far_direct, 1):
+            copy.wait_send()
+            self.tell_direct(d).wait_recv()
+            self.tell_direct(d).wait_send()
         for d in self.pairs():
             self.far[d - 1].wait_send()
             for z in range(n):
@@ -273,15 +304,17 @@
         sems = [local_sem.at[i], far_send.at[i], far_recv.at[i], near_send.at[i], near_recv.at[i]]
         return Gather(spot, own, full, sems, keep)
 
-    loads = [gather(i, w, weights.at[i]) for i, w in enumerate((wq, wk, wv, wo))]
+    loads = [None] + [gather(i, w, weights.at[i]) for i, w in ((1, wk), (2, wv), (3, wo))]
     keep = Keep(
         [(w, full.at[spot.shard]) for w, full in ((wi0, full_0), (wi1, full_1), (wff, full_2))], room, keep_sem
     )
     loads.append(gather(4, wi0, full_0, keep))
     spreads = [
-        Spread(spot, own, full, keep, [sem.at[i] for sem in spread_sems])
-        for i, (own, full) in enumerate(((wi1, full_1), (wff, full_2)))
+        Spread(spot, own, full, keep, [sem.at[i] for sem in spread_sems], direct)
+        for i, (own, full, direct) in enumerate(((wi1, full_1, shard_rows // 2), (wff, full_2, 0)))
     ]
+    keep_first = pltpu.make_async_copy(wq, weights.at[0, spot.shard], local_sem.at[0])
+    spreads.append(Spread(spot, wq, weights.at[0], keep_first, [sem.at[2] for sem in spread_sems]))
     flips = []
 
     def flip(value, out):
@@ -291,8 +324,13 @@
         flips.append(pltpu.make_async_copy(flipped, out, out_sem.at[5]))
         flips[-1].start()
 
-    loads[0].start_far()
-    for load in loads[:3]:
+    first = spreads[2]
+    first.start()
+    for load in loads[1:3]:
+        load.start_far()
+    first.keep.start()
+    first.start_near()
+    for load in loads[1:3]:
         load.start_near()
 
     @pl.loop(0, rows // 64)
@@ -310,23 +348,29 @@
         return dot(normed[:, at], weights[i, shard])
 
     moves = []
+    first.arrived()
+    for h in range(1, n):
+        first.hop(h)
     for i, load in enumerate(loads[:3]):
-        load.wait_own()
+        if i == 0:
+            first.wait()
+        else:
+            load.wait_own()
         acc[...] = term(i, spot.shard)
         acc[...] += term(i, spot.mate)
         keep.step()
-        load.pass_on()
-        if i < 2:
-            loads[i + 1].start_far()
-        else:
-            for spread in spreads:
+        if i:
+            load.pass_on()
+        if i == 2:
+            for spread in spreads[:2]:
                 spread.start()
-            for later in loads[3:] + spreads:
+            for later in loads[3:] + spreads[:2]:
                 later.start_near()
         keep.step()
         for d in range(1, spot.chips):
             acc[...] += term(i, lax.rem(spot.shard - 2 * d + shards, shards))
-        load.wait_near()
+        if i:
+            load.wait_near()
         for d in range(1, spot.chips):
             acc[...] += term(i, lax.rem(spot.mate - 2 * d + shards, shards))
         for k in range(n):
@@ -360,9 +404,8 @@
     def back(s, at, to):
         return remote(mixed.at[s, at], heads_in.at[me, s], back_send.at[s, at], back_recv.at[s, me], {"ctx": to})
 
-    @pl.loop(0, seqs * n)
-    def _(step):
-        s, a = step // n, lax.rem(step, n)
+    def attend(s, a):
+        step = s * n + a
         lane = lax.broadcasted_iota(jnp.int32, (part, lanes), 1)
         log_total = jnp.zeros((part, lanes), F32)
         for group in range(cols // lanes):
@@ -400,25 +443,23 @@
         def _():
             heads_in[a, s] = mixed[s, a]
 
-        @pl.when(step == 2)
+        @pl.when(step == 1)
         def _():
             spreads[0].hop(1)
 
-        @pl.when(step == 4)
+        @pl.when(step == 3)
         def _():
             loads[3].pass_on()
             loads[4].start_far()
-
-        @pl.when(step == 5)
+            spreads[0].start_direct()
+
+        @pl.when(step == 4)
         def _():
             spreads[1].hop(1)
 
-    if n > 2:
-        spreads[0].hop(2)
-    loads[3].wait_near()
-    outs[3].start()
     swaps = []
-    for s in range(seqs):
+
+    def project(s):
         at = pl.ds(s * part, part)
         for d in range(1, n):
             peer = lax.rem(me + d, n)
@@ -434,13 +475,23 @@
         swap = remote(normed.at[at], branch_in.at[s], swap_send.at[s], swap_recv.at[s], {"tp": 1 - spot.half})
         swap.start()
         swaps.append(swap)
+
+    for s in range(seqs):
+        pl.loop(0, n)(functools.partial(attend, s))
+        if s == 0:
+            loads[3].wait_near()
+            outs[3].start()
+            if n > 2:
+                spreads[0].hop(2)
+        project(s)
     if n > 2:
         spreads[1].hop(2)
     for h in range(3, n):
-        for spread in spreads:
+        for spread in spreads[:2]:
             spread.hop(h)
     loads[4].wait_own()
     loads[4].pass_on()
+    spreads[0].pass_on()
     for s in range(seqs):
         swaps[s].wait_recv()
 
@@ -456,9 +507,9 @@
 
     flip(normed_two[...], left_two)
     loads[4].wait_near()
-    for spread in spreads:
+    for spread in spreads[:2]:
         spread.wait()
-    for load in loads:
+    for load in loads[1:]:
         load.wait_sent()
     for move in moves + swaps:
         move.wait_send()
@@ -530,8 +581,9 @@
             dma((seqs,)),
             dma((6,)),
         ]
-        + [dma((2, chips))] * 2
-        + [dma((2, chips, n))] * 6,
+        + [dma((3, chips, 2))] * 2
+        + [dma((3, chips, n))] * 4
+        + [dma((3, chips, n + 1))] * 2,
         compiler_params=pltpu.CompilerParams(
             vmem_limit_bytes=60 * 2**20, collective_id=0, has_side_effects=True
         ),
@@ -911,10 +963,14 @@
             for s in range(seqs):
                 term[s, :, columns(j)] = total[s * part : (s + 1) * part].astype(BF16)
 
+            @pl.when(j == 1)
+            def _():
+                pump.step(fed_steps)
+
         for swap in swaps:
             swap.start()
         load(0, wff, 0).start()
-        pump.steps(fed_steps, fed_steps + 1)
+        pump.steps(fed_steps + 1, fed_steps + 2)
 
         @pl.loop(0, shards)
         def _(j):
@@ -930,7 +986,11 @@
             copy.start()
             copy.wait()
 
-        pump.steps(fed_steps + 1, fed_steps + 2)
+            @pl.when(j == 1)
+            def _():
+                pump.step(fed_steps + 2)
+
+        pump.steps(fed_steps + 3, fed_steps + 4)
 
     swaps = [
         remote(term.at[s], swap_in.at[s], swap_send.at[s], swap_recv.at[s], other_half) for s in range(seqs)
@@ -942,7 +1002,7 @@
         pltpu.SemaphoreType.DMA((2,)),
         pltpu.SemaphoreType.DMA((1,)),
     )
-    so_far = fed_steps + 2
+    so_far = fed_steps + 4
 
     def head_move(s, peer):
         return remote(
@@ -1110,8 +1170,9 @@
     so_far += seqs * groups
     lefts[2].start()
     lefts[2].wait()
-    pump.steps(so_far, so_far + 3)
-    so_far += 3
+    pump.steps(so_far, so_far + 1)
+    so_far += 1
+    assert so_far <= pump.early
     for s in range(seqs):
         for j in range(3):
             for d in range(1, n):

time: 718 us -> 679 us (0.946)
  Pallas kernels: 661 us -> 624 us
    pallas_call x1, Pallas kernels: 448 us -> 423 us  [per_device(): backward_call(dims)]
    pallas_call x1, Pallas kernels: 213 us -> 201 us  [per_device(): forward_call(dims)]
where the time goes in v5:
time: 679 us; the launch traced here: 670 us
  Pallas kernels  624 us (92%)
  other arithmetic  31.4 us (5%)
    pallas_call x1, Pallas kernels, per_device(): backward_call(dims)  423 us
    pallas_call x1, Pallas kernels, per_device(): forward_call(dims)  201 us
    convert_element_type x7, other arithmetic, per_device(): g.astype(F32)  15.4 us
  transfers between devices with their start and end apart: 4, of which 2 were waited for; matrix products, arithmetic and copies ran while one was open for 3% of the time, Pallas kernels for 0%

profile of v5, /device:TPU:0, one launch (start us, length us, event | category | flops | bytes accessed | tf_op | source)
XLA Modules:
  0.0 669.8 jit_solution(13288925412171532097)
XLA Ops:
  0.7 0.7 constant_dynamic-slice_fusion
  1.4 1.1 dynamic-slice_reduce_fusion
  2.6 0.7 convert_element_type.49
  3.3 0.7 stack.15
  4.0 2.1 fusion
  6.1 1.3 constant_dynamic-slice_fusion.1
  8.8 0.8 fusion.7.table
  10.3 200.5 %forward.1 = (f32[512,2048]{1,0:T(8,128)}, bf16[512,2048]{1,0:T(8,128)(2,1)}, bf16[512,1024]{1,0:T(8,128)(2,1)}, f32[2,4,256,128]{3,2,1,0:T(8,128)}, bf16[3,4,2,...) custom-call(bf16[512,2048]{1,0:T(8,128)(2,1)} %bitcast.26, ...), custom_call_target="tpu_custom_call" | custom-call | tf_op jit(solution)/shard_map/forward/pallas_call | solution.py:1419
  210.8 423.1 %backward.1 = (bf16[512,2560]{1,0:T(8,128)(2,1)}, bf16[512,2560]{1,0:T(8,128)(2,1)}, bf16[512,2560]{1,0:T(8,128)(2,1)}, bf16[512,1024]{1,0:T(8,128)(2,1)}, bf16[...) custom-call(f32[1,2048]{1,0:T(1,128)} %bitcast.33, ...), custom_call_target="tpu_custom_call" | custom-call | tf_op jit(solution)/shard_map/backward/pallas_call | solution.py:1424
  634.0 0.9 select_reduce_fusion
  635.3 4.7 fusion.3
  640.1 1.2 collective-permute-done
  641.3 3.7 collective-permute-done.1
  645.1 3.7 fusion.6
  648.9 1.0 collective-permute-start.3
  650.1 2.5 add_convert_fusion
  652.6 3.0 convert_element_type.61
  655.6 3.0 convert_element_type.62
  658.7 3.0 convert_element_type.63
  661.7 1.6 convert_element_type.57
  663.3 1.6 convert_element_type.58
  664.9 1.6 convert_element_type.59
  666.4 1.6 convert_element_type.60
  668.7 0.7 copy.27
  (60 shorter events, 3.7 us)
Async XLA Ops:
  0.6 8.2 %copy-start = (bf16[32,16]{0,1:T(8,128)(2,1)S(1)}, bf16[32,16]{0,1:T(8,128)(2,1)}, u32[]{:S(2)}) copy-start(bf16[32,16]{0,1:T(8,128)(2,1)} %param.25) | copy-start | bytes 3076
  4.0 206.8 %copy-start.14 = (f32[2048]{0:T(1024)}, f32[2048]{0:T(1024)S(1)}, u32[]{:S(2)}) copy-start(f32[2048]{0:T(1024)S(1)} %stack.15) | copy-start | bytes 24580
  635.3 4.7 copy-start.15
  635.3 9.8 %copy-start.2 = (bf16[2,256,2048]{2,1,0:T(8,128)(2,1)S(1)}, bf16[2,256,2048]{2,1,0:T(8,128)(2,1)}, u32[]{:S(2)}) copy-start(bf16[2,256,2048]{2,1,0:T(8,128)(2,1)} %param.13) | copy-start | bytes 6291460
  635.3 9.8 %copy-start.4 = (f32[512,2048]{1,0:T(8,128)S(1)}, f32[512,2048]{1,0:T(8,128)}, u32[]{:S(2)}) copy-start(f32[512,2048]{1,0:T(8,128)} %get-tuple-element.58) | copy-start | bytes 12582916
  640.0 1.3 collective-permute-start
  641.3 3.8 collective-permute-start.1
  645.1 3.8 collective-permute-start.2
  645.1 4.8 copy-start.3
  645.1 4.8 copy-start.8
  645.1 5.0 copy-start.9
  648.9 19.1 %collective-permute-start.3 = (f32[4608]{0:T(1024)S(1)}, f32[4608]{0:T(1024)S(1)}, u32[]{:S(2)}, u32[]{:S(2)}) collective-permute-start(f32[4608]{0:T(1024)S(1)} %add.54), channel_id=1, source_target_pairs={{0,4},{2,6},{4,0},{6,2},{1,5},{3,7},{5,1},{7,3},{8,12},{10,14},{12... | collective-permute-start | bytes 55304 | tf_op jit(solution)/shard_map/ppermute | solution.py:1358
  650.1 2.5 copy-start.7
  652.6 3.1 copy-start.6
  655.6 3.0 copy-start.5
  658.6 3.0 copy-start.13
  658.6 4.6 copy-start.12
  661.7 3.2 copy-start.11
  661.7 4.7 copy-start.10
  663.3 6.1 copy-start.1

commit v6 on v5

--- a/solution.py
+++ b/solution.py
@@ -32,10 +32,6 @@
     weighted = upstream * gain
     inner_average = jnp.mean(values * weighted, axis=-1, keepdims=True)
     return scale * weighted - values * scale * scale * scale * inner_average
-
-
-def geglu(gate, up):
-    return jax.nn.gelu(gate, approximate=True) * up
 
 
 def bias_rows(table_row, out):
@@ -282,13 +278,25 @@
                     self.left(d, h, me + h - 1).wait_send()
 
 
+def offset_buckets(dims, me, some_rows, out):
+    part, reach = dims.part, dims.n * dims.part
+    at = pl.ds(pl.multiple_of(me * part, part), part)
+    later = some_rows[0, 0:1, at].astype(F32)
+    earlier = some_rows[1, 7:8, at].astype(F32)
+    lane = lax.broadcasted_iota(jnp.int32, (1, part), 1)
+    out[:, : reach - part] = jnp.broadcast_to(earlier[:, :1], (1, reach - part))
+    out[:, reach - part : reach] = jnp.where(lane == 0, earlier[:, :1], pltpu.roll(earlier, 1, 1))
+    out[:, reach : reach + part] = later
+    out[:, reach + part :] = jnp.broadcast_to(later[:, part - 1 :], (1, reach - part))
+
+
 def forward_kernel(
-    dims, tokens, cotangent, gains, table, wq, wk, wv, wo, wi0, wi1, wff,
-    hidden, normed_two, attended, lse, pieces_out, left_g, left_one, left_two,
+    dims, tokens, cotangent, gain_one, gain_two, table, buckets, wq, wk, wv, wo, wi0, wi1, wff,
+    hidden, normed_two, attended, lse, by_offset, bias_table, pieces_out, left_g, left_one, left_two,
     full_q, full_k, full_v, full_o, full_0, full_1, full_2,
     normed, flipped, weights, acc, bias, staged, pieces, mixed, heads_in, rolled, branch_in,
     local_sem, far_send, far_recv, near_send, near_recv, head_send, head_recv, back_send, back_recv,
-    room, keep_sem,
+    room, some_rows, keep_sem, row_sem,
     swap_send, swap_recv, out_sem, *spread_sems,
 ):
     spot = Spot(*dims.mesh)
@@ -333,14 +341,30 @@
     for load in loads[1:3]:
         load.start_near()
 
+    row_copies = [
+        pltpu.make_async_copy(buckets.at[pl.ds(at, 8)], some_rows.at[i], row_sem.at[i])
+        for i, at in enumerate((0, part - 8))
+    ]
+    for copy in row_copies:
+        copy.start()
+
     @pl.loop(0, rows // 64)
     def _(i):
         at = pl.ds(pl.multiple_of(i * 64, 64), 64)
         values = tokens[at, :].astype(F32)
-        normed[at, :] = (values * rms_scale(values) * gains[0:1, :]).astype(BF16)
-
+        normed[at, :] = (values * rms_scale(values) * gain_one[...].astype(F32)).astype(BF16)
+
+    for copy in row_copies:
+        copy.wait()
+    offset_buckets(dims, me, some_rows, by_offset)
+    slots = table.shape[0]
+    hot = by_offset[...] == lax.broadcasted_iota(jnp.int32, (slots, by_offset.shape[1]), 0).astype(F32)
+    lane = lax.broadcasted_iota(jnp.int32, table.shape, 1)
     for head in range(dims.own_heads):
-        bias_rows(table[head : head + 1, :], rolled)
+        own = lane == me * dims.own_heads + head
+        column = jnp.sum(jnp.where(own, table[...].astype(F32), 0.0), axis=1, keepdims=True)
+        bias_table[head : head + 1, :] = jnp.sum(jnp.where(hot, column, 0.0), axis=0, keepdims=True)
+        bias_rows(bias_table[head : head + 1, :], rolled)
         bias[head] = rolled[...].astype(BF16)
 
     def term(i, shard):
@@ -503,7 +527,7 @@
                 normed[at, :].astype(F32) + branch_in[s, here, :].astype(F32)
             )
             hidden[at, :] = values
-            normed_two[at, :] = (values * rms_scale(values) * gains[1:2, :]).astype(BF16)
+            normed_two[at, :] = (values * rms_scale(values) * gain_two[...].astype(F32)).astype(BF16)
 
     flip(normed_two[...], left_two)
     loads[4].wait_near()
@@ -522,13 +546,14 @@
 
 
 class Dims:
-    def __init__(self, links, seqs, part, width, inner_width, units, heads):
-        self.mesh = (links.shard, links.ctx, links.tp)
-        self.n, self.seqs, self.part, self.width = links.ctx, seqs, part, width
+    def __init__(self, mesh, seqs, part, width, inner_width, units, heads, slots):
+        self.mesh = shards, ctx, tp = tuple(mesh.shape[a] for a in ("shard", "ctx", "tp"))
+        self.slots = slots
+        self.n, self.seqs, self.part, self.width = ctx, seqs, part, width
         self.inner_width, self.units = inner_width, units
         self.head_dim = inner_width // heads
-        self.cols, self.own_heads = inner_width // links.ctx, heads // links.ctx
-        self.shards, self.shard_rows = links.shard, width // links.shard
+        self.cols, self.own_heads = inner_width // ctx, heads // ctx
+        self.shards, self.shard_rows = shards, width // shards
 
 
 def forward_call(dims):
@@ -542,13 +567,15 @@
     block = (seqs, part, dims.cols)
     return pl.pallas_call(
         functools.partial(forward_kernel, dims),
-        in_specs=[vmem] * 4 + [anywhere] * 7,
-        out_specs=[vmem] * 4 + [anywhere] * 11,
+        in_specs=[vmem] * 5 + [anywhere] * 8,
+        out_specs=[vmem] * 6 + [anywhere] * 11,
         out_shape=[
             shape((rows, width), F32),
             shape((rows, width), BF16),
             shape((rows, inner), BF16),
             shape((seqs, n, part, lanes), F32),
+            shape((1, span), F32),
+            shape((dims.own_heads, span), F32),
             shape((3, n) + block, BF16),
         ]
         + [shape((width, rows), BF16)] * 3
@@ -576,6 +603,8 @@
             dma((seqs, n)),
             dma((seqs, n)),
             pltpu.VMEM((shard_rows, units), BF16),
+            pltpu.VMEM((2, 8, n * part), jnp.int32),
+            dma((2,)),
             dma((2,)),
             dma((seqs,)),
             dma((seqs,)),
@@ -593,6 +622,8 @@
 
 CHUNK = 512
 SLOTS = 4
+LAYER_STEPS = 4
+INPUT_STEPS = 3
 
 
 class Pump:
@@ -836,16 +867,17 @@
 
 
 def backward_kernel(
-    dims, gain_two, table,
-    lse_from, pieces_from, left_g, left_two, left_one, normed_two, attended, hidden, cotangent,
+    dims, gain_one, gain_two, table, by_offset,
+    tokens, lse_from, pieces_from, left_g, left_two, left_one, normed_two, attended, hidden, cotangent,
     wo, wq, wk, wv, wi0, wi1, wff,
     down_out, gate_out, up_out, o_out, q_out, k_out, v_out,
-    grad_hidden, ffn_term, ffn_other, term_one, other_one, ffn_gain, table_out,
+    layer_out, input_grad, grad_hidden, ffn_term, ffn_other, small_out,
+    other_one, norm_gain, ffn_gain, table_out, small, small_in,
     left, right, core_out, core_in, far_out, far_in, line, line_in, across_in, done,
     fed, term, swap_in, grads, grads_out, grads_in,
     right_sem, core_send, core_recv, far_send, far_recv, in_send, in_recv, across_send, across_recv,
     out_send, out_recv, fin_sem, swap_send, swap_recv, head_send, head_recv, back_send, back_recv,
-    one_send, one_recv, ffn_sem, local_sem,
+    one_send, one_recv, ffn_sem, local_sem, small_send, small_recv,
     core_credit, far_credit, in_credit, across_credit, out_credit,
 ):
     spot = Spot(*dims.mesh)
@@ -872,6 +904,7 @@
     ]
     spot.barrier()
     ffn_gain[...] = jnp.zeros_like(ffn_gain)
+    norm_gain[...] = jnp.zeros_like(norm_gain)
     table_out[...] = jnp.zeros_like(table_out)
 
     def feed(weights, values, given, sem, value_sem):
@@ -1033,7 +1066,7 @@
             grad = term[s, here, :].astype(F32) + swap_in[s, here, :].astype(F32)
             scale = rms_scale(h)
             ffn_gain[...] += jnp.sum(grad * h * scale, axis=0, keepdims=True)
-            total = given[here, :].astype(F32) + rms_back(h, scale, gain_two[...], grad)
+            total = given[here, :].astype(F32) + rms_back(h, scale, gain_two[...].astype(F32), grad)
             values[here, :] = total
             own[here, :] = total.astype(BF16)
 
@@ -1178,6 +1211,9 @@
             for d in range(1, n):
                 back_wait(j, s, lax.rem(me + d, n))
 
+    for copy in swaps:
+        copy.wait_send()
+
     def first_norm_terms(weights, values, sem):
         def load(shard):
             return [
@@ -1201,7 +1237,7 @@
             total += contract_cols(values[1], weights[shard % 2, 1])
             total += contract_cols(values[2], weights[shard % 2, 2])
             for s in range(seqs):
-                term_one[s, :, shard * shard_rows : (shard + 1) * shard_rows] = (
+                term[s, :, shard * shard_rows : (shard + 1) * shard_rows] = (
                     total[s * part : (s + 1) * part].astype(BF16)
                 )
 
@@ -1212,15 +1248,107 @@
         pltpu.SemaphoreType.DMA((2, 3)),
     )
     ones = [
-        remote(term_one.at[s], other_one.at[s], one_send.at[s], one_recv.at[s], other_half) for s in range(seqs)
+        remote(term.at[s], other_one.at[s], one_send.at[s], one_recv.at[s], other_half) for s in range(seqs)
     ]
     for swap in ones:
         swap.start()
+    pump.steps(so_far, so_far + LAYER_STEPS)
+    so_far += LAYER_STEPS
+    ffn_swap.wait_recv()
+
+    def layer_output(values, own, other, sem):
+        for s in range(seqs):
+            at = pl.ds(s * part, part)
+            copies = [
+                pltpu.make_async_copy(source.at[at, :], to, sem.at[i])
+                for i, (source, to) in enumerate(((hidden, values), (ffn_term, own), (ffn_other, other)))
+            ]
+            for copy in copies:
+                copy.start()
+            for copy in copies:
+                copy.wait()
+
+            @pl.loop(0, part // 64)
+            def _(i):
+                here = pl.ds(pl.multiple_of(i * 64, 64), 64)
+                total = own[here, :].astype(F32) + other[here, :].astype(F32)
+                own[here, :] = (values[here, :] + total).astype(BF16)
+
+            saved = pltpu.make_async_copy(own, layer_out.at[at, :], sem.at[0])
+            saved.start()
+            saved.wait()
+
+    pl.run_scoped(
+        layer_output,
+        pltpu.VMEM((part, width), F32),
+        pltpu.VMEM((part, width), BF16),
+        pltpu.VMEM((part, width), BF16),
+        pltpu.SemaphoreType.DMA((3,)),
+    )
+    pump.steps(so_far, so_far + INPUT_STEPS)
+    so_far += INPUT_STEPS
+
+    def first_norm_back(values, given, sem):
+        for s in range(seqs):
+            at = pl.ds(s * part, part)
+            copies = [
+                pltpu.make_async_copy(source.at[at, :], to, sem.at[i])
+                for i, (source, to) in enumerate(((grad_hidden, values), (tokens, given)))
+            ]
+            for copy in copies:
+                copy.start()
+            for copy in copies:
+                copy.wait()
+            ones[s].wait_recv()
+
+            @pl.loop(0, part // 64)
+            def _(i):
+                here = pl.ds(pl.multiple_of(i * 64, 64), 64)
+                x = given[here, :].astype(F32)
+                grad = term[s, here, :].astype(F32) + other_one[s, here, :].astype(F32)
+                scale = rms_scale(x)
+                norm_gain[...] += jnp.sum(grad * x * scale, axis=0, keepdims=True)
+                values[here, :] += rms_back(x, scale, gain_one[...].astype(F32), grad)
+
+            saved = pltpu.make_async_copy(values, input_grad.at[at, :], sem.at[0])
+            saved.start()
+            saved.wait()
+
+    pl.run_scoped(
+        first_norm_back,
+        pltpu.VMEM((part, width), F32),
+        pltpu.VMEM((part, width), BF16),
+        pltpu.SemaphoreType.DMA((2,)),
+    )
+
+    lines, slots = width // 128, small.shape[1] - 2 * (width // 128)
+    for i in range(lines):
+        small[0, i : i + 1, :] = norm_gain[:, i * 128 : (i + 1) * 128]
+        small[0, lines + i : lines + i + 1, :] = ffn_gain[:, i * 128 : (i + 1) * 128]
+    hot = by_offset[...] == lax.broadcasted_iota(jnp.int32, (slots, span), 0).astype(F32)
+    lane = lax.broadcasted_iota(jnp.int32, (slots, 128), 1)
+    table_part = jnp.zeros((slots, 128), F32)
+    for head in range(dims.own_heads):
+        column = jnp.sum(jnp.where(hot, table_out[head : head + 1, :], 0.0), axis=1, keepdims=True)
+        table_part = jnp.where(lane == me * dims.own_heads + head, column, table_part)
+    small[0, 2 * lines :, :] = table_part
+    partners = []
+    for axis, at, count in (("shard", spot.shard, shards), ("ctx", me, n)):
+        step = 1
+        while step < count:
+            partners.append({axis: at + step * (1 - 2 * lax.rem(at // step, 2))})
+            step *= 2
+    for i, partner in enumerate(partners):
+        copy = remote(small.at[i], small_in.at[i], small_send.at[i], small_recv.at[i], partner)
+        copy.start()
+        pump.steps(so_far, so_far + 1)
+        so_far += 1
+        copy.wait_recv()
+        copy.wait_send()
+        small[i + 1] = small[i] + small_in[i]
+    small_out[...] = small[len(partners)]
     pump.steps(so_far, pump.last)
-    for swap in swaps:
-        swap.wait_send()
     for copy in ones + [ffn_swap]:
-        copy.wait_recv()
         copy.wait_send()
     for s in range(seqs):
         for d in range(1, n):
@@ -1236,23 +1364,30 @@
     vmem, anywhere = pl.BlockSpec(memory_space=pltpu.VMEM), pl.BlockSpec(memory_space=pl.ANY)
     shape, dma, regular = jax.ShapeDtypeStruct, pltpu.SemaphoreType.DMA, pltpu.SemaphoreType.REGULAR
     far = max(chips - 1, 1)
+    stages = (shards * n).bit_length() - 1
+    lines = 2 * (width // 128) + dims.slots
     block = (shard_rows, CHUNK)
     return pl.pallas_call(
         functools.partial(backward_kernel, dims),
-        in_specs=[vmem] * 2 + [anywhere] * 16,
-        out_specs=[anywhere] * 10 + [vmem, anywhere, vmem, vmem],
+        in_specs=[vmem] * 4 + [anywhere] * 17,
+        out_specs=[anywhere] * 12 + [vmem],
         out_shape=[shape((shard_rows, units), BF16)] * 3
         + [shape((shard_rows, inner), BF16)] * 4
         + [
+            shape((rows, width), BF16),
+            shape((rows, width), F32),
             shape((rows, width), F32),
             shape((rows, width), BF16),
             shape((rows, width), BF16),
-            shape((seqs, part, width), BF16),
-            shape((seqs, part, width), BF16),
-            shape((1, width), F32),
-            shape((dims.own_heads, span), F32),
+            shape((lines, 128), F32),
         ],
         scratch_shapes=[
+            pltpu.VMEM((seqs, part, width), BF16),
+            pltpu.VMEM((1, width), F32),
+            pltpu.VMEM((1, width), F32),
+            pltpu.VMEM((dims.own_heads, span), F32),
+            pltpu.VMEM((stages + 1, lines, 128), F32),
+            pltpu.VMEM((stages, lines, 128), F32),
             pltpu.VMEM((3, width, rows), BF16),
             pltpu.VMEM((SLOTS, rows, CHUNK), BF16),
             pltpu.VMEM((2, chips) + block, BF16),
@@ -1280,7 +1415,7 @@
         + [dma((seqs, n))] * 2
         + [dma((3, seqs, n))] * 2
         + [dma((seqs,))] * 2
-        + [dma((2,)), dma((4,))]
+        + [dma((2,)), dma((4,)), dma((stages,)), dma((stages,))]
         + [regular, regular((far,)), regular, regular, regular],
         compiler_params=pltpu.CompilerParams(
             vmem_limit_bytes=62 * 2**20, collective_id=1, has_side_effects=True
@@ -1289,79 +1424,8 @@
     )
 
 
-def ring(n, d):
-    return [(i, (i + d) % n) for i in range(n)]
-
-
-class Links:
-    def __init__(self, mesh):
-        self.shard, self.ctx, self.tp = mesh.shape["shard"], mesh.shape["ctx"], mesh.shape["tp"]
-        self.chips = self.shard // 2
-
-    def to_core(self, value):
-        return lax.ppermute(value, "shard", [(i, i ^ 1) for i in range(self.shard)])
-
-    def to_chip(self, value, d):
-        n = self.shard
-        return lax.ppermute(value, "shard", [(i, (i + 2 * d) % n) for i in range(n)])
-
-    def tp_sum(self, value):
-        if self.tp != 2:
-            return lax.psum(value, "tp").astype(F32)
-        other = lax.ppermute(value, "tp", ring(2, 1))
-        return value.astype(F32) + other.astype(F32)
-
-    def ctx_sum(self, value):
-        low = value.astype(BF16)
-        if self.ctx != 4:
-            return lax.psum(low, "ctx").astype(F32)
-        inward = lax.ppermute(low, "ctx", [(0, 1), (3, 2)])
-        half = (low.astype(F32) + inward.astype(F32)).astype(BF16)
-        across = lax.ppermute(half, "ctx", [(1, 2), (2, 1)])
-        whole = (half.astype(F32) + across.astype(F32)).astype(BF16)
-        outward = lax.ppermute(whole, "ctx", [(1, 0), (2, 3)])
-        me = lax.axis_index("ctx")
-        middle = (me == 1) | (me == 2)
-        return jnp.where(middle, whole, outward).astype(F32)
-
-    def shard_sums(self, left, right):
-        n, chips = self.shard, self.chips
-        rows = left.shape[1] // n
-        me = lax.axis_index("shard")
-        chip, core = me // 2, me % 2
-
-        def term(chip_at, core_at):
-            at = (2 * chip_at + core_at) * rows
-            return contract_rows(lax.dynamic_slice_in_dim(left, at, rows, 1), right)
-
-        def chip_of(d):
-            return lax.rem(chip + d, chips)
-
-        order = list(range(1, chips)) + [0]
-        got = {d: self.to_core(term(chip_of(d), 1 - core).astype(BF16)) for d in order}
-        total = None
-        arrived = []
-        for d in order:
-            pair = term(chip_of(d), core) + got[d].astype(F32)
-            if d:
-                arrived.append(self.to_chip(pair.astype(BF16), d))
-            else:
-                total = pair
-        for value in arrived:
-            total = total + value.astype(F32)
-        return total
-
-    def small_sum(self, value):
-        for axis, n in (("shard", self.shard), ("ctx", self.ctx)):
-            step = 1
-            while step < n:
-                value = value + lax.ppermute(value, axis, [(i, i ^ step) for i in range(n)])
-                step *= 2
-        return value
-
-
 def per_device(
-    links,
+    mesh,
     tokens,
     cotangent,
     buckets,
@@ -1377,72 +1441,27 @@
     bucket_bias_table,
 ):
     seqs, part, width = tokens.shape
-    rows = seqs * part
+    rows, inner_width = seqs * part, query_weight.shape[1]
     slots, heads = bucket_bias_table.shape
-    inner_width = query_weight.shape[1]
-    head_dim = inner_width // heads
-    n = links.ctx
-    cols = inner_width // n
-    own_heads = heads // n
-    me = lax.axis_index("ctx")
-    gain_one = norm_gain.astype(F32)
-    gain_two = ffn_gain.astype(F32)
-
-    def gathered(weight):
-        return lax.all_gather(weight, "shard", axis=0, tiled=True)
-
-    def at_ctx(d):
-        return lax.rem(me + d + n, n)
-
-    corner = lax.dynamic_slice(buckets, (0, me * part), (part, part))
-    later, earlier = corner[0, :], corner[:, 0]
-    reach = n * part
-    by_offset = jnp.concatenate(
-        [
-            jnp.broadcast_to(earlier[part - 1 :], (reach - part + 1,)),
-            earlier[:0:-1],
-            later,
-            jnp.broadcast_to(later[part - 1 :], (reach - part,)),
-        ]
-    )
-    indicator = by_offset[None, :] == jnp.arange(slots, dtype=jnp.int32)[:, None]
-    own_table = lax.dynamic_slice(bucket_bias_table, (0, me * own_heads), (slots, own_heads))
-    offset_bias = lax.dot_general(
-        own_table, indicator.astype(BF16), (((0,), (0,)), ((), ())), preferred_element_type=F32
-    )
-    groups = cols // (2 * head_dim)
-    offset_bias = offset_bias.reshape(groups, 2, 2 * reach)
-
-    dims = Dims(links, seqs, part, width, inner_width, gate_weight.shape[1], heads)
+    dims = Dims(mesh, seqs, part, width, inner_width, gate_weight.shape[1], heads, slots)
     token_rows, upstream = tokens.reshape(rows, width), cotangent.reshape(rows, width)
-    bias_table = offset_bias.reshape(own_heads, 2 * reach)
-    hidden, normed_two, attended, lse, pieces, *lefts_and_weights = forward_call(dims)(
-        token_rows, upstream, jnp.stack([gain_one, gain_two]), bias_table,
+    gain_one, gain_two = norm_gain.reshape(1, width), ffn_gain.reshape(1, width)
+    hidden, normed_two, attended, lse, by_offset, bias_table, pieces, *lefts_and_weights = forward_call(dims)(
+        token_rows, upstream, gain_one, gain_two, bucket_bias_table, buckets,
         query_weight, key_weight, value_weight, output_weight, gate_weight, up_weight, down_weight,
     )
     left_g, left_one, left_two, wq, wk, wv, wo, wi0, wi1, wff = lefts_and_weights
-    *weight_grads, grad_hidden, ffn_term, ffn_other, term_one, other_one, grad_ffn_gain, offset_grad = backward_call(dims)(
-        gain_two.reshape(1, width), bias_table,
-        lse, pieces, left_g, left_two, left_one, normed_two, attended, hidden, upstream,
+    *weight_grads, result, grad_inputs, unused, unused_own, unused_other, small = backward_call(dims)(
+        gain_one, gain_two, bias_table, by_offset,
+        token_rows, lse, pieces, left_g, left_two, left_one, normed_two, attended, hidden, upstream,
         wo, wq, wk, wv, wi0, wi1, wff,
     )
-    inputs = token_rows.astype(F32)
-    scale_one = rms_scale(inputs)
     grad_down_w, grad_gate_w, grad_up_w, grad_output_w, grad_query_w, grad_key_w, grad_value_w = (
         g.astype(F32) for g in weight_grads
     )
-    result = (hidden + (ffn_term.astype(F32) + ffn_other.astype(F32))).astype(BF16).reshape(seqs, part, width)
-    grad_ffn_gain = grad_ffn_gain[0]
-    table_part = jnp.sum(jnp.where(indicator[:, None, :], offset_grad[None], 0.0), axis=-1)
-    grad_table = lax.dynamic_update_slice(
-        jnp.zeros((slots, heads), F32), table_part, (0, me * own_heads)
-    )
-    grad_normed = (term_one.astype(F32) + other_one.astype(F32)).reshape(rows, width)
-    grad_norm_gain = jnp.sum(grad_normed * inputs * scale_one, axis=0)
-    grad_inputs = grad_hidden + rms_back(inputs, scale_one, gain_one, grad_normed)
-    small = links.small_sum(jnp.concatenate([grad_norm_gain, grad_ffn_gain, grad_table.reshape(-1)]))
+    lines = width // 128
     return (
-        result,
+        result.reshape(seqs, part, width),
         grad_inputs.reshape(seqs, part, width),
         grad_query_w,
         grad_key_w,
@@ -1451,16 +1470,16 @@
         grad_gate_w,
         grad_up_w,
         grad_down_w,
-        small[:width],
-        small[width : 2 * width],
-        small[2 * width :].reshape(slots, heads),
+        small[:lines].reshape(width),
+        small[lines : 2 * lines].reshape(width),
+        small[2 * lines :, :heads],
     )
 
 
 def solution(mesh):
     rows, weights = P("shard", "ctx", None), P("shard", "tp")
     return jax.shard_map(
-        functools.partial(per_device, Links(mesh)),
+        functools.partial(per_device, mesh),
         mesh=mesh,
         in_specs=(rows, rows, P("ctx", None)) + (weights,) * 7 + (P(), P(), P(None, "tp")),
         out_specs=(rows, rows) + (weights,) * 7 + (P(), P(), P(None, "tp")),

time: 679 us -> 663 us (0.976)
  other arithmetic: 31.4 us -> 16.7 us
    reduce_sum x3 -> x0, other arithmetic: 7.71 us -> none  [the longest x1 4.69 us: per_device(): grad_norm_gain = jnp.sum(grad_normed * inputs * scale_one, axis=0)]
  transfers between devices with their start and end apart: 4 -> 0, of which waited for: 2 -> 0; matrix products, arithmetic and copies ran while one was open for 3% -> 0% of each run, Pallas kernels for 0% -> 0%
where the time goes in v6:
time: 663 us; the launch traced here: 654 us
  Pallas kernels  625 us (94%)
  other arithmetic  16.7 us (3%)
  local copies, waits for them, and re-layouts  11.7 us (2%)
    pallas_call x1, Pallas kernels, per_device(): backward_call(dims)  424 us
    pallas_call x1, Pallas kernels, per_device(): forward_call(dims)  200 us
    convert_element_type x7, other arithmetic, per_device(): g.astype(F32)  16.7 us

profile of v6, /device:TPU:0, one launch (start us, length us, event | category | flops | bytes accessed | tf_op | source)
XLA Modules:
  0.0 654.1 jit_solution(1423120241212022908)
XLA Ops:
  0.6 1.3 reshape.48.gain_one
  1.9 1.3 reshape.49.gain_two
  3.2 1.4 copy.25.table
  4.6 200.5 %forward.1 = (f32[512,2048]{1,0:T(8,128)}, bf16[512,2048]{1,0:T(8,128)(2,1)}, bf16[512,1024]{1,0:T(8,128)(2,1)}, f32[2,4,256,128]{3,2,1,0:T(8,128)}, f32[1,2048]...) custom-call(bf16[512,2048]{1,0:T(8,128)(2,1)} %bitcast.8, ...), custom_call_target="tpu_custom_call" | custom-call | tf_op jit(solution)/shard_map/forward/pallas_call | solution.py:1449
  205.0 424.1 %backward.1 = (bf16[512,2560]{1,0:T(8,128)(2,1)}, bf16[512,2560]{1,0:T(8,128)(2,1)}, bf16[512,2560]{1,0:T(8,128)(2,1)}, bf16[512,1024]{1,0:T(8,128)(2,1)}, bf16[...) custom-call(bf16[1,2048]{1,0:T(2,128)(2,1)} %reshape.48.gain_one, ...), custom_call_target="tpu_custom_call" | custom-call | tf_op jit(solution)/shard_map/backward/pallas_call | solution.py:1454
  629.2 0.0 copy-start.7
  629.2 0.8 slice.11
  630.0 1.3 slice_bitcast_fusion
  631.3 0.7 copy.26
  632.0 2.9 convert_element_type.21
  634.9 0.0 copy-done.7
  634.9 1.6 convert_element_type.22
  636.4 0.0 copy-done.6
  636.4 1.6 convert_element_type.23
  638.0 0.0 copy-done.5
  638.0 1.6 convert_element_type.24
  639.6 0.0 copy-done.3
  639.6 3.0 convert_element_type.25
  642.6 0.0 copy-done.2
  642.6 3.0 convert_element_type.26
  645.7 3.0 convert_element_type.27
  648.7 1.3 copy.29
  650.0 1.6 copy-done
  651.6 2.0 copy.30
  (9 shorter events, 0.0 us)
Async XLA Ops:
  629.2 5.7 copy-start.7
  632.0 4.5 copy-start.6
  634.9 3.1 copy-start.5
  636.4 3.1 copy-start.3
  639.6 3.0 copy-start.2
  642.6 3.0 copy-start.1
  645.7 3.0 copy-start.4
  648.7 2.9 copy-start

commit v7 on v6

--- a/solution.py
+++ b/solution.py
@@ -73,7 +73,7 @@
         semaphore = pltpu.get_barrier_semaphore()
         for peer in peers:
             pl.semaphore_signal(semaphore, inc=1, device_id=peer, device_id_type=MESH)
-        pl.semaphore_wait(semaphore, len(peers))
+        return lambda: pl.semaphore_wait(semaphore, len(peers))
 
 
 def remote(src, dst, send, recv, peer):
@@ -306,7 +306,7 @@
     rows = seqs * part
     lanes = 2 * head_dim
     per = 2
-    spot.barrier()
+    spot.barrier()()
 
     def gather(i, own, full, keep=None):
         sems = [local_sem.at[i], far_send.at[i], far_recv.at[i], near_send.at[i], near_recv.at[i]]
@@ -388,6 +388,9 @@
         if i == 2:
             for spread in spreads[:2]:
                 spread.start()
+            loads[3].start_far()
+            loads[4].start_far()
+            spreads[0].start_direct()
             for later in loads[3:] + spreads[:2]:
                 later.start_near()
         keep.step()
@@ -417,7 +420,6 @@
     flip(normed[...], left_one)
     spreads[0].arrived()
     spreads[1].arrived()
-    loads[3].start_far()
     flip(cotangent[...], left_g)
     for move in moves:
         move.wait_recv()
@@ -474,8 +476,6 @@
         @pl.when(step == 3)
         def _():
             loads[3].pass_on()
-            loads[4].start_far()
-            spreads[0].start_direct()
 
         @pl.when(step == 4)
         def _():
@@ -902,7 +902,7 @@
         pltpu.make_async_copy(source, left.at[i], local_sem.at[i])
         for i, source in ((0, left_g), (1, left_two), (0, left_one))
     ]
-    spot.barrier()
+    all_here = spot.barrier()
     ffn_gain[...] = jnp.zeros_like(ffn_gain)
     norm_gain[...] = jnp.zeros_like(norm_gain)
     table_out[...] = jnp.zeros_like(table_out)
@@ -950,6 +950,7 @@
             def _():
                 for copy in lefts[:2]:
                     copy.wait()
+                all_here()
 
             pump.step(c)
 
@@ -1424,6 +1425,69 @@
     )
 
 
+TILE = 64
+
+
+def finish_kernel(count, *refs):
+    sources, outs = refs[:count], refs[count : 2 * count]
+    taken, made = refs[2 * count : 3 * count], refs[3 * count : 4 * count]
+    take_sem, save_sem = refs[4 * count :]
+    tiles = [source.shape[0] // TILE for source in sources]
+
+    def at(i):
+        return pl.ds(pl.multiple_of(i * TILE, TILE), TILE)
+
+    def take(j, i):
+        return pltpu.make_async_copy(sources[j].at[at(i)], taken[j].at[at(i)], take_sem.at[j, i])
+
+    def save(j, i):
+        return pltpu.make_async_copy(made[j].at[at(i)], outs[j].at[at(i)], save_sem.at[j, i])
+
+    for j in range(count):
+        @pl.loop(0, tiles[j])
+        def _(i):
+            take(j, i).start()
+
+    for j in range(count):
+        @pl.loop(0, tiles[j])
+        def _(i):
+            take(j, i).wait()
+            if made[j].dtype != taken[j].dtype:
+                made[j][at(i), :] = taken[j][at(i), :].astype(made[j].dtype)
+            save(j, i).start()
+
+    for j in range(count):
+        @pl.loop(0, tiles[j])
+        def _(i):
+            save(j, i).wait()
+
+
+def finish(sources, types):
+    count = len(sources)
+    taken = [pltpu.VMEM(s.shape, s.dtype) for s in sources]
+    made = [pltpu.VMEM(s.shape, t) for s, t in zip(sources, types)]
+    same = [s.dtype == t for s, t in zip(sources, types)]
+    tiles = max(s.shape[0] for s in sources) // TILE
+
+    def kernel(*refs):
+        refs = list(refs)
+        made_at = iter(refs[3 * count : -2])
+        full = [refs[2 * count + j] if same[j] else next(made_at) for j in range(count)]
+        finish_kernel(count, *refs[: 3 * count], *full, *refs[-2:])
+
+    return pl.pallas_call(
+        kernel,
+        in_specs=[pl.BlockSpec(memory_space=pl.ANY)] * count,
+        out_specs=[pl.BlockSpec(memory_space=pl.ANY)] * count,
+        out_shape=[jax.ShapeDtypeStruct(s.shape, t) for s, t in zip(sources, types)],
+        scratch_shapes=taken
+        + [m for m, keep in zip(made, same) if not keep]
+        + [pltpu.SemaphoreType.DMA((count, tiles))] * 2,
+        compiler_params=pltpu.CompilerParams(vmem_limit_bytes=56 * 2**20),
+        name="finish",
+    )(*sources)
+
+
 def per_device(
     mesh,
     tokens,
@@ -1456,9 +1520,8 @@
         token_rows, lse, pieces, left_g, left_two, left_one, normed_two, attended, hidden, upstream,
         wo, wq, wk, wv, wi0, wi1, wff,
     )
-    grad_down_w, grad_gate_w, grad_up_w, grad_output_w, grad_query_w, grad_key_w, grad_value_w = (
-        g.astype(F32) for g in weight_grads
-    )
+    *weight_grads, grad_inputs, result = finish(weight_grads + [grad_inputs, result], [F32] * 8 + [BF16])
+    grad_down_w, grad_gate_w, grad_up_w, grad_output_w, grad_query_w, grad_key_w, grad_value_w = weight_grads
     lines = width // 128
     return (
         result.reshape(seqs, part, width),

time: 663 us -> 647 us (0.976)
  other arithmetic: 16.7 us -> 0 us
    pallas_call x0 -> x1, Pallas kernels: none -> 18 us  [finish(): pl.pallas_call(kernel, in_specs=[pl.BlockSpec(memory_space=pl.ANY)] * cou...]
    convert_element_type x7 -> x0, other arithmetic: 16.7 us -> none  [per_device(): g.astype(F32)]
    pallas_call x1, Pallas kernels: 424 us -> 414 us  [per_device(): backward_call(dims)]
where the time goes in v7:
time: 647 us; the launch traced here: 639 us
  Pallas kernels  631 us (98%)
  local copies, waits for them, and re-layouts  6.65 us (1%)
    pallas_call x1, Pallas kernels, per_device(): backward_call(dims)  414 us
    pallas_call x1, Pallas kernels, per_device(): forward_call(dims)  198 us
    pallas_call x1, Pallas kernels, finish(): pl.pallas_call(kernel, in_specs=[pl.BlockSpec(memory_space=pl.ANY)] * cou...  18 us

profile of v7, /device:TPU:0, one launch (start us, length us, event | category | flops | bytes accessed | tf_op | source)
XLA Modules:
  0.0 638.5 jit_solution(12341981529766688809)
XLA Ops:
  0.6 1.3 reshape.48.gain_one
  1.9 1.3 reshape.49.gain_two
  3.2 1.4 copy.25.table
  4.6 198.3 %forward.1 = (f32[512,2048]{1,0:T(8,128)}, bf16[512,2048]{1,0:T(8,128)(2,1)}, bf16[512,1024]{1,0:T(8,128)(2,1)}, f32[2,4,256,128]{3,2,1,0:T(8,128)}, f32[1,2048]...) custom-call(bf16[512,2048]{1,0:T(8,128)(2,1)} %bitcast.8, ...), custom_call_target="tpu_custom_call" | custom-call | tf_op jit(solution)/shard_map/forward/pallas_call | solution.py:1513
  202.9 414.5 %backward.1 = (bf16[512,2560]{1,0:T(8,128)(2,1)}, bf16[512,2560]{1,0:T(8,128)(2,1)}, bf16[512,2560]{1,0:T(8,128)(2,1)}, bf16[512,1024]{1,0:T(8,128)(2,1)}, bf16[...) custom-call(bf16[1,2048]{1,0:T(2,128)(2,1)} %reshape.48.gain_one, ...), custom_call_target="tpu_custom_call" | custom-call | tf_op jit(solution)/shard_map/backward/pallas_call | solution.py:1518
  617.4 0.7 slice.11
  618.1 1.3 slice_bitcast_fusion
  619.4 0.7 copy.26
  620.1 18.0 %finish.1 = (f32[512,2560]{1,0:T(8,128)}, f32[512,2560]{1,0:T(8,128)}, f32[512,2560]{1,0:T(8,128)}, f32[512,1024]{1,0:T(8,128)}, f32[512,1024]{1,0:T(8,128)}, /*...) custom-call(bf16[512,2560]{1,0:T(8,128)(2,1)} %get-tuple-element.65.refs_0_, ...), custom_call_target="tpu_custom_call" | custom-call | tf_op jit(solution)/shard_map/finish/pallas_call | solution.py:1478

commit v8 on v7

--- a/solution.py
+++ b/solution.py
@@ -291,7 +291,7 @@
 
 
 def forward_kernel(
-    dims, tokens, cotangent, gain_one, gain_two, table, buckets, wq, wk, wv, wo, wi0, wi1, wff,
+    dims, tokens, cotangent, gains, table, buckets, wq, wk, wv, wo, wi0, wi1, wff,
     hidden, normed_two, attended, lse, by_offset, bias_table, pieces_out, left_g, left_one, left_two,
     full_q, full_k, full_v, full_o, full_0, full_1, full_2,
     normed, flipped, weights, acc, bias, staged, pieces, mixed, heads_in, rolled, branch_in,
@@ -352,7 +352,7 @@
     def _(i):
         at = pl.ds(pl.multiple_of(i * 64, 64), 64)
         values = tokens[at, :].astype(F32)
-        normed[at, :] = (values * rms_scale(values) * gain_one[...].astype(F32)).astype(BF16)
+        normed[at, :] = (values * rms_scale(values) * gains[0:1, :]).astype(BF16)
 
     for copy in row_copies:
         copy.wait()
@@ -362,7 +362,7 @@
     lane = lax.broadcasted_iota(jnp.int32, table.shape, 1)
     for head in range(dims.own_heads):
         own = lane == me * dims.own_heads + head
-        column = jnp.sum(jnp.where(own, table[...].astype(F32), 0.0), axis=1, keepdims=True)
+        column = jnp.sum(jnp.where(own, table[...], 0.0), axis=1, keepdims=True)
         bias_table[head : head + 1, :] = jnp.sum(jnp.where(hot, column, 0.0), axis=0, keepdims=True)
         bias_rows(bias_table[head : head + 1, :], rolled)
         bias[head] = rolled[...].astype(BF16)
@@ -527,7 +527,7 @@
                 normed[at, :].astype(F32) + branch_in[s, here, :].astype(F32)
             )
             hidden[at, :] = values
-            normed_two[at, :] = (values * rms_scale(values) * gain_two[...].astype(F32)).astype(BF16)
+            normed_two[at, :] = (values * rms_scale(values) * gains[1:2, :]).astype(BF16)
 
     flip(normed_two[...], left_two)
     loads[4].wait_near()
@@ -567,7 +567,7 @@
     block = (seqs, part, dims.cols)
     return pl.pallas_call(
         functools.partial(forward_kernel, dims),
-        in_specs=[vmem] * 5 + [anywhere] * 8,
+        in_specs=[vmem] * 4 + [anywhere] * 8,
         out_specs=[vmem] * 6 + [anywhere] * 11,
         out_shape=[
             shape((rows, width), F32),
@@ -867,7 +867,7 @@
 
 
 def backward_kernel(
-    dims, gain_one, gain_two, table, by_offset,
+    dims, gains, table, by_offset,
     tokens, lse_from, pieces_from, left_g, left_two, left_one, normed_two, attended, hidden, cotangent,
     wo, wq, wk, wv, wi0, wi1, wff,
     down_out, gate_out, up_out, o_out, q_out, k_out, v_out,
@@ -921,10 +921,12 @@
                 for j, w in enumerate((wi0, wi1, wff))
             ]
 
-        for copy in load(0) + inputs + lefts[:2]:
+        for copy in load(0) + inputs:
             copy.start()
         for copy in inputs:
             copy.wait()
+        for copy in lefts[:2]:
+            copy.start()
         each = CHUNK // UNITS
 
         @pl.loop(0, units // CHUNK)
@@ -1067,7 +1069,7 @@
             grad = term[s, here, :].astype(F32) + swap_in[s, here, :].astype(F32)
             scale = rms_scale(h)
             ffn_gain[...] += jnp.sum(grad * h * scale, axis=0, keepdims=True)
-            total = given[here, :].astype(F32) + rms_back(h, scale, gain_two[...].astype(F32), grad)
+            total = given[here, :].astype(F32) + rms_back(h, scale, gains[1:2, :], grad)
             values[here, :] = total
             own[here, :] = total.astype(BF16)
 
@@ -1309,7 +1311,7 @@
                 grad = term[s, here, :].astype(F32) + other_one[s, here, :].astype(F32)
                 scale = rms_scale(x)
                 norm_gain[...] += jnp.sum(grad * x * scale, axis=0, keepdims=True)
-                values[here, :] += rms_back(x, scale, gain_one[...].astype(F32), grad)
+                values[here, :] += rms_back(x, scale, gains[0:1, :], grad)
 
             saved = pltpu.make_async_copy(values, input_grad.at[at, :], sem.at[0])
             saved.start()
@@ -1370,7 +1372,7 @@
     block = (shard_rows, CHUNK)
     return pl.pallas_call(
         functools.partial(backward_kernel, dims),
-        in_specs=[vmem] * 4 + [anywhere] * 17,
+        in_specs=[vmem] * 3 + [anywhere] * 17,
         out_specs=[anywhere] * 12 + [vmem],
         out_shape=[shape((shard_rows, units), BF16)] * 3
         + [shape((shard_rows, inner), BF16)] * 4
@@ -1425,23 +1427,24 @@
     )
 
 
-TILE = 64
-
-
-def finish_kernel(count, *refs):
+TILE = 256
+
+
+def finish_kernel(count, firsts, *refs):
     sources, outs = refs[:count], refs[count : 2 * count]
     taken, made = refs[2 * count : 3 * count], refs[3 * count : 4 * count]
     take_sem, save_sem = refs[4 * count :]
-    tiles = [source.shape[0] // TILE for source in sources]
-
-    def at(i):
-        return pl.ds(pl.multiple_of(i * TILE, TILE), TILE)
+    sizes = [min(out.shape[0], TILE) for out in outs]
+    tiles = [out.shape[0] // size for out, size in zip(outs, sizes)]
+
+    def at(j, i, first=0):
+        return pl.ds(pl.multiple_of(first + i * sizes[j], 16), sizes[j])
 
     def take(j, i):
-        return pltpu.make_async_copy(sources[j].at[at(i)], taken[j].at[at(i)], take_sem.at[j, i])
+        return pltpu.make_async_copy(sources[j].at[at(j, i, firsts[j])], taken[j].at[at(j, i)], take_sem.at[j, i])
 
     def save(j, i):
-        return pltpu.make_async_copy(made[j].at[at(i)], outs[j].at[at(i)], save_sem.at[j, i])
+        return pltpu.make_async_copy(made[j].at[at(j, i)], outs[j].at[at(j, i)], save_sem.at[j, i])
 
     for j in range(count):
         @pl.loop(0, tiles[j])
@@ -1453,7 +1456,7 @@
         def _(i):
             take(j, i).wait()
             if made[j].dtype != taken[j].dtype:
-                made[j][at(i), :] = taken[j][at(i), :].astype(made[j].dtype)
+                made[j][at(j, i), :] = taken[j][at(j, i), :].astype(made[j].dtype)
             save(j, i).start()
 
     for j in range(count):
@@ -1462,24 +1465,26 @@
             save(j, i).wait()
 
 
-def finish(sources, types):
-    count = len(sources)
-    taken = [pltpu.VMEM(s.shape, s.dtype) for s in sources]
-    made = [pltpu.VMEM(s.shape, t) for s, t in zip(sources, types)]
-    same = [s.dtype == t for s, t in zip(sources, types)]
-    tiles = max(s.shape[0] for s in sources) // TILE
+def finish(jobs):
+    count = len(jobs)
+    sources, firsts, lengths, types = zip(*jobs)
+    shapes = [(length, source.shape[1]) for source, length in zip(sources, lengths)]
+    taken = [pltpu.VMEM(shape, source.dtype) for shape, source in zip(shapes, sources)]
+    made = [pltpu.VMEM(shape, kind) for shape, kind in zip(shapes, types)]
+    same = [source.dtype == kind for source, kind in zip(sources, types)]
+    tiles = max(-(-length // TILE) for length in lengths)
 
     def kernel(*refs):
         refs = list(refs)
         made_at = iter(refs[3 * count : -2])
         full = [refs[2 * count + j] if same[j] else next(made_at) for j in range(count)]
-        finish_kernel(count, *refs[: 3 * count], *full, *refs[-2:])
+        finish_kernel(count, firsts, *refs[: 3 * count], *full, *refs[-2:])
 
     return pl.pallas_call(
         kernel,
         in_specs=[pl.BlockSpec(memory_space=pl.ANY)] * count,
         out_specs=[pl.BlockSpec(memory_space=pl.ANY)] * count,
-        out_shape=[jax.ShapeDtypeStruct(s.shape, t) for s, t in zip(sources, types)],
+        out_shape=[jax.ShapeDtypeStruct(shape, kind) for shape, kind in zip(shapes, types)],
         scratch_shapes=taken
         + [m for m, keep in zip(made, same) if not keep]
         + [pltpu.SemaphoreType.DMA((count, tiles))] * 2,
@@ -1509,20 +1514,23 @@
     slots, heads = bucket_bias_table.shape
     dims = Dims(mesh, seqs, part, width, inner_width, gate_weight.shape[1], heads, slots)
     token_rows, upstream = tokens.reshape(rows, width), cotangent.reshape(rows, width)
-    gain_one, gain_two = norm_gain.reshape(1, width), ffn_gain.reshape(1, width)
+    gains = jnp.stack([norm_gain, ffn_gain]).astype(F32)
     hidden, normed_two, attended, lse, by_offset, bias_table, pieces, *lefts_and_weights = forward_call(dims)(
-        token_rows, upstream, gain_one, gain_two, bucket_bias_table, buckets,
+        token_rows, upstream, gains, bucket_bias_table.astype(F32), buckets,
         query_weight, key_weight, value_weight, output_weight, gate_weight, up_weight, down_weight,
     )
     left_g, left_one, left_two, wq, wk, wv, wo, wi0, wi1, wff = lefts_and_weights
     *weight_grads, result, grad_inputs, unused, unused_own, unused_other, small = backward_call(dims)(
-        gain_one, gain_two, bias_table, by_offset,
+        gains, bias_table, by_offset,
         token_rows, lse, pieces, left_g, left_two, left_one, normed_two, attended, hidden, upstream,
         wo, wq, wk, wv, wi0, wi1, wff,
     )
-    *weight_grads, grad_inputs, result = finish(weight_grads + [grad_inputs, result], [F32] * 8 + [BF16])
+    lines = width // 128
+    jobs = [(g, 0, g.shape[0], F32) for g in weight_grads]
+    jobs += [(grad_inputs, 0, rows, F32), (result, 0, rows, BF16)]
+    jobs += [(small, 0, lines, F32), (small, lines, lines, F32), (small, 2 * lines, slots, F32)]
+    *weight_grads, grad_inputs, result, norm_gain_grad, ffn_gain_grad, table_grad = finish(jobs)
     grad_down_w, grad_gate_w, grad_up_w, grad_output_w, grad_query_w, grad_key_w, grad_value_w = weight_grads
-    lines = width // 128
     return (
         result.reshape(seqs, part, width),
         grad_inputs.reshape(seqs, part, width),
@@ -1533,9 +1541,9 @@
         grad_gate_w,
         grad_up_w,
         grad_down_w,
-        small[:lines].reshape(width),
-        small[lines : 2 * lines].reshape(width),
-        small[2 * lines :, :heads],
+        norm_gain_grad.reshape(width),
+        ffn_gain_grad.reshape(width),
+        table_grad[:, :heads],
     )
 
 

time: 647 us -> 645 us (level)
  no operation moved by 1% of the time
where the time goes in v8:
time: 645 us; the launch traced here: 636 us
  Pallas kernels  630 us (98%)
    pallas_call x1, Pallas kernels, per_device(): backward_call(dims)  415 us
    pallas_call x1, Pallas kernels, per_device(): forward_call(dims)  198 us
    pallas_call x1, Pallas kernels, finish(): pl.pallas_call(kernel, in_specs=[pl.BlockSpec(memory_space=pl.ANY)] * cou...  16.7 us

profile of v8, /device:TPU:0, one launch (start us, length us, event | category | flops | bytes accessed | tf_op | source)
XLA Modules:
  0.0 635.8 jit_solution(10159464737849249293)
XLA Ops:
  0.6 0.7 stack.9
  1.3 0.7 stack.10
  2.0 0.6 maximum_convert_fusion.gains
  2.7 1.4 copy.27.table
  4.0 198.4 %forward.1 = (f32[512,2048]{1,0:T(8,128)}, bf16[512,2048]{1,0:T(8,128)(2,1)}, bf16[512,1024]{1,0:T(8,128)(2,1)}, f32[2,4,256,128]{3,2,1,0:T(8,128)}, f32[1,2048]...) custom-call(bf16[512,2048]{1,0:T(8,128)(2,1)} %bitcast.7, ...), custom_call_target="tpu_custom_call" | custom-call | tf_op jit(solution)/shard_map/forward/pallas_call | solution.py:1518
  202.4 415.1 %backward.1 = (bf16[512,2560]{1,0:T(8,128)(2,1)}, bf16[512,2560]{1,0:T(8,128)(2,1)}, bf16[512,2560]{1,0:T(8,128)(2,1)}, bf16[512,1024]{1,0:T(8,128)(2,1)}, bf16[...) custom-call(f32[2,2048]{1,0:T(2,128)} %maximum_convert_fusion.gains,, ...), custom_call_target="tpu_custom_call" | custom-call | tf_op jit(solution)/shard_map/backward/pallas_call | solution.py:1523
  617.5 16.7 %finish.1 = (f32[512,2560]{1,0:T(8,128)}, f32[512,2560]{1,0:T(8,128)}, f32[512,2560]{1,0:T(8,128)}, f32[512,1024]{1,0:T(8,128)}, f32[512,1024]{1,0:T(8,128)}, /*...) custom-call(bf16[512,2560]{1,0:T(8,128)(2,1)} %get-tuple-element.68., ...), custom_call_target="tpu_custom_call" | custom-call | tf_op jit(solution)/shard_map/finish/pallas_call | solution.py:1483
  634.2 1.4 copy.28

commit v9 on v8

--- a/solution.py
+++ b/solution.py
@@ -510,12 +510,6 @@
         project(s)
     if n > 2:
         spreads[1].hop(2)
-    for h in range(3, n):
-        for spread in spreads[:2]:
-            spread.hop(h)
-    loads[4].wait_own()
-    loads[4].pass_on()
-    spreads[0].pass_on()
     for s in range(seqs):
         swaps[s].wait_recv()
 
@@ -530,6 +524,12 @@
             normed_two[at, :] = (values * rms_scale(values) * gains[1:2, :]).astype(BF16)
 
     flip(normed_two[...], left_two)
+    for h in range(3, n):
+        for spread in spreads[:2]:
+            spread.hop(h)
+    loads[4].wait_own()
+    loads[4].pass_on()
+    spreads[0].pass_on()
     loads[4].wait_near()
     for spread in spreads[:2]:
         spread.wait()

time: 645 us -> 651 us (level)
  Pallas kernels: 630 us -> 637 us
    pallas_call x1, Pallas kernels: 415 us -> 423 us  [per_device(): backward_call(dims)]
where the time goes in v9:
time: 651 us; the launch traced here: 643 us
  Pallas kernels  637 us (98%)
    pallas_call x1, Pallas kernels, per_device(): backward_call(dims)  423 us
    pallas_call x1, Pallas kernels, per_device(): forward_call(dims)  198 us
    pallas_call x1, Pallas kernels, finish(): pl.pallas_call(kernel, in_specs=[pl.BlockSpec(memory_space=pl.ANY)] * cou...  16.7 us

profile of v9, /device:TPU:0, one launch (start us, length us, event | category | flops | bytes accessed | tf_op | source)
XLA Modules:
  0.0 642.6 jit_solution(1429386066719140441)
XLA Ops:
  0.6 0.7 stack.9
  1.3 0.7 stack.10
  2.0 0.6 maximum_convert_fusion.gains
  2.7 1.4 copy.27.table
  4.0 197.5 %forward.1 = (f32[512,2048]{1,0:T(8,128)}, bf16[512,2048]{1,0:T(8,128)(2,1)}, bf16[512,1024]{1,0:T(8,128)(2,1)}, f32[2,4,256,128]{3,2,1,0:T(8,128)}, f32[1,2048]...) custom-call(bf16[512,2048]{1,0:T(8,128)(2,1)} %bitcast.7, ...), custom_call_target="tpu_custom_call" | custom-call | tf_op jit(solution)/shard_map/forward/pallas_call | solution.py:1518
  201.6 422.7 %backward.1 = (bf16[512,2560]{1,0:T(8,128)(2,1)}, bf16[512,2560]{1,0:T(8,128)(2,1)}, bf16[512,2560]{1,0:T(8,128)(2,1)}, bf16[512,1024]{1,0:T(8,128)(2,1)}, bf16[...) custom-call(f32[2,2048]{1,0:T(2,128)} %maximum_convert_fusion.gains,, ...), custom_call_target="tpu_custom_call" | custom-call | tf_op jit(solution)/shard_map/backward/pallas_call | solution.py:1523
  624.3 16.7 %finish.1 = (f32[512,2560]{1,0:T(8,128)}, f32[512,2560]{1,0:T(8,128)}, f32[512,2560]{1,0:T(8,128)}, f32[512,1024]{1,0:T(8,128)}, f32[512,1024]{1,0:T(8,128)}, /*...) custom-call(bf16[512,2560]{1,0:T(8,128)(2,1)} %get-tuple-element.68., ...), custom_call_target="tpu_custom_call" | custom-call | tf_op jit(solution)/shard_map/finish/pallas_call | solution.py:1483
  640.9 1.4 copy.28
